TPU v7x, 512 devices: a whole 4x4x16 slice. The times are simulated.
512 devices in a mesh: chan: 8 (over z_lo), base: 64 (over z_hi, x, y, core).
Axes of the slice: x: 4, y: 4, z: 16 (z_hi: 2, z_lo: 8; z = z_hi * 8 + z_lo), core: 2. Of those that a mesh axis runs over, the one named last changes fastest.
Arguments:
- screens: bfloat16 [256, 8, 4096], P('base'), may hold values from -6 to 6
- direction: bfloat16 [256, 8, 4096], P('base'), may hold values from -6 to 6
- sky: bfloat16 [16, 64, 1024], P(None, 'chan'), may hold values from 0.25 to 2
- weights: bfloat16 [2048, 64, 1024], P('base', 'chan'), may hold values from 0.049804688 to 1
- pairs: int32 [2048, 2], P('base'), may hold values from 0 to 255, as said below
- pointing: int32 [2048], P('base'), may hold values from 0 to 15
- counts: int32 [64], P('base'), may hold values from 8 to 32, as said below
Outputs:
- product: float32 [256, 8, 4096], P('base')
Inputs may be any that keep to these rules, and one draw needn't show every extreme that they name: `pairs`: station s is owned by base index s // 4. Both stations of a slot on base index b are owned by base indices within 2 of b, counting cyclically; the two stations of a slot differ. `counts`: some base index has all its slots live in every draw; the live slots of a base index are its first ones.
All inputs are finite; a program needn't handle non-finite values.
Results may differ from a plain program's by a relative error of at most 0.0043.
Values may be sent and summed in bfloat16 or wider, within the bound.
No kernel may reach another device: no remote copies, remote signals or barrier semaphores. Data moves between devices by JAX's collectives and lax.ppermute only.
A program may use at most 64 MiB of HBM per device.

v0:
```python
import math

import jax
import jax.numpy as jnp
from jax import lax
from jax.sharding import PartitionSpec as P

G = 64
W = 32
REACH = 2
ST_DEV = 4
CH_DEV = 8
SUB_BLOCK = 4


def shifted(value, axis, by):
    count = lax.axis_size(axis)
    return lax.ppermute(value, axis, [(i, (i + by) % count) for i in range(count)])


def dft_tables(length):
    position = jnp.arange(length, dtype=jnp.int32)
    product = position[:, None] * position[None, :] % length
    angles = product.astype(jnp.float32) * (2.0 * math.pi / length)
    norm_factor = 1.0 / math.sqrt(length)
    return (
        (jnp.cos(angles) * norm_factor).astype(jnp.bfloat16),
        (jnp.sin(angles) * norm_factor).astype(jnp.bfloat16),
    )


def transform(real_in, imag_in, cosine_table, sine_table, inverse):
    sine_signed = sine_table if inverse else -sine_table
    wide = jnp.float32

    def along_axis(pattern, part_real, part_imag):
        out_real = jnp.einsum(
            pattern, part_real, cosine_table, preferred_element_type=wide
        ) - jnp.einsum(pattern, part_imag, sine_signed, preferred_element_type=wide)
        out_imag = jnp.einsum(
            pattern, part_real, sine_signed, preferred_element_type=wide
        ) + jnp.einsum(pattern, part_imag, cosine_table, preferred_element_type=wide)
        return (out_real, out_imag)

    mid_real, mid_imag = along_axis("rcb,cd->rdb", real_in, imag_in)
    return along_axis("rdb,re->edb", mid_real.astype(jnp.bfloat16), mid_imag.astype(jnp.bfloat16))


def cut_windows(rows, row_start, col_start):

    def single(member, top_row, left_col):
        return lax.dynamic_slice(member, (0, top_row, left_col), (8, W, W))

    return jax.vmap(single)(rows, row_start, col_start)


def add_window(totals, station, top_row, left_col, window_piece):
    row_field = lax.dynamic_index_in_dim(totals, station, 0, keepdims=False).reshape(8, G, G)
    current = lax.dynamic_slice(row_field, (0, top_row, left_col), (8, W, W))
    row_field = lax.dynamic_update_slice(row_field, current + window_piece, (0, top_row, left_col))
    return lax.dynamic_update_index_in_dim(totals, row_field.reshape(8, G * G), station, 0)


def send_home(partials):
    owner_blocks = partials.reshape(2 * REACH + 1, ST_DEV, 8, partials.shape[-1])
    own_total = owner_blocks[REACH]
    for neighbour in range(-REACH, REACH + 1):
        if neighbour != 0:
            own_total = own_total + shifted(owner_blocks[neighbour + REACH], "base", neighbour)
    return own_total


def per_device(screens, direction, sky, weights, pairs, pointing, counts):
    base_count = lax.axis_size("base")
    myself = lax.axis_index("base")
    channels_total = CH_DEV * lax.axis_size("chan")
    stacked = jnp.stack([screens, direction])
    near_list = []
    for neighbour in range(-REACH, REACH + 1):
        if neighbour == 0:
            near_list.append(stacked)
        else:
            near_list.append(shifted(stacked, "base", -neighbour))
    nearby = jnp.concatenate(near_list, axis=1)
    cosine_table, sine_table = dft_tables(W)
    live_count = counts[0]
    loop_trips = (live_count + SUB_BLOCK - 1) // SUB_BLOCK
    table_rows = (2 * REACH + 1) * ST_DEV
    batch_width = SUB_BLOCK * CH_DEV * 4
    start_totals = jnp.zeros((table_rows, 8, G * G), jnp.float32)

    def visit(position, totals):
        first_slot = position * SUB_BLOCK
        station_ids = lax.dynamic_slice_in_dim(pairs, first_slot, SUB_BLOCK, 0)
        pointed = lax.dynamic_slice_in_dim(pointing, first_slot, SUB_BLOCK, 0)
        weight_rows = lax.dynamic_slice_in_dim(weights, first_slot, SUB_BLOCK, 0).astype(
            jnp.float32
        )
        owner_base = station_ids // ST_DEV
        local_slot = (owner_base - myself + REACH) % base_count * ST_DEV + station_ids % ST_DEV
        row_start = pointed // 4 * (G - W) // 3
        col_start = pointed % 4 * (G - W) // 3
        rows_p = nearby[:, local_slot[:, 0]].reshape(2, SUB_BLOCK, 8, G, G)
        rows_q = nearby[:, local_slot[:, 1]].reshape(2, SUB_BLOCK, 8, G, G)
        beam_p = cut_windows(rows_p[0], row_start, col_start).astype(jnp.float32)
        probe_p = cut_windows(rows_p[1], row_start, col_start).astype(jnp.float32)
        beam_q = cut_windows(rows_q[0], row_start, col_start).astype(jnp.float32)
        probe_q = cut_windows(rows_q[1], row_start, col_start).astype(jnp.float32)
        bp_real, bp_imag = (beam_p[:, :4], beam_p[:, 4:])
        bq_real, bq_imag = (beam_q[:, :4], beam_q[:, 4:])
        vp_real, vp_imag = (probe_p[:, :4], probe_p[:, 4:])
        vq_real, vq_imag = (probe_q[:, :4], probe_q[:, 4:])
        delta_real = vp_real * bq_real + vp_imag * bq_imag + bp_real * vq_real + bp_imag * vq_imag
        delta_imag = vp_imag * bq_real - vp_real * bq_imag + bp_imag * vq_real - bp_real * vq_imag
        sky_rows = sky[pointed].astype(jnp.float32).reshape(SUB_BLOCK, CH_DEV, W, W)
        sky_moved = sky_rows.transpose(2, 3, 0, 1)[..., None]
        weight_moved = weight_rows.reshape(SUB_BLOCK, CH_DEV, W, W).transpose(2, 3, 0, 1)[..., None]

        def spread_sky(part):
            return (
                (sky_moved * part.transpose(2, 3, 0, 1)[:, :, :, None, :])
                .reshape(W, W, batch_width)
                .astype(jnp.bfloat16)
            )

        freq_real, freq_imag = transform(
            spread_sky(delta_real), spread_sky(delta_imag), cosine_table, sine_table, False
        )
        freq_real = (
            (freq_real.reshape(W, W, SUB_BLOCK, CH_DEV, 4) * weight_moved)
            .reshape(W, W, batch_width)
            .astype(jnp.bfloat16)
        )
        freq_imag = (
            (freq_imag.reshape(W, W, SUB_BLOCK, CH_DEV, 4) * weight_moved)
            .reshape(W, W, batch_width)
            .astype(jnp.bfloat16)
        )
        back_real, back_imag = transform(freq_real, freq_imag, cosine_table, sine_table, True)
        alive_mask = (first_slot + jnp.arange(SUB_BLOCK, dtype=jnp.int32) < live_count).astype(
            jnp.float32
        )
        weighting = alive_mask / channels_total

        def fold_back(part):
            summed = jnp.sum(part.reshape(W, W, SUB_BLOCK, CH_DEV, 4) * sky_moved, axis=3)
            return summed.transpose(2, 3, 0, 1) * weighting[:, None, None, None]

        grad_real = fold_back(back_real)
        grad_imag = fold_back(back_imag)
        gain_p = jnp.concatenate(
            [bq_real * grad_real - bq_imag * grad_imag, bq_real * grad_imag + bq_imag * grad_real],
            axis=1,
        )
        gain_q = jnp.concatenate(
            [bp_real * grad_real + bp_imag * grad_imag, bp_imag * grad_real - bp_real * grad_imag],
            axis=1,
        )
        for member in range(SUB_BLOCK):
            totals = add_window(
                totals, local_slot[member, 0], row_start[member], col_start[member], gain_p[member]
            )
            totals = add_window(
                totals, local_slot[member, 1], row_start[member], col_start[member], gain_q[member]
            )
        return totals

    partials = lax.fori_loop(0, loop_trips, visit, start_totals)
    own_total = send_home(partials)
    result = lax.psum(own_total, "chan")
    return result


def solution(mesh):
    in_specs = (
        P("base", None, None),
        P("base", None, None),
        P(None, "chan", None),
        P("base", "chan", None),
        P("base", None),
        P("base"),
        P("base"),
    )
    out_specs = P("base", None, None)
    return jax.shard_map(
        per_device, mesh=mesh, in_specs=in_specs, out_specs=out_specs, check_vma=False
    )
```

profile of v0, /device:TPU:6, one launch (start us, length us, event | category | flops | bytes accessed | tf_op | source)
XLA Modules:
  0.0 1436.5 jit_solution(187547105481529021)
XLA Ops:
  7.7 3.5 collective-permute-start
  13.1 5.8 collective-permute-start.2
  18.9 2.4 collective-permute-start.3
  21.9 4.6 collective-permute-done
  27.3 3.6 collective-permute-done.1
  33.5 3.2 collective-permute-done.3
  39.4 449.8 %while.35 = (s32[]{:T(128)}, f32[20,8,4096]{2,1,0:T(8,128)}, s32[]{:T(128)}, s32[32,2]{0,1:T(2,128)S(1)}, s32[]{:T(128)}, /*index=5*/s32[32]{0:T(128)S(1)}, bf16...) while((s32[]{:T(128)}, f32[20,8,4096]{2,1,0:T(8,128)}, ...), condition=%wide.region_3.4_spmd.clone.clone, body=%wide.region_0.3_spmd.clone.clone.sunk | while | flops 138362416 | bytes 46807616 | solution.py:168
  39.5 2.3 gather_fusion
  42.8 10.5 while.36
  53.3 2.3 gather_fusion.1
  56.3 10.5 while.39
  67.5 10.5 while.37
  76.0 2.0 dynamic-slice_dynamic-update-slice_fusion.9
  78.7 10.5 while.38
  111.0 3.9 copy.112
  114.9 2.4 multiply_reduce_fusion.3
  127.1 3.1 dynamic_update_slice.177
  134.1 3.1 dynamic_update_slice.178
  144.5 3.1 dynamic_update_slice.179
  151.3 3.1 dynamic_update_slice.180
  162.2 3.1 dynamic_update_slice.181
  169.2 3.1 dynamic_update_slice.182
  179.9 3.1 dynamic_update_slice.183
  187.0 3.1 dynamic_update_slice.184
  191.0 2.3 gather_fusion
  194.2 10.5 while.36
  204.8 2.3 gather_fusion.1
  207.7 10.5 while.39
  218.9 10.5 while.37
  222.2 2.0 dynamic-slice_dynamic-update-slice_fusion.9
  230.1 10.5 while.38
  238.7 2.0 dynamic-slice_dynamic-update-slice_fusion.10
  262.5 3.9 copy.112
  266.3 2.4 multiply_reduce_fusion.3
  278.6 3.1 dynamic_update_slice.177
  285.6 3.1 dynamic_update_slice.178
  296.0 3.1 dynamic_update_slice.179
  302.8 3.1 dynamic_update_slice.180
  313.7 3.1 dynamic_update_slice.181
  320.7 3.1 dynamic_update_slice.182
  331.5 3.1 dynamic_update_slice.183
  338.5 3.1 dynamic_update_slice.184
  342.5 2.3 gather_fusion
  345.7 10.5 while.36
  356.3 2.3 gather_fusion.1
  359.2 10.5 while.39
  370.4 10.5 while.37
  371.1 2.0 dynamic-slice_dynamic-update-slice_fusion.9
  381.6 10.5 while.38
  414.0 3.9 copy.112
  417.8 2.4 multiply_reduce_fusion.3
  430.1 3.1 dynamic_update_slice.177
  437.1 3.1 dynamic_update_slice.178
  447.4 3.1 dynamic_update_slice.179
  454.2 3.1 dynamic_update_slice.180
  465.2 3.1 dynamic_update_slice.181
  472.2 3.1 dynamic_update_slice.182
  490.9 728.8 %collective-permute-start.4 = (f32[4,8,4096]{2,1,0:T(8,128)S(1)}, f32[4,8,4096]{2,1,0:T(8,128)S(1)}, u32[]{:S(2)}, u32[]{:S(2)}) collective-permute-start(f32[4,8,4096]{2,1,0:T(8,128)S(1)} %get-tuple-element.514), channel_id=1, source_target_pairs={{0,62},{1,63},{2,0},{3,1},{4,2},{5,3},{6,4},{7,5},{8,6},{9,7},{10,... | collective-permute-start | bytes 1572872 | tf_op jit(solution)/shard_map/ppermute | solution.py:18
  1221.6 2.4 collective-permute-start.6
  1226.3 5.6 collective-permute-done.5
  1231.9 4.8 collective-permute-done.6
  1236.7 6.1 collective-permute-done.7
  1242.8 2.0 add_add_fusion
  1244.8 183.0 %all-reduce.2.cloned.1.call-done = f32[4,8,4096]{2,1,0:T(8,128)} async-done(((f32[4,8,4096]{2,1,0:T(8,128)}), f32[4,8,4096]{2,1,0:T(8,128)}) %all-reduce.2.cloned.1.call-update) | async-done | bytes 524304 | tf_op jit(solution)/shard_map/psum | solution.py:170
  (484 shorter events, 263.9 us)
Async XLA Ops:
  6.5 25.3 %copy-start.6 = (bf16[4,8,4096]{2,1,0:T(8,128)(2,1)S(1)}, bf16[4,8,4096]{2,1,0:T(8,128)(2,1)}, u32[]{:S(2)}) copy-start(bf16[4,8,4096]{2,1,0:T(8,128)(2,1)} %param.9) | copy-start | bytes 786436
  6.5 25.3 %copy-start.5 = (bf16[4,8,4096]{2,1,0:T(8,128)(2,1)S(1)}, bf16[4,8,4096]{2,1,0:T(8,128)(2,1)}, u32[]{:S(2)}) copy-start(bf16[4,8,4096]{2,1,0:T(8,128)(2,1)} %param.10) | copy-start | bytes 786436
  6.5 1421.2 %all-reduce.2.cloned.1.call-start = ((), (), s32[]{:S(2)}) async-start(), calls=%async_computation | async-start | bytes 1048576 | tf_op jit(solution)/shard_map/psum | solution.py:170
  7.7 18.8 %collective-permute-start = (bf16[2,4,8,4096]{3,2,1,0:T(8,128)(2,1)S(1)}, bf16[2,4,8,4096]{3,2,1,0:T(8,128)(2,1)S(1)}, u32[]{:S(2)}, u32[]{:S(2)}) collective-permute-start(bf16[2,4,8,4096]{3,2,1,0:T(8,128)(2,1)S(1)} %pad_maximum_fusion.2), channel_id=1, source_target_pairs={{0,2},{1,3},{2,4},{3,5},{4,6},{5,7},{6,8},{7,9},{8,10},{9,11},{10,... | collective-permute-start | bytes 1572872 | tf_op jit(solution)/shard_map/ppermute | solution.py:18
  11.2 19.8 %collective-permute-start.1 = (bf16[2,4,8,4096]{3,2,1,0:T(8,128)(2,1)S(1)}, bf16[2,4,8,4096]{3,2,1,0:T(8,128)(2,1)S(1)}, u32[]{:S(2)}, u32[]{:S(2)}) collective-permute-start(bf16[2,4,8,4096]{3,2,1,0:T(8,128)(2,1)S(1)} %pad_maximum_fusion.2), channel_id=1, source_target_pairs={{0,1},{1,2},{2,3},{3,4},{4,5},{5,6},{6,7},{7,8},{8,9},{9,10},{10,1... | collective-permute-start | bytes 1572872 | tf_op jit(solution)/shard_map/ppermute | solution.py:18
  13.1 19.6 %collective-permute-start.2 = (bf16[2,4,8,4096]{3,2,1,0:T(8,128)(2,1)S(1)}, bf16[2,4,8,4096]{3,2,1,0:T(8,128)(2,1)S(1)}, u32[]{:S(2)}, u32[]{:S(2)}) collective-permute-start(bf16[2,4,8,4096]{3,2,1,0:T(8,128)(2,1)S(1)} %pad_maximum_fusion.2), channel_id=1, source_target_pairs={{0,63},{1,0},{2,1},{3,2},{4,3},{5,4},{6,5},{7,6},{8,7},{9,8},{10,9... | collective-permute-start | bytes 1572872 | tf_op jit(solution)/shard_map/ppermute | solution.py:18
  18.9 17.9 %collective-permute-start.3 = (bf16[2,4,8,4096]{3,2,1,0:T(8,128)(2,1)S(1)}, bf16[2,4,8,4096]{3,2,1,0:T(8,128)(2,1)S(1)}, u32[]{:S(2)}, u32[]{:S(2)}) collective-permute-start(bf16[2,4,8,4096]{3,2,1,0:T(8,128)(2,1)S(1)} %pad_maximum_fusion.2), channel_id=1, source_target_pairs={{0,62},{1,63},{2,0},{3,1},{4,2},{5,3},{6,4},{7,5},{8,6},{9,7},{10,... | collective-permute-start | bytes 1572872 | tf_op jit(solution)/shard_map/ppermute | solution.py:18
  32.7 6.8 copy-start.7
  32.7 6.8 copy-start.8
  66.9 22.4 %copy-start = (f32[4,8,32,32]{3,2,1,0:T(8,128)}, f32[4,8,32,32]{3,2,1,0:T(8,128)S(1)}, u32[]{:S(2)}) copy-start(f32[4,8,32,32]{3,2,1,0:T(8,128)S(1)} %convert_element_type.429) | copy-start | bytes 393220 | tf_op jit(solution)/shard_map/while
  91.9 3.1 copy-start.2
  105.7 0.7 copy-start.4
  108.6 6.3 copy-start.3
  114.9 3.0 copy-start.1
  218.3 22.4 %copy-start = (f32[4,8,32,32]{3,2,1,0:T(8,128)}, f32[4,8,32,32]{3,2,1,0:T(8,128)S(1)}, u32[]{:S(2)}) copy-start(f32[4,8,32,32]{3,2,1,0:T(8,128)S(1)} %convert_element_type.429) | copy-start | bytes 393220 | tf_op jit(solution)/shard_map/while
  243.4 3.1 copy-start.2
  257.1 0.7 copy-start.4
  260.1 6.3 copy-start.3
  266.3 3.0 copy-start.1
  369.8 22.4 %copy-start = (f32[4,8,32,32]{3,2,1,0:T(8,128)}, f32[4,8,32,32]{3,2,1,0:T(8,128)S(1)}, u32[]{:S(2)}) copy-start(f32[4,8,32,32]{3,2,1,0:T(8,128)S(1)} %convert_element_type.429) | copy-start | bytes 393220 | tf_op jit(solution)/shard_map/while
  394.8 3.1 copy-start.2
  408.6 0.7 copy-start.4
  411.6 6.3 copy-start.3
  417.8 3.0 copy-start.1
  490.9 735.5 %collective-permute-start.4 = (f32[4,8,4096]{2,1,0:T(8,128)S(1)}, f32[4,8,4096]{2,1,0:T(8,128)S(1)}, u32[]{:S(2)}, u32[]{:S(2)}) collective-permute-start(f32[4,8,4096]{2,1,0:T(8,128)S(1)} %get-tuple-element.514), channel_id=1, source_target_pairs={{0,62},{1,63},{2,0},{3,1},{4,2},{5,3},{6,4},{7,5},{8,6},{9,7},{10,... | collective-permute-start | bytes 1572872 | tf_op jit(solution)/shard_map/ppermute | solution.py:18
  1219.6 12.3 collective-permute-start.5
  1221.6 15.2 %collective-permute-start.6 = (f32[4,8,4096]{2,1,0:T(8,128)S(1)}, f32[4,8,4096]{2,1,0:T(8,128)S(1)}, u32[]{:S(2)}, u32[]{:S(2)}) collective-permute-start(f32[4,8,4096]{2,1,0:T(8,128)S(1)} %get-tuple-element.517), channel_id=1, source_target_pairs={{0,1},{1,2},{2,3},{3,4},{4,5},{5,6},{6,7},{7,8},{8,9},{9,10},{10,1... | collective-permute-start | bytes 1572872 | tf_op jit(solution)/shard_map/ppermute | solution.py:18
  1224.0 18.9 %collective-permute-start.7 = (f32[4,8,4096]{2,1,0:T(8,128)S(1)}, f32[4,8,4096]{2,1,0:T(8,128)S(1)}, u32[]{:S(2)}, u32[]{:S(2)}) collective-permute-start(f32[4,8,4096]{2,1,0:T(8,128)S(1)} %get-tuple-element.516), channel_id=1, source_target_pairs={{0,2},{1,3},{2,4},{3,5},{4,6},{5,7},{6,8},{7,9},{8,10},{9,11},{10,... | collective-permute-start | bytes 1572872 | tf_op jit(solution)/shard_map/ppermute | solution.py:18
Sparse Core Ops, SparseCore 0:
  1244.9 182.7 all-reduce.1
where the time goes:
time: 1450 us; the launch traced here: 1440 us
  starting transfers between devices  749 us (52%)
  local copies, waits for them, and re-layouts  311 us (21%)
  waiting for transfers between devices  211 us (15%)
  loops' own time  93.3 us (6%)
  matrix products  30.3 us (2%)
  other arithmetic  28.3 us (2%)
    ppermute x8, starting transfers between devices, shifted(): lax.ppermute(value, axis, [(i, (i + by) % count) for i in range(count)])  749 us
    psum x1, waiting for transfers between devices, per_device(): result = lax.psum(own_total, 'chan')  183 us
    gather x144, local copies, waits for them, and re-layouts  125 us
    another operation x1, loops' own time, per_device(): partials = lax.fori_loop(0, loop_trips, visit, start_totals)  92.2 us
    dynamic_update_slice x24, local copies, waits for them, and re-layouts, add_window(): lax.dynamic_update_slice(row_field, current + window_piece, (0, top_row,...  70.6 us
  transfers between devices with their start and end apart: 9, of which 8 were waited for; matrix products, arithmetic and copies ran while one was open for 0% of the time, Pallas kernels for 0%

commit v1 on v0

v1 whole, which is shorter than its diff:
```python
import math

import jax
import jax.numpy as jnp
from jax import lax
from jax.experimental import pallas as pl
from jax.experimental.pallas import tpu as pltpu
from jax.sharding import PartitionSpec as P

G = 64
W = 32
REACH = 2
ST_DEV = 4
SUB_DEV = 32
CH_DEV = 8
POLS = 4
HALVES = 2
GROUP = 4
QUADS = SUB_DEV // GROUP
QUADS_HALF = QUADS // HALVES
PARTS = POLS * HALVES
LANES = GROUP * W
NEAR = 2 * REACH + 1
SMEM = pltpu.SMEM
VMEM = pltpu.VMEM


def shifted(value, axis, by):
    count = lax.axis_size(axis)
    return lax.ppermute(value, axis, [(i, (i + by) % count) for i in range(count)])


def pass_tables():
    position = jnp.arange(W, dtype=jnp.int32)
    product = position[:, None] * position[None, :] % W
    angles = product.astype(jnp.float32) * (2.0 * math.pi / W)
    norm_factor = 1.0 / math.sqrt(W)
    cosine = jnp.cos(angles) * norm_factor
    sine = jnp.sin(angles) * norm_factor
    eye = jnp.eye(GROUP, dtype=jnp.float32)

    def right(sign):
        cos_block, sin_block = jnp.kron(eye, cosine), sign * jnp.kron(eye, sine)
        return jnp.block([[cos_block, sin_block], [-sin_block, cos_block]])

    def left(sign):
        return jnp.kron(eye, jnp.block([[cosine, -sign * sine], [sign * sine, cosine]]))

    return jnp.stack([right(-1.0), left(-1.0), right(1.0), left(1.0)]).astype(jnp.bfloat16)


def swap_halves(value):
    return pltpu.roll(value, G, 1)


def lane_index(rows):
    return lax.broadcasted_iota(jnp.int32, (rows, 2 * G), 1)


def delta_kernel(meta, *refs):
    near, out, wide = refs[:NEAR], refs[NEAR], refs[NEAR + 1]
    half = meta[4, 0]
    for block in range(NEAR):
        wide[pl.ds(block * ST_DEV, ST_DEV)] = near[block][...].astype(jnp.float32)
    lane = lane_index(W)
    for step in range(QUADS_HALF):
        real = jnp.zeros((W, LANES), jnp.float32)
        imag = jnp.zeros((W, LANES), jnp.float32)
        for member in range(GROUP):
            slot = (HALVES * step + half) * GROUP + member
            rows = pl.ds(meta[2, slot], W)
            left = meta[3, slot]
            beam_p = wide[meta[0, slot], 0, rows, :]
            probe_p = wide[meta[0, slot], 1, rows, :]
            beam_q = wide[meta[1, slot], 0, rows, :]
            probe_q = wide[meta[1, slot], 1, rows, :]
            same = probe_p * beam_q + beam_p * probe_q
            cross = probe_p * swap_halves(beam_q) - swap_halves(beam_p) * probe_q
            sum_real = same + swap_halves(same)
            sum_imag = swap_halves(cross) - cross
            shift = lax.rem(member * W + 2 * G - left, 2 * G)
            mine = (lane >= member * W) & (lane < (member + 1) * W)
            real = jnp.where(mine, pltpu.roll(sum_real, shift, 1), real)
            imag = jnp.where(mine, pltpu.roll(sum_imag, shift, 1), imag)
        out[step, 0] = real.astype(jnp.bfloat16)
        out[step, 1] = imag.astype(jnp.bfloat16)


def hessian_kernel(meta, delta, weights, sky, tables, out, sky_wide):
    live = meta[5, 0]
    quads = (live + GROUP - 1) // GROUP
    lane = lane_index(W)
    right_forward, left_forward = tables[0], tables[1]
    right_inverse, left_inverse = tables[2], tables[3]
    wide = jnp.float32
    half_type = jnp.bfloat16

    def dot(a, b):
        return jnp.dot(a, b, preferred_element_type=wide)

    def to_rows(value):
        groups = []
        for group in range(CH_DEV // GROUP):
            pieces = []
            for member in range(GROUP):
                first = (group * GROUP + member) * W
                for part in range(2):
                    pieces.append(value[first : first + W, part * LANES : (part + 1) * LANES])
            groups.append(jnp.concatenate(pieces, axis=0))
        return jnp.concatenate(groups, axis=1)

    def piece(value, channel, part):
        group, member = channel // GROUP, channel % GROUP
        first = (member * 2 + part) * W
        return value[first : first + W, group * LANES : (group + 1) * LANES]

    def visit(quad, carry):
        step, half = quad // HALVES, quad % HALVES
        for channel in range(CH_DEV):
            chosen = sky[meta[6, quad * GROUP], channel].astype(wide)
            for member in range(1, GROUP):
                other = sky[meta[6, quad * GROUP + member], channel].astype(wide)
                chosen = jnp.where(lane >= member * W, other, chosen)
            sky_wide[channel] = chosen
        for pol in range(POLS):
            part_index = pol * HALVES + half
            real = delta[part_index, step, 0].astype(wide)
            imag = delta[part_index, step, 1].astype(wide)
            lifted = jnp.concatenate(
                [
                    jnp.concatenate(
                        [
                            (sky_wide[channel] * real).astype(half_type),
                            (sky_wide[channel] * imag).astype(half_type),
                        ],
                        axis=1,
                    )
                    for channel in range(CH_DEV)
                ],
                axis=0,
            )
            middle = dot(lifted, right_forward).astype(half_type)
            freq = dot(left_forward, to_rows(middle))
            weighted = jnp.concatenate(
                [
                    jnp.concatenate(
                        [
                            (
                                piece(freq, channel, part) * weights[quad, channel].astype(wide)
                            ).astype(half_type)
                            for part in range(2)
                        ],
                        axis=1,
                    )
                    for channel in range(CH_DEV)
                ],
                axis=0,
            )
            middle = dot(weighted, right_inverse).astype(half_type)
            back = dot(left_inverse, to_rows(middle))
            for part in range(2):
                total = sky_wide[0] * piece(back, 0, part)
                for channel in range(1, CH_DEV):
                    total = total + sky_wide[channel] * piece(back, channel, part)
                out[part_index, step, part] = total.astype(half_type)
        return carry

    lax.fori_loop(0, quads, visit, 0)

    def blank(quad, carry):
        for pol in range(POLS):
            out[pol * HALVES + quad % HALVES, quad // HALVES] = jnp.zeros((2, W, LANES), half_type)
        return carry

    lax.fori_loop(quads, QUADS, blank, 0)


def product_kernel(channels_total, meta, grads, *refs):
    near, out, beams, totals = refs[:NEAR], refs[NEAR], refs[NEAR + 1], refs[NEAR + 2]
    half, live = meta[4, 0], meta[5, 0]
    for block in range(NEAR):
        beams[pl.ds(block * ST_DEV, ST_DEV)] = near[block][:, 0].astype(jnp.float32)
    totals[...] = jnp.zeros_like(totals)
    lane = lane_index(W)
    column = lax.rem(lane, G)
    scale = 1.0 / channels_total

    for step in range(QUADS_HALF):
        first = (HALVES * step + half) * GROUP

        @pl.when(first < live)
        def _():
            real = grads[0, step, 0].astype(jnp.float32)
            imag = grads[0, step, 1].astype(jnp.float32)
            for source in range(1, CH_DEV):
                real = real + grads[source, step, 0].astype(jnp.float32)
                imag = imag + grads[source, step, 1].astype(jnp.float32)
            real = real * scale
            imag = imag * scale
            for member in range(GROUP):
                slot = first + member

                @pl.when(slot < live)
                def _():
                    rows = pl.ds(meta[2, slot], W)
                    left = meta[3, slot]
                    station_p, station_q = meta[0, slot], meta[1, slot]
                    low = lax.rem(left + 2 * G - member * W, 2 * G)
                    high = lax.rem(left + 3 * G - member * W, 2 * G)
                    inside = (column >= left) & (column < left + W)
                    upper = lane >= G

                    def placed(value):
                        both = jnp.where(
                            upper, pltpu.roll(value, high, 1), pltpu.roll(value, low, 1)
                        )
                        return jnp.where(inside, both, 0.0)

                    grad_real = placed(real)
                    grad_imag = placed(imag)
                    grad_imag = jnp.where(upper, grad_imag, -grad_imag)
                    beam_p = beams[station_p, rows, :]
                    beam_q = beams[station_q, rows, :]
                    totals[station_p, rows, :] += (
                        beam_q * grad_real + swap_halves(beam_q) * grad_imag
                    )
                    totals[station_q, rows, :] += (
                        beam_p * grad_real - swap_halves(beam_p) * grad_imag
                    )

    for block in range(NEAR):
        out[block] = totals[pl.ds(block * ST_DEV, ST_DEV)].astype(jnp.bfloat16)


def call(kernel, out_shape, in_specs, scratch_shapes):
    return pl.pallas_call(
        kernel,
        out_shape=out_shape,
        in_specs=in_specs,
        out_specs=pl.BlockSpec(memory_space=VMEM),
        scratch_shapes=scratch_shapes,
        compiler_params=pltpu.CompilerParams(vmem_limit_bytes=48 * 1024 * 1024),
    )


def per_device(screens, direction, sky, weights, pairs, pointing, counts):
    base_count = lax.axis_size("base")
    myself = lax.axis_index("base")
    channels_total = CH_DEV * lax.axis_size("chan")
    chunk = lax.axis_index("chan")
    pol, half = chunk // HALVES, chunk % HALVES
    in_smem = pl.BlockSpec(memory_space=SMEM)
    in_vmem = pl.BlockSpec(memory_space=VMEM)

    stacked = jnp.stack([screens, direction], axis=1)
    own = jnp.concatenate(
        [
            lax.dynamic_index_in_dim(stacked, part * POLS + pol, 2, keepdims=False).reshape(
                ST_DEV, 2, G, G
            )
            for part in range(2)
        ],
        axis=-1,
    )
    near = [
        own if by == 0 else shifted(own, "base", -by) for by in range(-REACH, REACH + 1)
    ]

    alive = jnp.arange(SUB_DEV, dtype=jnp.int32) < counts[0]
    local = (pairs // ST_DEV - myself + REACH) % base_count * ST_DEV + pairs % ST_DEV
    local = jnp.where(alive[:, None], local, 0)
    meta = jnp.stack(
        [
            local[:, 0],
            local[:, 1],
            pointing // 4 * (G - W) // 3,
            pointing % 4 * (G - W) // 3,
            jnp.broadcast_to(half, (SUB_DEV,)),
            jnp.broadcast_to(counts[0], (SUB_DEV,)),
            pointing,
        ]
    ).astype(jnp.int32)

    chunk_shape = (QUADS_HALF, 2, W, LANES)
    delta_mine = call(
        delta_kernel,
        jax.ShapeDtypeStruct(chunk_shape, jnp.bfloat16),
        [in_smem] + [in_vmem] * NEAR,
        [pltpu.VMEM((NEAR * ST_DEV, 2, G, 2 * G), jnp.float32)],
    )(meta, *near)
    delta = lax.all_gather(delta_mine, "chan")

    weight_quads = (
        weights.reshape(QUADS, GROUP, CH_DEV, W, W)
        .transpose(0, 2, 3, 1, 4)
        .reshape(QUADS, CH_DEV, W, LANES)
    )
    sky_tiled = jnp.tile(sky.reshape(-1, CH_DEV, W, W), (1, 1, 1, GROUP))
    partial = call(
        hessian_kernel,
        jax.ShapeDtypeStruct((PARTS,) + chunk_shape, jnp.bfloat16),
        [in_smem] + [in_vmem] * 4,
        [pltpu.VMEM((CH_DEV, W, LANES), jnp.float32)],
    )(meta, delta, weight_quads, sky_tiled, pass_tables())
    grads = lax.all_to_all(partial, "chan", 0, 0, tiled=True)

    def make_product(*args):
        return product_kernel(channels_total, *args)

    sums = call(
        make_product,
        jax.ShapeDtypeStruct((NEAR, ST_DEV, G, 2 * G), jnp.bfloat16),
        [in_smem] + [in_vmem] * (1 + NEAR),
        [
            pltpu.VMEM((NEAR * ST_DEV, G, 2 * G), jnp.float32),
            pltpu.VMEM((NEAR * ST_DEV, G, 2 * G), jnp.float32),
        ],
    )(meta, grads, *near)
    mine = sums[REACH].astype(jnp.float32)
    for by in range(-REACH, REACH + 1):
        if by != 0:
            mine = mine + shifted(sums[by + REACH], "base", by).astype(jnp.float32)
    every = lax.all_gather(mine.astype(jnp.bfloat16), "chan")
    every = every.reshape(POLS, HALVES, ST_DEV, G, 2, G).astype(jnp.float32)
    result = every[:, 0] + every[:, 1]
    return result.transpose(1, 3, 0, 2, 4).reshape(ST_DEV, 2 * POLS, G * G)


def solution(mesh):
    in_specs = (
        P("base", None, None),
        P("base", None, None),
        P(None, "chan", None),
        P("base", "chan", None),
        P("base", None),
        P("base"),
        P("base"),
    )
    out_specs = P("base", None, None)
    return jax.shard_map(
        per_device, mesh=mesh, in_specs=in_specs, out_specs=out_specs, check_vma=False
    )
```

time: 1450 us -> 230 us (0.16)
  the two profiles are of different devices: /device:TPU:6 before, /device:TPU:0 now
where the time goes in v1:
time: 230 us; the launch traced here: 229 us
  blocking collectives  124 us (54%)
  starting transfers between devices  34.5 us (15%)
  local copies, waits for them, and re-layouts  25.7 us (11%)
  Pallas kernels  20.9 us (9%)
  waiting for transfers between devices  18.5 us (8%)
  other arithmetic  4.57 us (2%)
    all_gather x1, blocking collectives, per_device(): every = lax.all_gather(mine.astype(jnp.bfloat16), 'chan')  48 us
    all_gather x1, blocking collectives, per_device(): delta = lax.all_gather(delta_mine, 'chan')  47.7 us
    ppermute x8, starting transfers between devices, shifted(): lax.ppermute(value, axis, [(i, (i + by) % count) for i in range(count)])  34.5 us
    all_to_all x1, blocking collectives, per_device(): grads = lax.all_to_all(partial, 'chan', 0, 0, tiled=True)  27.9 us
    ppermute x8, waiting for transfers between devices, shifted(): lax.ppermute(value, axis, [(i, (i + by) % count) for i in range(count)])  18.5 us
    pallas_call x1, Pallas kernels, per_device(): call(hessian_kernel, jax.ShapeDtypeStruct((PARTS,) + chunk_shape, jnp.bfl...  16.6 us
    another operation x3, local copies, waits for them, and re-layouts, per_device(): sky_tiled = jnp.tile(sky.reshape(-1, CH_DEV, W, W), (1, 1, 1, GROUP))  10.5 us
    reshape x2, local copies, waits for them, and re-layouts, per_device(): weights.reshape(QUADS, GROUP, CH_DEV, W, W).transpose(0, 2, 3, 1, 4)  8.19 us
  transfers between devices with their start and end apart: 8, of which 2 were waited for; matrix products, arithmetic and copies ran while one was open for 11% of the time, Pallas kernels for 0%

profile of v1, /device:TPU:0, one launch (start us, length us, event | category | flops | bytes accessed | tf_op | source)
XLA Modules:
  0.0 229.0 jit_solution(12701121302113330003)
XLA Ops:
  0.0 1.6 fusion.10
  1.6 0.1 copy.12
  1.7 0.1 reshape.141
  1.8 0.1 copy.13
  1.9 0.0 copy-start.1
  2.0 0.1 reshape.142
  2.1 0.1 pad_maximum_fusion.5.refs_2_.args_4_
  2.2 1.9 collective-permute-start
  4.1 1.9 collective-permute-start.1
  6.1 16.6 %collective-permute-start.2 = (bf16[4,2,64,128]{3,2,1,0:T(8,128)(2,1)S(1)}, bf16[4,2,64,128]{3,2,1,0:T(8,128)(2,1)S(1)}, u32[]{:S(2)}, u32[]{:S(2)}) collective-permute-start(bf16[4,2,64,128]{3,2,1,0:T(8,128)(2,1)S(1)} %pad_maximum_fusion.5.refs_2_.args_4_), channel_id=1, source_target_pairs={{0,63},{1,0},{2,1},{3,2},{4,3},{5,4},{6,5},{7,6},{8,7},{9,8},{10,9... | collective-permute-start | bytes 393224 | tf_op jit(solution)/shard_map/ppermute | solution.py:30
  22.7 3.9 %collective-permute-start.3 = (bf16[4,2,64,128]{3,2,1,0:T(8,128)(2,1)S(1)}, bf16[4,2,64,128]{3,2,1,0:T(8,128)(2,1)S(1)}, u32[]{:S(2)}, u32[]{:S(2)}) collective-permute-start(bf16[4,2,64,128]{3,2,1,0:T(8,128)(2,1)S(1)} %pad_maximum_fusion.5.refs_2_.args_4_), channel_id=1, source_target_pairs={{0,62},{1,63},{2,0},{3,1},{4,2},{5,3},{6,4},{7,5},{8,6},{9,7},{10,... | collective-permute-start | bytes 393224 | tf_op jit(solution)/shard_map/ppermute | solution.py:30
  26.6 0.1 cosine_multiply_fusion
  26.7 0.1 broadcast_multiply_fusion.1
  27.4 0.7 fusion.28
  28.2 0.7 fusion.30
  28.8 0.3 fusion.1
  29.2 0.1 reshape.146
  29.3 0.1 reshape.149
  29.4 0.1 reshape.153
  29.5 0.1 reshape.155
  29.7 0.1 reshape.156
  29.8 0.1 fusion.15
  29.9 0.2 multiply_convert_fusion.1
  30.2 0.2 mul.397
  30.4 0.2 mul.400
  30.6 0.0 copy-done.1
  30.6 0.8 tile.10
  31.4 4.4 %tile.11 = bf16[16,8,32,4,32]{4,3,2,1,0:T(4,128)(2,1)} broadcast(bf16[16,8,32,32]{3,2,1,0:T(8,128)(2,1)S(1)} %tile.10), dimensions={0,1,2,4} | broadcast | bytes 1310720 | tf_op jit(solution)/shard_map/tile | solution.py:298
  35.8 0.0 copy-start
  35.8 5.3 %tile.12.sky = bf16[16,8,32,128]{3,2,1,0:T(8,128)(2,1)S(1)} reshape(bf16[16,8,32,4,32]{4,3,2,1,0:T(4,128)(2,1)} %tile.11) | data formatting | bytes 2097152 | tf_op jit(solution)/shard_map/tile | solution.py:298
  41.1 0.0 copy-done
  41.1 2.6 %reshape.143 = bf16[8,4,8,32,32]{4,3,2,1,0:T(8,128)(2,1)} reshape(bf16[32,8,1024]{2,1,0:T(8,128)(2,1)S(1)} %copy-done) | data formatting | bytes 1048576 | tf_op jit(solution)/shard_map/reshape | solution.py:294
  43.7 5.6 %copy.17 = bf16[8,4,8,32,32]{4,1,3,2,0:T(4,128)(2,1)} copy(bf16[8,4,8,32,32]{4,3,2,1,0:T(8,128)(2,1)} %reshape.143) | data formatting | bytes 1048576 | tf_op jit(solution)/shard_map/reshape | solution.py:294
  49.3 0.0 copy-start.2
  49.3 3.1 %reshape.144.weights = bf16[8,8,32,128]{3,2,1,0:T(8,128)(2,1)S(1)} reshape(bf16[8,8,32,4,32]{4,3,2,1,0:T(4,128)(2,1)} %bitcast.46) | data formatting | bytes 1048576 | tf_op jit(solution)/shard_map/reshape | solution.py:296
  52.4 0.0 copy-done.2
  52.5 0.1 pad_maximum_fusion.tables
  52.5 0.0 collective-permute-done.refs_0_.args_2_
  52.5 0.0 collective-permute-done.1.refs_1_.args_3_
  52.5 0.0 collective-permute-done.2.refs_3_.args_5_
  52.6 0.0 collective-permute-done.3.refs_4_.args_6_
  52.6 2.0 shard_map.73
  54.6 47.7 %all-gather = bf16[32,2,32,128]{3,2,1,0:T(8,128)(2,1)S(1)} all-gather(bf16[4,2,32,128]{3,2,1,0:T(8,128)(2,1)S(1)} %shard_map.73), channel_id=2, replica_groups=mesh['chan'=8,'base'=64] {'chan'}, dimensions={0}, use_global_device_ids=true | all-gather | bytes 589824 | tf_op jit(solution)/shard_map/all_gather | solution.py:291
  102.3 16.6 %shard_map.74 = bf16[8,4,2,32,128]{4,3,2,1,0:T(8,128)(2,1)S(1)} custom-call(s32[7,32]{1,0:T(8,128)S(1)} %stack.38.meta.args_0_, bf16[8,4,2,32,128]{4,3,2,1,0:T(8,128)(2,1)S(1)} %bitcast.45, bf16[8,8,32,128]{3,2,1,0:T(8,128)(2,1)S(1)} %reshape.144.weights, bf16[16,8,32,128]{3,2,1,0:T(8,128)(2,1)S(1)} %tile.12.sky, bf16[4,256,256]{2,1,0:T(8,128)(2,1)S(1)} %pad_maximum_fusion.tables), custom_call_target="tpu_custom_call" | custom-call | tf_op jit(solution)/shard_map/pallas_call | solution.py:299
  118.9 27.9 %all_to_all.5.args_1_ = bf16[8,4,2,32,128]{4,3,2,1,0:T(8,128)(2,1)S(1)} all-to-all(bf16[8,4,2,32,128]{4,3,2,1,0:T(8,128)(2,1)S(1)} %shard_map.74), channel_id=1, replica_groups=mesh['chan'=8,'base'=64] {'chan'}, dimensions={0} | all-to-all | bytes 1048576 | tf_op jit(solution)/shard_map/all_to_all | solution.py:305
  146.8 2.3 %shard_map.75 = bf16[5,4,64,128]{3,2,1,0:T(8,128)(2,1)S(1)} custom-call(s32[7,32]{1,0:T(8,128)S(1)} %stack.38.meta.args_0_, bf16[8,4,2,32,128]{4,3,2,1,0:T(8,128)(2,1)S(1)} %all_to_all.5.args_1_, bf16[4,2,64,128]{3,2,1,0:T(8,128)(2,1)S(1)} %collective-permute-done.refs_0_.args_2_, bf16[4,2,64,128]{3,2,1,0:T(8,128)(2,1)S(1)} %collective-permute-done.1.refs_1_.args_3_, ...), custom_call_target="tpu_custom_call" | custom-call | tf_op jit(solution)/shard_map/pallas_call | solution.py:310
  149.2 1.9 collective-permute-start.4
  151.1 1.9 collective-permute-start.5
  153.0 2.4 %collective-permute-start.6 = (bf16[4,64,128]{2,1,0:T(8,128)(2,1)S(1)}, bf16[4,64,128]{2,1,0:T(8,128)(2,1)S(1)}, u32[]{:S(2)}, u32[]{:S(2)}) collective-permute-start(bf16[4,64,128]{2,1,0:T(8,128)(2,1)S(1)} %get-tuple-element.9), channel_id=1, source_target_pairs={{0,1},{1,2},{2,3},{3,4},{4,5},{5,6},{6,7},{7,8},{8,9},{9,10},{10,1... | collective-permute-start | bytes 196616 | tf_op jit(solution)/shard_map/ppermute | solution.py:30
  155.4 3.9 %collective-permute-start.7 = (bf16[4,64,128]{2,1,0:T(8,128)(2,1)S(1)}, bf16[4,64,128]{2,1,0:T(8,128)(2,1)S(1)}, u32[]{:S(2)}, u32[]{:S(2)}) collective-permute-start(bf16[4,64,128]{2,1,0:T(8,128)(2,1)S(1)} %get-tuple-element.8), channel_id=1, source_target_pairs={{0,2},{1,3},{2,4},{3,5},{4,6},{5,7},{6,8},{7,9},{8,10},{9,11},{10,... | collective-permute-start | bytes 196616 | tf_op jit(solution)/shard_map/ppermute | solution.py:30
  159.4 0.0 collective-permute-done.4
  159.4 0.0 collective-permute-done.5
  159.4 12.3 %collective-permute-done.6 = bf16[4,64,128]{2,1,0:T(8,128)(2,1)S(1)} collective-permute-done((bf16[4,64,128]{2,1,0:T(8,128)(2,1)S(1)}, bf16[4,64,128]{2,1,0:T(8,128)(2,1)S(1)}, u32[]{:S(2)}, u32[]{:S(2)}) %collective-permute-start.6) | collective-permute-done | bytes 65568 | tf_op jit(solution)/shard_map/ppermute | solution.py:30
  171.7 6.2 %collective-permute-done.7 = bf16[4,64,128]{2,1,0:T(8,128)(2,1)S(1)} collective-permute-done((bf16[4,64,128]{2,1,0:T(8,128)(2,1)S(1)}, bf16[4,64,128]{2,1,0:T(8,128)(2,1)S(1)}, u32[]{:S(2)}, u32[]{:S(2)}) %collective-permute-start.7) | collective-permute-done | bytes 65568 | tf_op jit(solution)/shard_map/ppermute | solution.py:30
  177.9 0.1 fusion.14
  178.0 48.0 %all-gather.1 = bf16[32,64,128]{2,1,0:T(8,128)(2,1)S(1)} all-gather(bf16[4,64,128]{2,1,0:T(8,128)(2,1)S(1)} %fusion.14), channel_id=3, replica_groups=mesh['chan'=8,'base'=64] {'chan'}, dimensions={0}, use_global_device_ids=true | all-gather | bytes 589824 | tf_op jit(solution)/shard_map/all_gather | solution.py:323
  226.0 1.1 reshape.152
  227.1 0.5 fusion
  227.7 0.1 copy.15
  227.8 1.2 reshape.145
  (8 shorter events, 0.1 us)
Async XLA Ops:
  1.9 28.7 %copy-start.1 = (bf16[16,8,1024]{2,1,0:T(8,128)(2,1)S(1)}, bf16[16,8,1024]{2,1,0:T(8,128)(2,1)}, u32[]{:S(2)}) copy-start(bf16[16,8,1024]{2,1,0:T(8,128)(2,1)} %param.9) | copy-start | bytes 786436
  2.2 50.3 %collective-permute-start = (bf16[4,2,64,128]{3,2,1,0:T(8,128)(2,1)S(1)}, bf16[4,2,64,128]{3,2,1,0:T(8,128)(2,1)S(1)}, u32[]{:S(2)}, u32[]{:S(2)}) collective-permute-start(bf16[4,2,64,128]{3,2,1,0:T(8,128)(2,1)S(1)} %pad_maximum_fusion.5.refs_2_.args_4_), channel_id=1, source_target_pairs={{0,2},{1,3},{2,4},{3,5},{4,6},{5,7},{6,8},{7,9},{8,10},{9,11},{10,... | collective-permute-start | bytes 393224 | tf_op jit(solution)/shard_map/ppermute | solution.py:30
  4.1 48.4 %collective-permute-start.1 = (bf16[4,2,64,128]{3,2,1,0:T(8,128)(2,1)S(1)}, bf16[4,2,64,128]{3,2,1,0:T(8,128)(2,1)S(1)}, u32[]{:S(2)}, u32[]{:S(2)}) collective-permute-start(bf16[4,2,64,128]{3,2,1,0:T(8,128)(2,1)S(1)} %pad_maximum_fusion.5.refs_2_.args_4_), channel_id=1, source_target_pairs={{0,1},{1,2},{2,3},{3,4},{4,5},{5,6},{6,7},{7,8},{8,9},{9,10},{10,1... | collective-permute-start | bytes 393224 | tf_op jit(solution)/shard_map/ppermute | solution.py:30
  6.1 46.5 %collective-permute-start.2 = (bf16[4,2,64,128]{3,2,1,0:T(8,128)(2,1)S(1)}, bf16[4,2,64,128]{3,2,1,0:T(8,128)(2,1)S(1)}, u32[]{:S(2)}, u32[]{:S(2)}) collective-permute-start(bf16[4,2,64,128]{3,2,1,0:T(8,128)(2,1)S(1)} %pad_maximum_fusion.5.refs_2_.args_4_), channel_id=1, source_target_pairs={{0,63},{1,0},{2,1},{3,2},{4,3},{5,4},{6,5},{7,6},{8,7},{9,8},{10,9... | collective-permute-start | bytes 393224 | tf_op jit(solution)/shard_map/ppermute | solution.py:30
  22.7 29.9 %collective-permute-start.3 = (bf16[4,2,64,128]{3,2,1,0:T(8,128)(2,1)S(1)}, bf16[4,2,64,128]{3,2,1,0:T(8,128)(2,1)S(1)}, u32[]{:S(2)}, u32[]{:S(2)}) collective-permute-start(bf16[4,2,64,128]{3,2,1,0:T(8,128)(2,1)S(1)} %pad_maximum_fusion.5.refs_2_.args_4_), channel_id=1, source_target_pairs={{0,62},{1,63},{2,0},{3,1},{4,2},{5,3},{6,4},{7,5},{8,6},{9,7},{10,... | collective-permute-start | bytes 393224 | tf_op jit(solution)/shard_map/ppermute | solution.py:30
  35.8 5.3 %copy-start = (bf16[32,8,1024]{2,1,0:T(8,128)(2,1)S(1)}, bf16[32,8,1024]{2,1,0:T(8,128)(2,1)}, u32[]{:S(2)}) copy-start(bf16[32,8,1024]{2,1,0:T(8,128)(2,1)} %param.10) | copy-start | bytes 1572868
  49.3 3.1 %copy-start.2 = (s32[32]{0:T(128)S(1)}, s32[32]{0:T(128)}, u32[]{:S(2)}) copy-start(s32[32]{0:T(128)} %param.12) | copy-start | bytes 388
  149.2 10.2 %collective-permute-start.4 = (bf16[4,64,128]{2,1,0:T(8,128)(2,1)S(1)}, bf16[4,64,128]{2,1,0:T(8,128)(2,1)S(1)}, u32[]{:S(2)}, u32[]{:S(2)}) collective-permute-start(bf16[4,64,128]{2,1,0:T(8,128)(2,1)S(1)} %get-tuple-element.7), channel_id=1, source_target_pairs={{0,62},{1,63},{2,0},{3,1},{4,2},{5,3},{6,4},{7,5},{8,6},{9,7},{10,... | collective-permute-start | bytes 196616 | tf_op jit(solution)/shard_map/ppermute | solution.py:30
  151.1 8.3 %collective-permute-start.5 = (bf16[4,64,128]{2,1,0:T(8,128)(2,1)S(1)}, bf16[4,64,128]{2,1,0:T(8,128)(2,1)S(1)}, u32[]{:S(2)}, u32[]{:S(2)}) collective-permute-start(bf16[4,64,128]{2,1,0:T(8,128)(2,1)S(1)} %get-tuple-element.10), channel_id=1, source_target_pairs={{0,63},{1,0},{2,1},{3,2},{4,3},{5,4},{6,5},{7,6},{8,7},{9,8},{10,9... | collective-permute-start | bytes 196616 | tf_op jit(solution)/shard_map/ppermute | solution.py:30
  153.0 18.6 %collective-permute-start.6 = (bf16[4,64,128]{2,1,0:T(8,128)(2,1)S(1)}, bf16[4,64,128]{2,1,0:T(8,128)(2,1)S(1)}, u32[]{:S(2)}, u32[]{:S(2)}) collective-permute-start(bf16[4,64,128]{2,1,0:T(8,128)(2,1)S(1)} %get-tuple-element.9), channel_id=1, source_target_pairs={{0,1},{1,2},{2,3},{3,4},{4,5},{5,6},{6,7},{7,8},{8,9},{9,10},{10,1... | collective-permute-start | bytes 196616 | tf_op jit(solution)/shard_map/ppermute | solution.py:30
  155.4 22.5 %collective-permute-start.7 = (bf16[4,64,128]{2,1,0:T(8,128)(2,1)S(1)}, bf16[4,64,128]{2,1,0:T(8,128)(2,1)S(1)}, u32[]{:S(2)}, u32[]{:S(2)}) collective-permute-start(bf16[4,64,128]{2,1,0:T(8,128)(2,1)S(1)} %get-tuple-element.8), channel_id=1, source_target_pairs={{0,2},{1,3},{2,4},{3,5},{4,6},{5,7},{6,8},{7,9},{8,10},{9,11},{10,... | collective-permute-start | bytes 196616 | tf_op jit(solution)/shard_map/ppermute | solution.py:30

commit v2 on v1

v2 whole, which is shorter than its diff:
```python
import math

import jax
import jax.numpy as jnp
from jax import lax
from jax.experimental import pallas as pl
from jax.experimental.pallas import tpu as pltpu
from jax.sharding import PartitionSpec as P

G = 64
W = 32
REACH = 2
ST_DEV = 4
SUB_DEV = 32
CH_DEV = 8
POLS = 4
HALVES = 2
GROUP = 4
QUADS = SUB_DEV // GROUP
HALF_ROWS = W // HALVES
PARTS = POLS * HALVES
LANES = GROUP * W
NEAR = 2 * REACH + 1
SETS = 2
CHANNELS = SETS * CH_DEV
POLS_DEV = POLS // SETS
SMEM = pltpu.SMEM
VMEM = pltpu.VMEM


def across_chan(value, bit):
    count = lax.axis_size("chan")
    return lax.ppermute(value, "chan", [(i, i ^ bit) for i in range(count)])


def to_sibling(value):
    count = lax.axis_size("base")
    return lax.ppermute(value, "base", [(i, i ^ 1) for i in range(count)])


def turned_half(base, base_count):
    return base * 2 // base_count


def across_chips(value, phase):
    base_count, chan_count = lax.axis_size("base"), lax.axis_size("chan")
    perm = []
    for chan in range(chan_count):
        for base in range(base_count):
            step = 2 if (base // 2 + phase) % 2 == 0 else -2
            target = (base + step) % base_count
            turn = turned_half(base, base_count) ^ turned_half(target, base_count)
            perm.append((chan * base_count + base, (chan ^ (4 * turn)) * base_count + target))
    return lax.ppermute(value, ("chan", "base"), perm)


def pass_tables():
    position = jnp.arange(W, dtype=jnp.int32)
    product = position[:, None] * position[None, :] % W
    angles = product.astype(jnp.float32) * (2.0 * math.pi / W)
    norm_factor = 1.0 / math.sqrt(W)
    cosine = jnp.cos(angles) * norm_factor
    sine = jnp.sin(angles) * norm_factor
    order = jnp.arange(W, dtype=jnp.int32).reshape(8, 4).T[jnp.array([0, 2, 1, 3])].reshape(W)
    cosine_rows, sine_rows = cosine[order][:, order], sine[order][:, order]
    eye = jnp.eye(GROUP, dtype=jnp.float32)

    def right(sign):
        cos_block, sin_block = jnp.kron(eye, cosine), sign * jnp.kron(eye, sine)
        return jnp.block([[cos_block, sin_block], [-sin_block, cos_block]])

    def left(sign):
        return jnp.kron(eye, jnp.block([[cosine_rows, -sign * sine_rows], [sign * sine_rows, cosine_rows]]))

    return jnp.stack([right(-1.0), left(-1.0), right(1.0), left(1.0)]).astype(jnp.bfloat16)


def swap_halves(value):
    return pltpu.roll(value, G, 1)


def lane_index(rows):
    return lax.broadcasted_iota(jnp.int32, (rows, 2 * G), 1)


def prep_kernel(meta, weights, sky, weight_quads, sky_quads, stage, sky_stage):
    wide = jnp.float32
    quads = (meta[5, 0] + GROUP - 1) // GROUP
    lane = lane_index(8)
    low_half = lane < 2 * W
    even_group = lax.rem(lane, 2 * W) < W

    def turned(value, dest):
        for high in range(8):
            dest[pl.ds(high, CH_DEV, stride=8), :] = value[:, high * LANES : (high + 1) * LANES]

    def turn_sky(point, carry):
        turned(sky[point].astype(wide), sky_stage.at[point])
        return carry

    lax.fori_loop(0, sky.shape[0], turn_sky, 0)

    def exchange(first, second, keep, by):
        return (
            jnp.where(keep, first, pltpu.roll(second, by, 1)),
            jnp.where(keep, pltpu.roll(first, LANES - by, 1), second),
        )

    def side_by_side(members):
        a, c = exchange(members[0], members[2], low_half, 2 * W)
        b, d = exchange(members[1], members[3], low_half, 2 * W)
        a, b = exchange(a, b, even_group, W)
        c, d = exchange(c, d, even_group, W)
        return jnp.concatenate([a, c, b, d], axis=0).astype(jnp.bfloat16)

    def visit(quad, carry):
        for member in range(GROUP):
            turned(weights[quad * GROUP + member].astype(wide), stage.at[member])
        points = [meta[6, quad * GROUP + member] for member in range(GROUP)]
        for channel in range(CH_DEV):
            rows = pl.ds(channel * 8, 8)
            weight_quads[quad, channel] = side_by_side(
                [stage[member, rows, :] for member in range(GROUP)]
            )
            sky_quads[quad, channel] = side_by_side(
                [sky_stage[points[member], rows, :] for member in range(GROUP)]
            )
        return carry

    lax.fori_loop(0, quads, visit, 0)


def delta_kernel(meta, own, chip_a, chip_b, sibling, out, wide, turn):
    quads = (meta[5, 0] + GROUP - 1) // GROUP
    for block, value in enumerate((own, chip_a, chip_b, sibling.at[0], sibling.at[1])):
        wide[pl.ds(block * ST_DEV, ST_DEV)] = value[...].astype(jnp.float32)
    lane = lane_index(HALF_ROWS)

    def visit(quad, carry):
        real = jnp.zeros((HALF_ROWS, LANES), jnp.float32)
        imag = jnp.zeros((HALF_ROWS, LANES), jnp.float32)
        for member in range(GROUP):
            slot = quad * GROUP + member
            rows = pl.ds(meta[2, slot], HALF_ROWS)
            left = meta[3, slot]
            beam_p = wide[meta[0, slot], 0, rows, :]
            probe_p = wide[meta[0, slot], 1, rows, :]
            beam_q = wide[meta[1, slot], 0, rows, :]
            probe_q = wide[meta[1, slot], 1, rows, :]
            same = probe_p * beam_q + beam_p * probe_q
            cross = probe_p * swap_halves(beam_q) - swap_halves(beam_p) * probe_q
            sum_real = same + swap_halves(same)
            sum_imag = swap_halves(cross) - cross
            shift = lax.rem(member * W + 2 * G - left, 2 * G)
            mine = (lane >= member * W) & (lane < (member + 1) * W)
            real = jnp.where(mine, pltpu.roll(sum_real, shift, 1), real)
            imag = jnp.where(mine, pltpu.roll(sum_imag, shift, 1), imag)
        for part, value in enumerate((real, imag)):
            turn[part] = value
            out[quad, part] = jnp.concatenate(
                [turn[part, pl.ds(low, 8, stride=2), :] for low in range(2)], axis=0
            ).astype(jnp.bfloat16)
        return carry

    lax.fori_loop(0, quads, visit, 0)


def hessian_kernel(
    meta, mine, over_four, over_two, weights_0, weights_1, sky_0, sky_1, tables, kept, sent
):
    quads = (meta[5, 0] + GROUP - 1) // GROUP
    delta = ((mine, over_four), (over_two.at[0], over_two.at[1]))
    grads = (kept, sent)
    lane = lane_index(HALF_ROWS)
    right_forward, left_forward = tables[0], tables[1]
    right_inverse, left_inverse = tables[2], tables[3]
    wide = jnp.float32
    half_type = jnp.bfloat16

    def weight(quad, channel):
        return (weights_0, weights_1)[channel // CH_DEV][quad, channel % CH_DEV].astype(wide)

    def bright(quad, channel):
        return (sky_0, sky_1)[channel // CH_DEV][quad, channel % CH_DEV].astype(wide)

    def dot(a, b):
        return jnp.dot(a, b, preferred_element_type=wide)

    def to_rows(value):
        groups = []
        for group in range(POLS_DEV * CHANNELS // GROUP):
            pieces = []
            for member in range(GROUP):
                first = (group * GROUP + member) * W
                for part in range(2):
                    pieces.append(value[first : first + W, part * LANES : (part + 1) * LANES])
            groups.append(jnp.concatenate(pieces, axis=0))
        return jnp.concatenate(groups, axis=1)

    def piece(value, pol, channel, part):
        group, member = pol * (CHANNELS // GROUP) + channel // GROUP, channel % GROUP
        first = (member * 2 + part) * W
        return value[first : first + W, group * LANES : (group + 1) * LANES]

    def visit(quad, carry):
        odd = jnp.full((HALF_ROWS, LANES), meta[7, quad * GROUP], jnp.int32)
        for member in range(1, GROUP):
            odd = jnp.where(lane >= member * W, meta[7, quad * GROUP + member], odd)
        odd = odd > 0

        def both_rows(pol, part):
            first, second = (value[quad, part].astype(wide) for value in delta[pol])
            return jnp.concatenate(
                [jnp.where(odd, second, first), jnp.where(odd, first, second)], axis=0
            )

        images = [[both_rows(pol, part) for part in range(2)] for pol in range(POLS_DEV)]
        lifted = jnp.concatenate(
            [
                jnp.concatenate(
                    [
                        (bright(quad, channel) * images[pol][part]).astype(half_type)
                        for part in range(2)
                    ],
                    axis=1,
                )
                for pol in range(POLS_DEV)
                for channel in range(CHANNELS)
            ],
            axis=0,
        )
        middle = dot(lifted, right_forward).astype(half_type)
        freq = dot(left_forward, to_rows(middle))
        weighted = jnp.concatenate(
            [
                jnp.concatenate(
                    [
                        (
                            piece(freq, pol, channel, part) * weight(quad, channel)
                        ).astype(half_type)
                        for part in range(2)
                    ],
                    axis=1,
                )
                for pol in range(POLS_DEV)
                for channel in range(CHANNELS)
            ],
            axis=0,
        )
        middle = dot(weighted, right_inverse).astype(half_type)
        back = dot(left_inverse, to_rows(middle))
        for pol in range(POLS_DEV):
            for part in range(2):
                total = bright(quad, 0) * piece(back, pol, 0, part)
                for channel in range(1, CHANNELS):
                    total = total + bright(quad, channel) * piece(
                        back, pol, channel, part
                    )
                even_rows, odd_rows = total[:HALF_ROWS], total[HALF_ROWS:]
                chunks = (
                    jnp.where(odd, odd_rows, even_rows),
                    jnp.where(odd, even_rows, odd_rows),
                )
                for half in range(HALVES):
                    grads[pol][half, quad, part] = chunks[half].astype(half_type)
        return carry

    lax.fori_loop(0, quads, visit, 0)


def product_kernel(
    channels_total,
    meta,
    kept,
    over_two,
    over_four,
    own,
    chip_a,
    chip_b,
    sibling,
    out_own,
    out_chips,
    out_sibling,
    beams,
    totals,
    turn,
):
    live = meta[5, 0]
    quads = (live + GROUP - 1) // GROUP
    for block, value in enumerate((own, chip_a, chip_b, sibling.at[0], sibling.at[1])):
        beams[pl.ds(block * ST_DEV, ST_DEV)] = value[:, 0].astype(jnp.float32)
    totals[...] = jnp.zeros_like(totals)
    lane = lane_index(HALF_ROWS)
    column = lax.rem(lane, G)
    upper = lane >= G
    scale = 1.0 / channels_total

    def visit(quad, carry):
        for part in range(2):
            total = kept[0, quad, part].astype(jnp.float32)
            total = total + over_two[0, quad, part].astype(jnp.float32)
            total = total + over_four[quad, part].astype(jnp.float32)
            total = total * scale
            for low in range(2):
                turn[part, pl.ds(low, 8, stride=2), :] = total[low * 8 : (low + 1) * 8]
        real, imag = turn[0], turn[1]
        for member in range(GROUP):
            slot = quad * GROUP + member
            rows = pl.ds(meta[2, slot], HALF_ROWS)
            left = meta[3, slot]
            station_p, station_q = meta[0, slot], meta[1, slot]
            low = lax.rem(left + 2 * G - member * W, 2 * G)
            high = lax.rem(left + 3 * G - member * W, 2 * G)
            inside = (column >= left) & (column < left + W) & (slot < live)

            def placed(value):
                both = jnp.where(upper, pltpu.roll(value, high, 1), pltpu.roll(value, low, 1))
                return jnp.where(inside, both, 0.0)

            grad_real = placed(real)
            grad_imag = placed(imag)
            grad_imag = jnp.where(upper, grad_imag, -grad_imag)
            beam_p = beams[station_p, rows, :]
            beam_q = beams[station_q, rows, :]
            totals[station_p, rows, :] += beam_q * grad_real + swap_halves(beam_q) * grad_imag
            totals[station_q, rows, :] += beam_p * grad_real - swap_halves(beam_p) * grad_imag
        return carry

    lax.fori_loop(0, quads, visit, 0)
    out_own[...] = totals[:ST_DEV]
    for block in range(2):
        out_chips[block] = totals[pl.ds((1 + block) * ST_DEV, ST_DEV)]
        out_sibling[block] = totals[pl.ds((3 + block) * ST_DEV, ST_DEV)].astype(jnp.bfloat16)


def result_kernel(meta, mine, over_four, over_two, over_one, out, stage):
    half, low, high = meta[4, 0], meta[9, 0], meta[10, 0]
    lane = lane_index(G // 2)
    lower = lane < G
    own_first = jnp.full((G // 2, 2 * G), half, jnp.int32) == 0
    pairs = (
        (mine, over_four),
        (over_two.at[0], over_two.at[1]),
        (over_one.at[0], over_one.at[1]),
        (over_one.at[2], over_one.at[3]),
    )
    for turn, (same, other) in enumerate(pairs):
        pol = (high ^ (turn // 2)) * 2 + (low ^ (turn % 2))
        for station in range(ST_DEV):
            a = same[station].astype(jnp.float32)
            b = other[station].astype(jnp.float32)
            even, odd = jnp.where(own_first, a, b), jnp.where(own_first, b, a)
            real = jnp.where(lower, even, swap_halves(odd))
            imag = jnp.where(lower, swap_halves(even), odd)
            stage[station, pl.ds(pol, G // 2, stride=2 * POLS), :] = real
            stage[station, pl.ds(pol + POLS, G // 2, stride=2 * POLS), :] = imag
    for station in range(ST_DEV):
        for pair in range(G // 2):
            out[station, :, pair * 2 * G : (pair + 1) * 2 * G] = stage[
                station, pair * 2 * POLS : (pair + 1) * 2 * POLS, :
            ]


def call(kernel, out_shape, in_specs, scratch_shapes):
    return pl.pallas_call(
        kernel,
        out_shape=out_shape,
        in_specs=in_specs,
        out_specs=jax.tree.map(lambda _: pl.BlockSpec(memory_space=VMEM), out_shape),
        scratch_shapes=scratch_shapes,
        compiler_params=pltpu.CompilerParams(vmem_limit_bytes=48 * 1024 * 1024),
    )


def per_device(screens, direction, sky, weights, pairs, pointing, counts):
    base_count = lax.axis_size("base")
    myself = lax.axis_index("base")
    channels_total = CH_DEV * lax.axis_size("chan")
    part = lax.axis_index("chan") ^ (4 * turned_half(myself, base_count))
    pol_high, pol_low, half = part % 2, part // 2 % 2, part // 4
    core, chip_odd = myself % 2, myself // 2 % 2
    in_smem = pl.BlockSpec(memory_space=SMEM)
    in_vmem = pl.BlockSpec(memory_space=VMEM)

    weights_other = across_chan(weights, 1)
    sky_other = across_chan(sky, 1)

    stacked = jnp.stack([screens, direction], axis=1).reshape(ST_DEV, 2, 2, POLS, G // 2, 2, G)
    own = lax.dynamic_index_in_dim(stacked, pol_high * 2 + pol_low, 3, keepdims=False)
    own = lax.dynamic_index_in_dim(own, half, 4, keepdims=False)
    own = jnp.concatenate([own[:, :, 0], own[:, :, 1]], axis=-1)
    chip_a = across_chips(own, 0)
    chip_b = across_chips(own, 1)
    shared_is_a = core == chip_odd
    sibling = to_sibling(jnp.stack([own, jnp.where(shared_is_a, chip_a, chip_b)]))
    near = (own, chip_a, chip_b, sibling)

    alive = jnp.arange(SUB_DEV, dtype=jnp.int32) < counts[0]
    offset = (pairs // ST_DEV - myself + REACH) % base_count - REACH
    block = jnp.where(
        offset == 0,
        0,
        jnp.where(
            jnp.abs(offset) == 2,
            1 + ((offset == 2) == (chip_odd == 1)),
            3 + ((offset == 1) == (core == 1)),
        ),
    )
    local = jnp.where(alive[:, None], block * ST_DEV + pairs % ST_DEV, 0)
    row_start = pointing // 4 * (G - W) // 3

    def spread(value):
        return jnp.broadcast_to(value, (SUB_DEV,))

    meta = jnp.stack(
        [
            local[:, 0],
            local[:, 1],
            (row_start + 1 - half) // 2,
            pointing % 4 * (G - W) // 3,
            spread(half),
            spread(counts[0]),
            pointing,
            row_start % 2 ^ half,
            spread(0),
            spread(pol_low),
            spread(pol_high),
        ]
    ).astype(jnp.int32)

    def prepared(weights, sky):
        quad_shape = (QUADS, CH_DEV, W, LANES)
        return call(
            prep_kernel,
            [jax.ShapeDtypeStruct(quad_shape, jnp.bfloat16)] * 2,
            [in_smem] + [in_vmem] * 2,
            [
                pltpu.VMEM((GROUP, CH_DEV * 8, LANES), jnp.float32),
                pltpu.VMEM((sky.shape[0], CH_DEV * 8, LANES), jnp.float32),
            ],
        )(meta, weights, sky)

    weights_0, sky_0 = prepared(weights, sky)
    weights_1, sky_1 = prepared(weights_other, sky_other)

    chunk_shape = (QUADS, 2, HALF_ROWS, LANES)
    turn = pltpu.VMEM((2, HALF_ROWS, LANES), jnp.float32)
    delta = call(
        delta_kernel,
        jax.ShapeDtypeStruct(chunk_shape, jnp.bfloat16),
        [in_smem] + [in_vmem] * len(near),
        [pltpu.VMEM((NEAR * ST_DEV, 2, G // 2, 2 * G), jnp.float32), turn],
    )(meta, *near)
    over_four = across_chan(delta, 4)
    over_two = across_chan(jnp.stack([delta, over_four]), 2)

    kept, sent = call(
        hessian_kernel,
        [jax.ShapeDtypeStruct((HALVES,) + chunk_shape, jnp.bfloat16)] * 2,
        [in_smem] + [in_vmem] * 8,
        [],
    )(
        meta, delta, over_four, over_two, weights_0, weights_1, sky_0, sky_1, pass_tables()
    )
    wide = jnp.float32
    back_two = across_chan(sent, 2)
    other_half = kept[1].astype(wide) + back_two[1].astype(wide)
    back_four = across_chan(other_half.astype(jnp.bfloat16), 4)

    def make_product(*args):
        return product_kernel(channels_total, *args)

    table = pltpu.VMEM((NEAR * ST_DEV, G // 2, 2 * G), wide)
    block_shape = (ST_DEV, G // 2, 2 * G)
    sum_own, sum_chips, sum_sibling = call(
        make_product,
        [
            jax.ShapeDtypeStruct(block_shape, wide),
            jax.ShapeDtypeStruct((2,) + block_shape, wide),
            jax.ShapeDtypeStruct((2,) + block_shape, jnp.bfloat16),
        ],
        [in_smem] + [in_vmem] * (3 + len(near)),
        [table, table, turn],
    )(meta, kept, back_two, back_four, *near)
    from_sibling = to_sibling(sum_sibling).astype(wide)
    sum_a = sum_chips[0] + jnp.where(shared_is_a, from_sibling[1], 0.0)
    sum_b = sum_chips[1] + jnp.where(shared_is_a, 0.0, from_sibling[1])
    from_b = across_chips(sum_b.astype(jnp.bfloat16), 1)
    from_a = across_chips(sum_a.astype(jnp.bfloat16), 0)
    mine = sum_own + from_sibling[0] + from_a.astype(wide) + from_b.astype(wide)
    mine = mine.astype(jnp.bfloat16)
    over_four = across_chan(mine, 4)
    pair = jnp.stack([mine, over_four])
    over_two = across_chan(pair, 2)
    over_one = across_chan(jnp.concatenate([pair, over_two]), 1)
    return call(
        result_kernel,
        jax.ShapeDtypeStruct((ST_DEV, 2 * POLS, G * G), wide),
        [in_smem] + [in_vmem] * 4,
        [pltpu.VMEM((ST_DEV, G // 2 * 2 * POLS, 2 * G), wide)],
    )(meta, mine, over_four, over_two, over_one)


def solution(mesh):
    in_specs = (
        P("base", None, None),
        P("base", None, None),
        P(None, "chan", None),
        P("base", "chan", None),
        P("base", None),
        P("base"),
        P("base"),
    )
    out_specs = P("base", None, None)
    return jax.shard_map(
        per_device, mesh=mesh, in_specs=in_specs, out_specs=out_specs, check_vma=False
    )
```

time: 230 us -> 140 us (0.61)
  the two profiles are of different devices: /device:TPU:0 before, /device:TPU:64 now
where the time goes in v2:
time: 140 us; the launch traced here: 139 us
  starting transfers between devices  54.1 us (39%)
  waiting for transfers between devices  48.5 us (35%)
  Pallas kernels  19.6 us (14%)
  local copies, waits for them, and re-layouts  11.6 us (8%)
  other arithmetic  4.35 us (3%)
    ppermute x9, waiting for transfers between devices, across_chan(): return lax.ppermute(value, 'chan', [(i, i ^ bit) for i in range(count)])  33.9 us
    ppermute x9, starting transfers between devices, across_chan(): return lax.ppermute(value, 'chan', [(i, i ^ bit) for i in range(count)])  28.8 us
    ppermute x4, starting transfers between devices, across_chips(): return lax.ppermute(value, ('chan', 'base'), perm)  21.5 us
    ppermute x4, waiting for transfers between devices, across_chips(): return lax.ppermute(value, ('chan', 'base'), perm)  12.4 us
    pallas_call x1, Pallas kernels, per_device(): call(hessian_kernel, [jax.ShapeDtypeStruct((HALVES,) + chunk_shape, jnp.b...  8.43 us
    pallas_call x2, Pallas kernels, prepared(): call(prep_kernel, [jax.ShapeDtypeStruct(quad_shape, jnp.bfloat16)] * 2, [...  5.18 us
    ppermute x2, starting transfers between devices, to_sibling(): return lax.ppermute(value, 'base', [(i, i ^ 1) for i in range(count)])  3.84 us
  transfers between devices with their start and end apart: 15, of which 10 were waited for; matrix products, arithmetic and copies ran while one was open for 8% of the time, Pallas kernels for 6%

profile of v2, /device:TPU:64, one launch (start us, length us, event | category | flops | bytes accessed | tf_op | source)
XLA Modules:
  0.0 139.3 jit_solution(5606888573609462037)
XLA Ops:
  0.0 1.5 %stack.74 = bf16[4,1,2,4,32,2,64]{6,5,4,3,2,0,1:T(2,128)(2,1)S(1)} reshape(bf16[4,8,4096]{2,1,0:T(8,128)(2,1)} %param.8) | data formatting | bytes 524288 | tf_op jit(solution)/shard_map/stack | solution.py:388
  1.5 0.1 copy.9
  1.6 0.8 copy-done.2
  2.4 0.5 stack.75
  3.0 0.1 copy.10
  3.2 0.1 pad_maximum_fusion.8.own.args_4_
  3.3 15.7 %collective-permute-start.1 = (bf16[4,2,32,128]{3,2,1,0:T(8,128)(2,1)S(1)}, bf16[4,2,32,128]{3,2,1,0:T(8,128)(2,1)S(1)}, u32[]{:S(2)}, u32[]{:S(2)}) collective-permute-start(bf16[4,2,32,128]{3,2,1,0:T(8,128)(2,1)S(1)} %pad_maximum_fusion.8.own.args_4_), channel_id=1, source_target_pairs={{0,318},{1,319},{2,4},{3,5},{4,2},{5,3},{6,8},{7,9},{8,6},{9,7},{1... | collective-permute-start | bytes 196616 | tf_op jit(solution)/shard_map/ppermute | solution.py:54
  19.0 1.9 %collective-permute-start = (bf16[4,2,32,128]{3,2,1,0:T(8,128)(2,1)S(1)}, bf16[4,2,32,128]{3,2,1,0:T(8,128)(2,1)S(1)}, u32[]{:S(2)}, u32[]{:S(2)}) collective-permute-start(bf16[4,2,32,128]{3,2,1,0:T(8,128)(2,1)S(1)} %pad_maximum_fusion.8.own.args_4_), channel_id=1, source_target_pairs={{0,2},{1,3},{2,0},{3,1},{4,6},{5,7},{6,4},{7,5},{8,10},{9,11},{10,... | collective-permute-start | bytes 196616 | tf_op jit(solution)/shard_map/ppermute | solution.py:54
  20.9 2.9 %collective-permute-start.6 = (bf16[16,8,1024]{2,1,0:T(8,128)(2,1)S(1)}, bf16[16,8,1024]{2,1,0:T(8,128)(2,1)S(1)}, u32[]{:S(2)}, u32[]{:S(2)}) collective-permute-start(bf16[16,8,1024]{2,1,0:T(8,128)(2,1)S(1)} %copy-done.1), channel_id=1, source_target_pairs={{0,64},{64,0},{128,192},{192,128},{256,320},{320,256},{384,448},{4... | collective-permute-start | bytes 786440 | tf_op jit(solution)/shard_map/ppermute | solution.py:33
  23.9 2.9 %collective-permute-start.5 = (bf16[32,8,1024]{2,1,0:T(8,128)(2,1)S(1)}, bf16[32,8,1024]{2,1,0:T(8,128)(2,1)S(1)}, u32[]{:S(2)}, u32[]{:S(2)}) collective-permute-start(bf16[32,8,1024]{2,1,0:T(8,128)(2,1)S(1)} %copy-done), channel_id=1, source_target_pairs={{0,64},{64,0},{128,192},{192,128},{256,320},{320,256},{384,448},{4... | collective-permute-start | bytes 1572872 | tf_op jit(solution)/shard_map/ppermute | solution.py:33
  26.8 0.1 sine_multiply_fusion
  27.6 0.7 copy-done.4
  28.3 0.6 copy-done.3
  29.0 0.6 copy-done.5
  29.6 0.6 gather_fusion
  30.2 0.1 reshape.176
  30.3 0.6 gather_fusion.3
  30.9 0.1 copy.12
  31.0 0.6 gather_fusion.4
  31.5 0.6 gather_fusion.1
  32.1 0.1 copy.11
  32.2 0.6 gather_fusion.2
  32.8 0.1 fusion.15
  32.9 0.1 copy.13
  32.9 0.1 copy.14
  33.2 1.9 %collective-permute-start.2 = (bf16[2,4,2,32,128]{4,3,2,1,0:T(8,128)(2,1)S(1)}, bf16[2,4,2,32,128]{4,3,2,1,0:T(8,128)(2,1)S(1)}, u32[]{:S(2)}, u32[]{:S(2)}) collective-permute-start(bf16[2,4,2,32,128]{4,3,2,1,0:T(8,128)(2,1)S(1)} %pad_maximum_fusion.5), channel_id=1, source_target_pairs={{0,1},{1,0},{2,3},{3,2},{4,5},{5,4},{6,7},{7,6},{8,9},{9,8},{10,11... | collective-permute-start | bytes 393224 | tf_op jit(solution)/shard_map/ppermute | solution.py:38
  35.1 0.3 fusion
  35.4 1.0 collective-permute-done.2.sibling.args_7_
  36.4 2.6 %shard_map.82.mine = bf16[8,2,16,128]{3,2,1,0:T(8,128)(2,1)S(1)} custom-call(s32[11,32]{1,0:T(8,128)S(1)} %stack.73.meta.args_0_, bf16[4,2,32,128]{3,2,1,0:T(8,128)(2,1)S(1)} %pad_maximum_fusion.8.own.args_4_, bf16[4,2,32,128]{3,2,1,0:T(8,128)(2,1)S(1)} %collective-permute-done.chip_a.args_5_, ...), custom_call_target="tpu_custom_call" | custom-call | tf_op jit(solution)/shard_map/pallas_call | solution.py:448
  39.0 5.5 %collective-permute-start.3 = (bf16[8,2,16,128]{3,2,1,0:T(8,128)(2,1)S(1)}, bf16[8,2,16,128]{3,2,1,0:T(8,128)(2,1)S(1)}, u32[]{:S(2)}, u32[]{:S(2)}) collective-permute-start(bf16[8,2,16,128]{3,2,1,0:T(8,128)(2,1)S(1)} %shard_map.82.mine), channel_id=1, source_target_pairs={{0,256},{64,320},{128,384},{192,448},{256,0},{320,64},{384,128},{4... | collective-permute-start | bytes 196616 | tf_op jit(solution)/shard_map/ppermute | solution.py:33
  44.4 0.9 multiply_convert_fusion.1
  45.4 0.1 reshape.182
  45.5 0.1 reshape.180
  45.6 0.1 reshape.185
  45.8 0.1 reshape.184
  45.9 0.1 reshape.177
  46.0 4.0 %collective-permute-done.3.over_four = bf16[8,2,16,128]{3,2,1,0:T(8,128)(2,1)S(1)} collective-permute-done((bf16[8,2,16,128]{3,2,1,0:T(8,128)(2,1)S(1)}, bf16[8,2,16,128]{3,2,1,0:T(8,128)(2,1)S(1)}, u32[]{:S(2)}, u32[]{:S(2)}) %collective-permute-start.3) | collective-permute-done | bytes 65568 | tf_op jit(solution)/shard_map/ppermute | solution.py:33
  50.1 0.7 pad_maximum_fusion.6
  50.7 6.0 %collective-permute-start.4 = (bf16[2,8,2,16,128]{4,3,2,1,0:T(8,128)(2,1)}, bf16[2,8,2,16,128]{4,3,2,1,0:T(8,128)(2,1)S(1)}, u32[]{:S(2)}, u32[]{:S(2)}) collective-permute-start(bf16[2,8,2,16,128]{4,3,2,1,0:T(8,128)(2,1)} %pad_maximum_fusion.6), channel_id=1, source_target_pairs={{0,128},{64,192},{128,0},{192,64},{256,384},{320,448},{384,256},{4... | collective-permute-start | bytes 393224 | tf_op jit(solution)/shard_map/ppermute | solution.py:33
  56.7 0.7 fusion.6
  57.4 2.6 %shard_map.83 = (bf16[8,8,32,128]{3,2,1,0:T(8,128)(2,1)S(1)}, bf16[8,8,32,128]{3,2,1,0:T(8,128)(2,1)S(1)}) custom-call(s32[11,32]{1,0:T(8,128)S(1)} %stack.73.meta.args_0_, bf16[32,8,1024]{2,1,0:T(8,128)(2,1)S(1)} %copy-done, bf16[16,8,1024]{2,1,0:T(8,128)(2,1)S(1)} %copy-done.1), custom_call_target="tpu_custom_call" | custom-call | tf_op jit(solution)/shard_map/pallas_call | solution.py:433
  60.0 1.8 %mul.348 = bf16[1,256,256]{2,1,0:T(8,128)(2,1)} reshape(bf16[4,64,4,64]{3,2,1,0:T(4,128)(2,1)} %get-tuple-element.38) | data formatting | bytes 262144 | tf_op jit(solution)/shard_map/jit(kron)/mul | solution.py:73
  61.9 0.9 mul.351
  62.7 1.2 pad_maximum_fusion.tables
  63.9 2.6 %shard_map.84 = (bf16[8,8,32,128]{3,2,1,0:T(8,128)(2,1)S(1)}, bf16[8,8,32,128]{3,2,1,0:T(8,128)(2,1)S(1)}) custom-call(s32[11,32]{1,0:T(8,128)S(1)} %stack.73.meta.args_0_, bf16[32,8,1024]{2,1,0:T(8,128)(2,1)S(1)} %collective-permute-done.5.weights, bf16[16,8,1024]{2,1,0:T(8,128)(2,1)S(1)} %collective-permute-done.6.sky), custom_call_target="tpu_custom_call" | custom-call | tf_op jit(solution)/shard_map/pallas_call | solution.py:433
  66.5 8.4 %shard_map.85 = (bf16[2,8,2,16,128]{4,3,2,1,0:T(8,128)(2,1)S(1)}, bf16[2,8,2,16,128]{4,3,2,1,0:T(8,128)(2,1)S(1)}) custom-call(s32[11,32]{1,0:T(8,128)S(1)} %stack.73.meta.args_0_, bf16[8,2,16,128]{3,2,1,0:T(8,128)(2,1)S(1)} %shard_map.82.mine, bf16[8,2,16,128]{3,2,1,0:T(8,128)(2,1)S(1)} %collective-permute-done.3.over_four, ...), custom_call_target="tpu_custom_call" | custom-call | tf_op jit(solution)/shard_map/pallas_call | solution.py:457
  75.0 1.9 %collective-permute-start.7 = (bf16[2,8,2,16,128]{4,3,2,1,0:T(8,128)(2,1)S(1)}, bf16[2,8,2,16,128]{4,3,2,1,0:T(8,128)(2,1)S(1)}, u32[]{:S(2)}, u32[]{:S(2)}) collective-permute-start(bf16[2,8,2,16,128]{4,3,2,1,0:T(8,128)(2,1)S(1)} %get-tuple-element.19), channel_id=1, source_target_pairs={{0,128},{64,192},{128,0},{192,64},{256,384},{320,448},{384,256},{4... | collective-permute-start | bytes 393224 | tf_op jit(solution)/shard_map/ppermute | solution.py:33
  76.9 5.8 %collective-permute-done.7.args_2_ = bf16[2,8,2,16,128]{4,3,2,1,0:T(8,128)(2,1)S(1)} collective-permute-done((bf16[2,8,2,16,128]{4,3,2,1,0:T(8,128)(2,1)S(1)}, bf16[2,8,2,16,128]{4,3,2,1,0:T(8,128)(2,1)S(1)}, u32[]{:S(2)}, u32[]{:S(2)}) %collective-permute-start.7) | collective-permute-done | bytes 131104 | tf_op jit(solution)/shard_map/ppermute | solution.py:33
  82.7 2.8 %collective-permute-start.8 = (bf16[8,2,16,128]{3,2,1,0:T(8,128)(2,1)S(1)}, bf16[8,2,16,128]{3,2,1,0:T(8,128)(2,1)S(1)}, u32[]{:S(2)}, u32[]{:S(2)}) collective-permute-start(bf16[8,2,16,128]{3,2,1,0:T(8,128)(2,1)S(1)} %fusion.10), channel_id=1, source_target_pairs={{0,256},{64,320},{128,384},{192,448},{256,0},{320,64},{384,128},{4... | collective-permute-start | bytes 196616 | tf_op jit(solution)/shard_map/ppermute | solution.py:33
  85.5 7.3 %collective-permute-done.8.args_3_ = bf16[8,2,16,128]{3,2,1,0:T(8,128)(2,1)S(1)} collective-permute-done((bf16[8,2,16,128]{3,2,1,0:T(8,128)(2,1)S(1)}, bf16[8,2,16,128]{3,2,1,0:T(8,128)(2,1)S(1)}, u32[]{:S(2)}, u32[]{:S(2)}) %collective-permute-start.8) | collective-permute-done | bytes 65568 | tf_op jit(solution)/shard_map/ppermute | solution.py:33
  92.8 1.8 %shard_map.86 = (f32[4,32,128]{2,1,0:T(8,128)S(1)}, f32[2,4,32,128]{3,2,1,0:T(8,128)S(1)}, bf16[2,4,32,128]{3,2,1,0:T(8,128)(2,1)S(1)}) custom-call(s32[11,32]{1,0:T(8,128)S(1)} %stack.73.meta.args_0_, bf16[2,8,2,16,128]{4,3,2,1,0:T(8,128)(2,1)S(1)} %get-tuple-element.18.args_1_, bf16[2,8,2,16,128]{4,3,2,1,0:T(8,128)(2,1)S(1)} %collective-permute-done.7.args_2_, ...), custom_call_target="tpu_custom_call" | custom-call | tf_op jit(solution)/shard_map/pallas_call | solution.py:475
  94.6 1.9 %collective-permute-start.9 = (bf16[2,4,32,128]{3,2,1,0:T(8,128)(2,1)S(1)}, bf16[2,4,32,128]{3,2,1,0:T(8,128)(2,1)S(1)}, u32[]{:S(2)}, u32[]{:S(2)}) collective-permute-start(bf16[2,4,32,128]{3,2,1,0:T(8,128)(2,1)S(1)} %get-tuple-element.21), channel_id=1, source_target_pairs={{0,1},{1,0},{2,3},{3,2},{4,5},{5,4},{6,7},{7,6},{8,9},{9,8},{10,11... | collective-permute-start | bytes 196616 | tf_op jit(solution)/shard_map/ppermute | solution.py:38
  96.5 1.2 collective-permute-done.9
  97.8 1.9 %collective-permute-start.10 = (bf16[4,32,128]{2,1,0:T(8,128)(2,1)S(1)}, bf16[4,32,128]{2,1,0:T(8,128)(2,1)S(1)}, u32[]{:S(2)}, u32[]{:S(2)}) collective-permute-start(bf16[4,32,128]{2,1,0:T(8,128)(2,1)S(1)} %get-tuple-element.25), channel_id=1, source_target_pairs={{0,2},{1,3},{2,0},{3,1},{4,6},{5,7},{6,4},{7,5},{8,10},{9,11},{10,... | collective-permute-start | bytes 98312 | tf_op jit(solution)/shard_map/ppermute | solution.py:54
  99.7 1.9 %collective-permute-start.11 = (bf16[4,32,128]{2,1,0:T(8,128)(2,1)S(1)}, bf16[4,32,128]{2,1,0:T(8,128)(2,1)S(1)}, u32[]{:S(2)}, u32[]{:S(2)}) collective-permute-start(bf16[4,32,128]{2,1,0:T(8,128)(2,1)S(1)} %get-tuple-element.26), channel_id=1, source_target_pairs={{0,318},{1,319},{2,4},{3,5},{4,2},{5,3},{6,8},{7,9},{8,6},{9,7},{1... | collective-permute-start | bytes 98312 | tf_op jit(solution)/shard_map/ppermute | solution.py:54
  101.6 2.0 %collective-permute-done.10 = bf16[4,32,128]{2,1,0:T(8,128)(2,1)S(1)} collective-permute-done((bf16[4,32,128]{2,1,0:T(8,128)(2,1)S(1)}, bf16[4,32,128]{2,1,0:T(8,128)(2,1)S(1)}, u32[]{:S(2)}, u32[]{:S(2)}) %collective-permute-start.10) | collective-permute-done | bytes 32800 | tf_op jit(solution)/shard_map/ppermute | solution.py:54
  103.6 10.4 %collective-permute-done.11 = bf16[4,32,128]{2,1,0:T(8,128)(2,1)S(1)} collective-permute-done((bf16[4,32,128]{2,1,0:T(8,128)(2,1)S(1)}, bf16[4,32,128]{2,1,0:T(8,128)(2,1)S(1)}, u32[]{:S(2)}, u32[]{:S(2)}) %collective-permute-start.11) | collective-permute-done | bytes 32800 | tf_op jit(solution)/shard_map/ppermute | solution.py:54
  114.0 2.5 %collective-permute-start.12 = (bf16[4,32,128]{2,1,0:T(8,128)(2,1)S(1)}, bf16[4,32,128]{2,1,0:T(8,128)(2,1)S(1)}, u32[]{:S(2)}, u32[]{:S(2)}) collective-permute-start(bf16[4,32,128]{2,1,0:T(8,128)(2,1)S(1)} %fusion.14.mine), channel_id=1, source_target_pairs={{0,256},{64,320},{128,384},{192,448},{256,0},{320,64},{384,128},{4... | collective-permute-start | bytes 98312 | tf_op jit(solution)/shard_map/ppermute | solution.py:33
  116.5 7.3 %collective-permute-done.12.over_four = bf16[4,32,128]{2,1,0:T(8,128)(2,1)S(1)} collective-permute-done((bf16[4,32,128]{2,1,0:T(8,128)(2,1)S(1)}, bf16[4,32,128]{2,1,0:T(8,128)(2,1)S(1)}, u32[]{:S(2)}, u32[]{:S(2)}) %collective-permute-start.12) | collective-permute-done | bytes 32800 | tf_op jit(solution)/shard_map/ppermute | solution.py:33
  123.7 2.5 %collective-permute-start.13 = (bf16[2,4,32,128]{3,2,1,0:T(8,128)(2,1)S(1)}, bf16[2,4,32,128]{3,2,1,0:T(8,128)(2,1)S(1)}, u32[]{:S(2)}, u32[]{:S(2)}) collective-permute-start(bf16[2,4,32,128]{3,2,1,0:T(8,128)(2,1)S(1)} %pad_maximum_fusion.9), channel_id=1, source_target_pairs={{0,128},{64,192},{128,0},{192,64},{256,384},{320,448},{384,256},{4... | collective-permute-start | bytes 196616 | tf_op jit(solution)/shard_map/ppermute | solution.py:33
  126.2 4.6 %collective-permute-done.13.over_two = bf16[2,4,32,128]{3,2,1,0:T(8,128)(2,1)S(1)} collective-permute-done((bf16[2,4,32,128]{3,2,1,0:T(8,128)(2,1)S(1)}, bf16[2,4,32,128]{3,2,1,0:T(8,128)(2,1)S(1)}, u32[]{:S(2)}, u32[]{:S(2)}) %collective-permute-start.13) | collective-permute-done | bytes 65568 | tf_op jit(solution)/shard_map/ppermute | solution.py:33
  130.8 1.9 %collective-permute-start.14 = (bf16[4,4,32,128]{3,2,1,0:T(8,128)(2,1)S(1)}, bf16[4,4,32,128]{3,2,1,0:T(8,128)(2,1)S(1)}, u32[]{:S(2)}, u32[]{:S(2)}) collective-permute-start(bf16[4,4,32,128]{3,2,1,0:T(8,128)(2,1)S(1)} %pad_maximum_fusion.7), channel_id=1, source_target_pairs={{0,64},{64,0},{128,192},{192,128},{256,320},{320,256},{384,448},{4... | collective-permute-start | bytes 393224 | tf_op jit(solution)/shard_map/ppermute | solution.py:33
  132.7 4.9 %collective-permute-done.14.over_one = bf16[4,4,32,128]{3,2,1,0:T(8,128)(2,1)S(1)} collective-permute-done((bf16[4,4,32,128]{3,2,1,0:T(8,128)(2,1)S(1)}, bf16[4,4,32,128]{3,2,1,0:T(8,128)(2,1)S(1)}, u32[]{:S(2)}, u32[]{:S(2)}) %collective-permute-start.14) | collective-permute-done | bytes 131104 | tf_op jit(solution)/shard_map/ppermute | solution.py:33
  137.7 1.7 %shard_map.87 = f32[4,8,4096]{2,1,0:T(8,128)} custom-call(s32[11,32]{1,0:T(8,128)S(1)} %stack.73.meta.args_0_, bf16[4,32,128]{2,1,0:T(8,128)(2,1)S(1)} %fusion.14.mine, bf16[4,32,128]{2,1,0:T(8,128)(2,1)S(1)} %collective-permute-done.12.over_four, bf16[2,4,32,128]{3,2,1,0:T(8,128)(2,1)S(1)} %collective-permute-done.13.over_two, ...), custom_call_target="tpu_custom_call" | custom-call | tf_op jit(solution)/shard_map/pallas_call | solution.py:496
  (40 shorter events, 0.4 us)
Async XLA Ops:
  1.5 1.0 copy-start.2
  3.1 20.8 %copy-start = (bf16[32,8,1024]{2,1,0:T(8,128)(2,1)S(1)}, bf16[32,8,1024]{2,1,0:T(8,128)(2,1)}, u32[]{:S(2)}) copy-start(bf16[32,8,1024]{2,1,0:T(8,128)(2,1)} %weights.1) | copy-start | bytes 1572868
  3.1 17.8 %copy-start.1 = (bf16[16,8,1024]{2,1,0:T(8,128)(2,1)S(1)}, bf16[16,8,1024]{2,1,0:T(8,128)(2,1)}, u32[]{:S(2)}) copy-start(bf16[16,8,1024]{2,1,0:T(8,128)(2,1)} %sky.1) | copy-start | bytes 786436
  3.3 29.9 %collective-permute-start.1 = (bf16[4,2,32,128]{3,2,1,0:T(8,128)(2,1)S(1)}, bf16[4,2,32,128]{3,2,1,0:T(8,128)(2,1)S(1)}, u32[]{:S(2)}, u32[]{:S(2)}) collective-permute-start(bf16[4,2,32,128]{3,2,1,0:T(8,128)(2,1)S(1)} %pad_maximum_fusion.8.own.args_4_), channel_id=1, source_target_pairs={{0,318},{1,319},{2,4},{3,5},{4,2},{5,3},{6,8},{7,9},{8,6},{9,7},{1... | collective-permute-start | bytes 196616 | tf_op jit(solution)/shard_map/ppermute | solution.py:54
  19.0 14.1 %collective-permute-start = (bf16[4,2,32,128]{3,2,1,0:T(8,128)(2,1)S(1)}, bf16[4,2,32,128]{3,2,1,0:T(8,128)(2,1)S(1)}, u32[]{:S(2)}, u32[]{:S(2)}) collective-permute-start(bf16[4,2,32,128]{3,2,1,0:T(8,128)(2,1)S(1)} %pad_maximum_fusion.8.own.args_4_), channel_id=1, source_target_pairs={{0,2},{1,3},{2,0},{3,1},{4,6},{5,7},{6,4},{7,5},{8,10},{9,11},{10,... | collective-permute-start | bytes 196616 | tf_op jit(solution)/shard_map/ppermute | solution.py:54
  20.9 43.0 %collective-permute-start.6 = (bf16[16,8,1024]{2,1,0:T(8,128)(2,1)S(1)}, bf16[16,8,1024]{2,1,0:T(8,128)(2,1)S(1)}, u32[]{:S(2)}, u32[]{:S(2)}) collective-permute-start(bf16[16,8,1024]{2,1,0:T(8,128)(2,1)S(1)} %copy-done.1), channel_id=1, source_target_pairs={{0,64},{64,0},{128,192},{192,128},{256,320},{320,256},{384,448},{4... | collective-permute-start | bytes 786440 | tf_op jit(solution)/shard_map/ppermute | solution.py:33
  23.9 40.0 %collective-permute-start.5 = (bf16[32,8,1024]{2,1,0:T(8,128)(2,1)S(1)}, bf16[32,8,1024]{2,1,0:T(8,128)(2,1)S(1)}, u32[]{:S(2)}, u32[]{:S(2)}) collective-permute-start(bf16[32,8,1024]{2,1,0:T(8,128)(2,1)S(1)} %copy-done), channel_id=1, source_target_pairs={{0,64},{64,0},{128,192},{192,128},{256,320},{320,256},{384,448},{4... | collective-permute-start | bytes 1572872 | tf_op jit(solution)/shard_map/ppermute | solution.py:33
  27.6 0.7 copy-start.4
  28.3 0.7 copy-start.3
  29.0 0.7 copy-start.5
  33.2 3.2 %collective-permute-start.2 = (bf16[2,4,2,32,128]{4,3,2,1,0:T(8,128)(2,1)S(1)}, bf16[2,4,2,32,128]{4,3,2,1,0:T(8,128)(2,1)S(1)}, u32[]{:S(2)}, u32[]{:S(2)}) collective-permute-start(bf16[2,4,2,32,128]{4,3,2,1,0:T(8,128)(2,1)S(1)} %pad_maximum_fusion.5), channel_id=1, source_target_pairs={{0,1},{1,0},{2,3},{3,2},{4,5},{5,4},{6,7},{7,6},{8,9},{9,8},{10,11... | collective-permute-start | bytes 393224 | tf_op jit(solution)/shard_map/ppermute | solution.py:38
  39.0 11.1 %collective-permute-start.3 = (bf16[8,2,16,128]{3,2,1,0:T(8,128)(2,1)S(1)}, bf16[8,2,16,128]{3,2,1,0:T(8,128)(2,1)S(1)}, u32[]{:S(2)}, u32[]{:S(2)}) collective-permute-start(bf16[8,2,16,128]{3,2,1,0:T(8,128)(2,1)S(1)} %shard_map.82.mine), channel_id=1, source_target_pairs={{0,256},{64,320},{128,384},{192,448},{256,0},{320,64},{384,128},{4... | collective-permute-start | bytes 196616 | tf_op jit(solution)/shard_map/ppermute | solution.py:33
  50.7 15.8 %collective-permute-start.4 = (bf16[2,8,2,16,128]{4,3,2,1,0:T(8,128)(2,1)}, bf16[2,8,2,16,128]{4,3,2,1,0:T(8,128)(2,1)S(1)}, u32[]{:S(2)}, u32[]{:S(2)}) collective-permute-start(bf16[2,8,2,16,128]{4,3,2,1,0:T(8,128)(2,1)} %pad_maximum_fusion.6), channel_id=1, source_target_pairs={{0,128},{64,192},{128,0},{192,64},{256,384},{320,448},{384,256},{4... | collective-permute-start | bytes 393224 | tf_op jit(solution)/shard_map/ppermute | solution.py:33
  75.0 7.8 %collective-permute-start.7 = (bf16[2,8,2,16,128]{4,3,2,1,0:T(8,128)(2,1)S(1)}, bf16[2,8,2,16,128]{4,3,2,1,0:T(8,128)(2,1)S(1)}, u32[]{:S(2)}, u32[]{:S(2)}) collective-permute-start(bf16[2,8,2,16,128]{4,3,2,1,0:T(8,128)(2,1)S(1)} %get-tuple-element.19), channel_id=1, source_target_pairs={{0,128},{64,192},{128,0},{192,64},{256,384},{320,448},{384,256},{4... | collective-permute-start | bytes 393224 | tf_op jit(solution)/shard_map/ppermute | solution.py:33
  82.7 10.1 %collective-permute-start.8 = (bf16[8,2,16,128]{3,2,1,0:T(8,128)(2,1)S(1)}, bf16[8,2,16,128]{3,2,1,0:T(8,128)(2,1)S(1)}, u32[]{:S(2)}, u32[]{:S(2)}) collective-permute-start(bf16[8,2,16,128]{3,2,1,0:T(8,128)(2,1)S(1)} %fusion.10), channel_id=1, source_target_pairs={{0,256},{64,320},{128,384},{192,448},{256,0},{320,64},{384,128},{4... | collective-permute-start | bytes 196616 | tf_op jit(solution)/shard_map/ppermute | solution.py:33
  94.6 3.1 %collective-permute-start.9 = (bf16[2,4,32,128]{3,2,1,0:T(8,128)(2,1)S(1)}, bf16[2,4,32,128]{3,2,1,0:T(8,128)(2,1)S(1)}, u32[]{:S(2)}, u32[]{:S(2)}) collective-permute-start(bf16[2,4,32,128]{3,2,1,0:T(8,128)(2,1)S(1)} %get-tuple-element.21), channel_id=1, source_target_pairs={{0,1},{1,0},{2,3},{3,2},{4,5},{5,4},{6,7},{7,6},{8,9},{9,8},{10,11... | collective-permute-start | bytes 196616 | tf_op jit(solution)/shard_map/ppermute | solution.py:38
  97.8 5.8 %collective-permute-start.10 = (bf16[4,32,128]{2,1,0:T(8,128)(2,1)S(1)}, bf16[4,32,128]{2,1,0:T(8,128)(2,1)S(1)}, u32[]{:S(2)}, u32[]{:S(2)}) collective-permute-start(bf16[4,32,128]{2,1,0:T(8,128)(2,1)S(1)} %get-tuple-element.25), channel_id=1, source_target_pairs={{0,2},{1,3},{2,0},{3,1},{4,6},{5,7},{6,4},{7,5},{8,10},{9,11},{10,... | collective-permute-start | bytes 98312 | tf_op jit(solution)/shard_map/ppermute | solution.py:54
  99.7 14.3 %collective-permute-start.11 = (bf16[4,32,128]{2,1,0:T(8,128)(2,1)S(1)}, bf16[4,32,128]{2,1,0:T(8,128)(2,1)S(1)}, u32[]{:S(2)}, u32[]{:S(2)}) collective-permute-start(bf16[4,32,128]{2,1,0:T(8,128)(2,1)S(1)} %get-tuple-element.26), channel_id=1, source_target_pairs={{0,318},{1,319},{2,4},{3,5},{4,2},{5,3},{6,8},{7,9},{8,6},{9,7},{1... | collective-permute-start | bytes 98312 | tf_op jit(solution)/shard_map/ppermute | solution.py:54
  114.0 9.7 %collective-permute-start.12 = (bf16[4,32,128]{2,1,0:T(8,128)(2,1)S(1)}, bf16[4,32,128]{2,1,0:T(8,128)(2,1)S(1)}, u32[]{:S(2)}, u32[]{:S(2)}) collective-permute-start(bf16[4,32,128]{2,1,0:T(8,128)(2,1)S(1)} %fusion.14.mine), channel_id=1, source_target_pairs={{0,256},{64,320},{128,384},{192,448},{256,0},{320,64},{384,128},{4... | collective-permute-start | bytes 98312 | tf_op jit(solution)/shard_map/ppermute | solution.py:33
  123.7 7.1 %collective-permute-start.13 = (bf16[2,4,32,128]{3,2,1,0:T(8,128)(2,1)S(1)}, bf16[2,4,32,128]{3,2,1,0:T(8,128)(2,1)S(1)}, u32[]{:S(2)}, u32[]{:S(2)}) collective-permute-start(bf16[2,4,32,128]{3,2,1,0:T(8,128)(2,1)S(1)} %pad_maximum_fusion.9), channel_id=1, source_target_pairs={{0,128},{64,192},{128,0},{192,64},{256,384},{320,448},{384,256},{4... | collective-permute-start | bytes 196616 | tf_op jit(solution)/shard_map/ppermute | solution.py:33
  130.8 6.9 %collective-permute-start.14 = (bf16[4,4,32,128]{3,2,1,0:T(8,128)(2,1)S(1)}, bf16[4,4,32,128]{3,2,1,0:T(8,128)(2,1)S(1)}, u32[]{:S(2)}, u32[]{:S(2)}) collective-permute-start(bf16[4,4,32,128]{3,2,1,0:T(8,128)(2,1)S(1)} %pad_maximum_fusion.7), channel_id=1, source_target_pairs={{0,64},{64,0},{128,192},{192,128},{256,320},{320,256},{384,448},{4... | collective-permute-start | bytes 393224 | tf_op jit(solution)/shard_map/ppermute | solution.py:33

commit v3 on v2

v3 whole, which is shorter than its diff:
```python
import functools
import math

import jax
import jax.numpy as jnp
import ml_dtypes
import numpy as np
from jax import lax
from jax.experimental import pallas as pl
from jax.experimental.pallas import tpu as pltpu
from jax.sharding import PartitionSpec as P

G = 64
W = 32
REACH = 2
ST_DEV = 4
SUB_DEV = 32
CH_DEV = 8
POLS = 4
HALVES = 2
GROUP = 4
QUADS = SUB_DEV // GROUP
HALF_ROWS = W // HALVES
PARTS = POLS * HALVES
LANES = GROUP * W
NEAR = 2 * REACH + 1
QUADS_STEP = 4
SETS = 2
SMEM = pltpu.SMEM
VMEM = pltpu.VMEM


def across_chan(value, bit):
    count = lax.axis_size("chan")
    return lax.ppermute(value, "chan", [(i, i ^ bit) for i in range(count)])


def to_sibling(value):
    count = lax.axis_size("base")
    return lax.ppermute(value, "base", [(i, i ^ 1) for i in range(count)])


def turned_half(base, base_count):
    return base * 2 // base_count


def across_chips(value, phase):
    base_count, chan_count = lax.axis_size("base"), lax.axis_size("chan")
    perm = []
    for chan in range(chan_count):
        for base in range(base_count):
            step = 2 if (base // 2 + phase) % 2 == 0 else -2
            target = (base + step) % base_count
            turn = turned_half(base, base_count) ^ turned_half(target, base_count)
            perm.append((chan * base_count + base, (chan ^ (4 * turn)) * base_count + target))
    return lax.ppermute(value, ("chan", "base"), perm)


def pass_tables():
    position = np.arange(W, dtype=np.int32)
    product = position[:, None] * position[None, :] % W
    angles = product.astype(np.float32) * np.float32(2.0 * math.pi / W)
    norm_factor = np.float32(1.0 / math.sqrt(W))
    cosine = np.cos(angles) * norm_factor
    sine = np.sin(angles) * norm_factor
    order = np.arange(W).reshape(8, 4).T[[0, 2, 1, 3]].reshape(W)
    cosine_rows, sine_rows = cosine[order][:, order], sine[order][:, order]
    eye = np.eye(GROUP, dtype=np.float32)

    def right(sign):
        cos_block, sin_block = np.kron(eye, cosine), sign * np.kron(eye, sine)
        return np.block([[cos_block, sin_block], [-sin_block, cos_block]])

    def left(sign):
        turn = np.block([[cosine_rows, -sign * sine_rows], [sign * sine_rows, cosine_rows]])
        return np.kron(eye, turn)

    tables = np.stack([right(-1.0), left(-1.0), right(1.0), left(1.0)])
    return jnp.asarray(tables.astype(ml_dtypes.bfloat16))


def swap_halves(value):
    return pltpu.roll(value, G, 1)


def lane_index(rows):
    return lax.broadcasted_iota(jnp.int32, (rows, 2 * G), 1)


def to_row_order(value, dest):
    for high in range(8):
        dest[pl.ds(high, CH_DEV, stride=8), :] = value[:, high * LANES : (high + 1) * LANES]


def exchange(first, second, keep, by):
    return (
        jnp.where(keep, first, pltpu.roll(second, by, 1)),
        jnp.where(keep, pltpu.roll(first, LANES - by, 1), second),
    )


def side_by_side(members):
    lane = lane_index(8)
    low_half = lane < 2 * W
    even_group = lax.rem(lane, 2 * W) < W
    a, c = exchange(members[0], members[2], low_half, 2 * W)
    b, d = exchange(members[1], members[3], low_half, 2 * W)
    a, b = exchange(a, b, even_group, W)
    c, d = exchange(c, d, even_group, W)
    return jnp.concatenate([a, c, b, d], axis=0).astype(jnp.bfloat16)


def weights_kernel(meta, weights, out, stage):
    def visit(quad, carry):
        for member in range(GROUP):
            value = weights[quad * GROUP + member].astype(jnp.float32)
            to_row_order(value, stage.at[member])
        for channel in range(CH_DEV):
            rows = pl.ds(channel * 8, 8)
            out[quad, channel] = side_by_side([stage[member, rows, :] for member in range(GROUP)])
        return carry

    lax.fori_loop(0, (meta[5, 0] + GROUP - 1) // GROUP, visit, 0)


def sky_kernel(first, meta, sky, out, stage):
    def turn(point, carry):
        to_row_order(sky[first + point].astype(jnp.float32), stage.at[point])
        return carry

    lax.fori_loop(0, stage.shape[0], turn, 0)

    def visit(quad, carry):
        points = [meta[6, quad * GROUP + member] for member in range(GROUP)]
        for channel in range(CH_DEV):
            rows = pl.ds(channel * 8, 8)
            out[quad, channel] = side_by_side([stage[point, rows, :] for point in points])
        return carry

    lax.fori_loop(0, (meta[5, 0] + GROUP - 1) // GROUP, visit, 0)


def own_kernel(screens, direction, out, stage):
    chan = lax.axis_index("chan")
    pol = chan % 2 * 2 + chan // 2 % 2
    lower = lane_index(G // 2) < G
    for station in range(ST_DEV):
        for kind, source in enumerate((screens, direction)):
            value = source[station].astype(jnp.float32)
            spot = stage.at[station * 2 + kind]
            for pair in range(G // 2):
                spot[pair * 2 * POLS : (pair + 1) * 2 * POLS, :] = value[
                    :, pair * 2 * G : (pair + 1) * 2 * G
                ]
            real = spot[pl.ds(pol, G // 2, stride=2 * POLS), :]
            imag = spot[pl.ds(pol + POLS, G // 2, stride=2 * POLS), :]
            even = jnp.where(lower, real, swap_halves(imag))
            odd = jnp.where(lower, swap_halves(real), imag)
            out[station, kind, 0] = even.astype(jnp.bfloat16)
            out[station, kind, 1] = odd.astype(jnp.bfloat16)


def group_index(rows):
    return lane_index(rows) // W


def delta_kernel(meta, own, chip_a, chip_b, sibling, out, beams, turned, probes, turn):
    quads = (meta[5, 0] + GROUP - 1) // GROUP
    for block, value in enumerate((own, chip_a, chip_b, sibling.at[0], sibling.at[1])):
        for member in range(ST_DEV):
            station = block * ST_DEV + member
            for half in range(HALVES):
                beam = value[member, 0, half].astype(jnp.float32)
                beams[station, half] = beam
                probes[station, half] = value[member, 1, half].astype(jnp.float32)
                turned[station, half] = swap_halves(beam)
    group = group_index(HALF_ROWS)

    def visit(quad, carry):
        for half in range(HALVES):
            same = [jnp.zeros((HALF_ROWS, LANES), jnp.float32)] * 2
            cross = [jnp.zeros((HALF_ROWS, LANES), jnp.float32)] * 2
            for member in range(GROUP):
                slot = quad * GROUP + member
                rows = pl.ds(meta[(2, 4)[half], slot], HALF_ROWS)
                station_p, station_q = meta[0, slot], meta[1, slot]
                probe_p = probes[station_p, half, rows, :]
                probe_q = probes[station_q, half, rows, :]
                beam_p = beams[station_p, half, rows, :]
                beam_q = beams[station_q, half, rows, :]
                sum_same = probe_p * beam_q + beam_p * probe_q
                sum_cross = (
                    probe_p * turned[station_q, half, rows, :]
                    - turned[station_p, half, rows, :] * probe_q
                )
                shift = lax.rem(member * W + 2 * G - meta[3, slot], 2 * G)
                sum_same = pltpu.roll(sum_same, shift, 1)
                sum_cross = pltpu.roll(sum_cross, shift, 1)
                for place in range(2):
                    mine = group == (member + 2 * place) % GROUP
                    same[place] = jnp.where(mine, sum_same, same[place])
                    cross[place] = jnp.where(mine, sum_cross, cross[place])
            real = same[0] + swap_halves(same[1])
            imag = swap_halves(cross[1]) - cross[0]
            for part, value in enumerate((real, imag)):
                turn[half, part] = value
                out[quad, part, half] = jnp.concatenate(
                    [turn[half, part, pl.ds(low, 8, stride=2), :] for low in range(2)], axis=0
                ).astype(jnp.bfloat16)
        return carry

    lax.fori_loop(0, quads, visit, 0)


def hessian_kernel(meta, delta, weights_0, weights_1, sky_0, sky_1, tables, out):
    quads = (meta[5, 0] + GROUP - 1) // GROUP
    lane = lane_index(HALF_ROWS)
    right_forward, left_forward = tables[0], tables[1]
    right_inverse, left_inverse = tables[2], tables[3]
    wide = jnp.float32
    half_type = jnp.bfloat16
    channels = SETS * CH_DEV
    images = [(member, channel) for member in range(QUADS_STEP) for channel in range(channels)]

    def weight(quad, channel):
        return (weights_0, weights_1)[channel // CH_DEV][quad, channel % CH_DEV]

    def bright(quad, channel):
        return (sky_0, sky_1)[channel // CH_DEV][quad, channel % CH_DEV]

    def dot(a, b):
        return jnp.dot(a, b, preferred_element_type=wide)

    def to_rows(value):
        groups = []
        for group in range(len(images) // GROUP):
            pieces = []
            for member in range(GROUP):
                first = (group * GROUP + member) * W
                for part in range(2):
                    pieces.append(value[first : first + W, part * LANES : (part + 1) * LANES])
            groups.append(jnp.concatenate(pieces, axis=0))
        return jnp.concatenate(groups, axis=1)

    def piece(value, image, part):
        group, member = image // GROUP, image % GROUP
        first = (member * 2 + part) * W
        return value[first : first + W, group * LANES : (group + 1) * LANES]

    def both_parts(make):
        return jnp.concatenate(
            [
                jnp.concatenate([make(image, part) for part in range(2)], axis=1)
                for image in range(len(images))
            ],
            axis=0,
        )

    def visit(step, carry):
        quad_of = [step * QUADS_STEP + member for member in range(QUADS_STEP)]
        odd = []
        for quad in quad_of:
            value = jnp.full((HALF_ROWS, LANES), meta[7, quad * GROUP], jnp.int32)
            for member in range(1, GROUP):
                value = jnp.where(lane >= member * W, meta[7, quad * GROUP + member], value)
            odd.append(value > 0)

        def both_rows(member, part):
            first, second = (
                delta[quad_of[member], part, half].astype(wide) for half in range(HALVES)
            )
            rows = [
                jnp.where(odd[member], second, first),
                jnp.where(odd[member], first, second),
            ]
            return jnp.concatenate(rows, axis=0).astype(half_type)

        fields = [
            [both_rows(member, part) for part in range(2)] for member in range(QUADS_STEP)
        ]

        def lift(image, part):
            member, channel = images[image]
            return bright(quad_of[member], channel) * fields[member][part]

        middle = dot(both_parts(lift), right_forward).astype(half_type)
        freq = dot(left_forward, to_rows(middle))

        def weigh(image, part):
            member, channel = images[image]
            factor = weight(quad_of[member], channel).astype(wide)
            return (piece(freq, image, part) * factor).astype(half_type)

        middle = dot(both_parts(weigh), right_inverse).astype(half_type)
        back = dot(left_inverse, to_rows(middle))
        for member, quad in enumerate(quad_of):
            for part in range(2):
                total = None
                for channel in range(channels):
                    term = bright(quad, channel).astype(wide) * piece(
                        back, images.index((member, channel)), part
                    )
                    total = term if total is None else total + term
                even_rows, odd_rows = total[:HALF_ROWS], total[HALF_ROWS:]
                chunks = (
                    jnp.where(odd[member], odd_rows, even_rows),
                    jnp.where(odd[member], even_rows, odd_rows),
                )
                for half in range(HALVES):
                    out[quad, part, half] = chunks[half].astype(half_type)
        return carry

    lax.fori_loop(0, (quads + QUADS_STEP - 1) // QUADS_STEP, visit, 0)


def product_kernel(
    channels_total,
    meta,
    kept,
    over_two,
    beams,
    turned,
    out_own,
    out_chips,
    out_sibling,
    totals,
    turn,
):
    live = meta[5, 0]
    quads = (live + GROUP - 1) // GROUP
    totals[...] = jnp.zeros_like(totals)
    group = group_index(HALF_ROWS)
    scale = 1.0 / channels_total

    def visit(quad, carry):
        for half in range(HALVES):
            for part in range(2):
                total = kept[quad, part, half].astype(jnp.float32)
                total = total + over_two[quad, part, half].astype(jnp.float32)
                total = total * scale
                for low in range(2):
                    turn[half, part, pl.ds(low, 8, stride=2), :] = total[low * 8 : (low + 1) * 8]
        for half in range(HALVES):
            real, imag = turn[half, 0], turn[half, 1]
            real_high, imag_high = swap_halves(real), swap_halves(imag)
            for member in range(GROUP):
                slot = quad * GROUP + member
                rows = pl.ds(meta[(2, 4)[half], slot], HALF_ROWS)
                station_p, station_q = meta[0, slot], meta[1, slot]
                shift = lax.rem(meta[3, slot] + 2 * G - member * W, 2 * G)
                alive = slot < live
                low = (group == member) & alive
                high = (group == (member + 2) % GROUP) & alive
                grad_real = jnp.where(low, real, jnp.where(high, real_high, 0.0))
                grad_imag = jnp.where(low, -imag, jnp.where(high, imag_high, 0.0))
                grad_real = pltpu.roll(grad_real, shift, 1)
                grad_imag = pltpu.roll(grad_imag, shift, 1)
                totals[station_p, half, rows, :] += (
                    beams[station_q, half, rows, :] * grad_real
                    + turned[station_q, half, rows, :] * grad_imag
                )
                totals[station_q, half, rows, :] += (
                    beams[station_p, half, rows, :] * grad_real
                    - turned[station_p, half, rows, :] * grad_imag
                )
        return carry

    lax.fori_loop(0, quads, visit, 0)
    out_own[...] = totals[:ST_DEV]
    for block in range(2):
        out_chips[block] = totals[pl.ds((1 + block) * ST_DEV, ST_DEV)]
        out_sibling[block] = totals[pl.ds((3 + block) * ST_DEV, ST_DEV)].astype(jnp.bfloat16)


def result_kernel(mine, over_two, over_one, out, stage):
    chan = lax.axis_index("chan")
    high, low = chan % 2, chan // 2 % 2
    lower = lane_index(G // 2) < G
    for turn, value in enumerate((mine, over_two, over_one.at[0], over_one.at[1])):
        pol = (high ^ (turn // 2)) * 2 + (low ^ (turn % 2))
        for station in range(ST_DEV):
            even = value[station, 0].astype(jnp.float32)
            odd = value[station, 1].astype(jnp.float32)
            real = jnp.where(lower, even, swap_halves(odd))
            imag = jnp.where(lower, swap_halves(even), odd)
            stage[station, pl.ds(pol, G // 2, stride=2 * POLS), :] = real
            stage[station, pl.ds(pol + POLS, G // 2, stride=2 * POLS), :] = imag
    for station in range(ST_DEV):
        for pair in range(G // 2):
            out[station, :, pair * 2 * G : (pair + 1) * 2 * G] = stage[
                station, pair * 2 * POLS : (pair + 1) * 2 * POLS, :
            ]


def call(kernel, out_shape, in_specs, scratch_shapes):
    return pl.pallas_call(
        kernel,
        out_shape=out_shape,
        in_specs=in_specs,
        out_specs=jax.tree.map(lambda _: pl.BlockSpec(memory_space=VMEM), out_shape),
        scratch_shapes=scratch_shapes,
        compiler_params=pltpu.CompilerParams(vmem_limit_bytes=48 * 1024 * 1024),
    )


def per_device(screens, direction, sky, weights, pairs, pointing, counts):
    base_count = lax.axis_size("base")
    myself = lax.axis_index("base")
    channels_total = CH_DEV * lax.axis_size("chan")
    core, chip_odd = myself % 2, myself // 2 % 2
    in_smem = pl.BlockSpec(memory_space=SMEM)
    in_vmem = pl.BlockSpec(memory_space=VMEM)

    alive = jnp.arange(SUB_DEV, dtype=jnp.int32) < counts[0]
    offset = (pairs // ST_DEV - myself + REACH) % base_count - REACH
    block = jnp.where(
        offset == 0,
        0,
        jnp.where(
            jnp.abs(offset) == 2,
            1 + ((offset == 2) == (chip_odd == 0)),
            3 + ((offset == 1) == (core == 1)),
        ),
    )
    local = jnp.where(alive[:, None], block * ST_DEV + pairs % ST_DEV, 0)
    row_start = pointing // 4 * (G - W) // 3

    def spread(value):
        return jnp.broadcast_to(value, (SUB_DEV,))

    meta = jnp.stack(
        [
            local[:, 0],
            local[:, 1],
            (row_start + 1) // 2,
            pointing % 4 * (G - W) // 3,
            row_start // 2,
            spread(counts[0]),
            pointing,
            row_start % 2,
        ]
    ).astype(jnp.int32)

    own = call(
        own_kernel,
        jax.ShapeDtypeStruct((ST_DEV, 2, HALVES, G // 2, 2 * G), jnp.bfloat16),
        [in_vmem] * 2,
        [pltpu.VMEM((2 * ST_DEV, G * POLS, 2 * G), jnp.float32)],
    )(screens, direction)
    chip_a = across_chips(own, 1)
    chip_b = across_chips(own, 0)
    other = across_chan(jnp.concatenate([weights, sky]), 1)
    shared_is_a = core != chip_odd
    sibling = to_sibling(jnp.stack([own, jnp.where(shared_is_a, chip_a, chip_b)]))

    delta_shape = (QUADS, 2, HALVES, HALF_ROWS, LANES)
    turn = pltpu.VMEM((HALVES, 2, HALF_ROWS, LANES), jnp.float32)
    field_shape = (NEAR * ST_DEV, HALVES, G // 2, 2 * G)
    field = pltpu.VMEM(field_shape, jnp.float32)
    delta, beams, turned = call(
        delta_kernel,
        [jax.ShapeDtypeStruct(delta_shape, jnp.bfloat16)]
        + [jax.ShapeDtypeStruct(field_shape, jnp.float32)] * 2,
        [in_smem] + [in_vmem] * 4,
        [field, turn],
    )(meta, own, chip_a, chip_b, sibling)
    over_two = across_chan(delta, 2)
    wide = jnp.float32
    tables = pass_tables()
    quad_shape = jax.ShapeDtypeStruct((QUADS, CH_DEV, W, LANES), jnp.bfloat16)

    def turned_sky(value, first):
        stage = pltpu.VMEM((sky.shape[0], CH_DEV * 8, LANES), wide)
        kernel = functools.partial(sky_kernel, first)
        return call(kernel, quad_shape, [in_smem, in_vmem], [stage])(meta, value)

    def turned_weights(value):
        stage = pltpu.VMEM((GROUP, CH_DEV * 8, LANES), wide)
        return call(weights_kernel, quad_shape, [in_smem, in_vmem], [stage])(meta, value)

    weighting = (turned_weights(weights), turned_weights(other))
    brightness = (turned_sky(sky, 0), turned_sky(other, SUB_DEV))

    def hessian(delta):
        return call(
            hessian_kernel,
            jax.ShapeDtypeStruct(delta_shape, jnp.bfloat16),
            [in_smem] + [in_vmem] * 6,
            [],
        )(meta, delta, *weighting, *brightness, tables)

    sent, delta = lax.optimization_barrier((hessian(over_two), delta))
    back_two = across_chan(sent, 2)
    kept = hessian(delta)

    def make_product(*args):
        return product_kernel(channels_total, *args)

    block_shape = (ST_DEV, HALVES, G // 2, 2 * G)
    sum_own, sum_chips, sum_sibling = call(
        make_product,
        [
            jax.ShapeDtypeStruct(block_shape, wide),
            jax.ShapeDtypeStruct((2,) + block_shape, wide),
            jax.ShapeDtypeStruct((2,) + block_shape, jnp.bfloat16),
        ],
        [in_smem] + [in_vmem] * 4,
        [field, turn],
    )(meta, kept, back_two, beams, turned)
    from_sibling = to_sibling(sum_sibling).astype(wide)
    sum_a = sum_chips[0] + jnp.where(shared_is_a, from_sibling[1], 0.0)
    sum_b = sum_chips[1] + jnp.where(shared_is_a, 0.0, from_sibling[1])
    from_a = across_chips(sum_a.astype(jnp.bfloat16), 1)
    from_b = across_chips(sum_b.astype(jnp.bfloat16), 0)
    mine = sum_own + from_sibling[0] + from_a.astype(wide) + from_b.astype(wide)
    mine = mine.astype(jnp.bfloat16)
    other = across_chan(mine, 4)
    mine = (mine.astype(wide) + other.astype(wide)).astype(jnp.bfloat16)
    over_two = across_chan(mine, 2)
    over_one = across_chan(jnp.stack([mine, over_two]), 1)
    return call(
        result_kernel,
        jax.ShapeDtypeStruct((ST_DEV, 2 * POLS, G * G), wide),
        [in_vmem] * 3,
        [pltpu.VMEM((ST_DEV, G // 2 * 2 * POLS, 2 * G), wide)],
    )(mine, over_two, over_one)


def solution(mesh):
    in_specs = (
        P("base", None, None),
        P("base", None, None),
        P(None, "chan", None),
        P("base", "chan", None),
        P("base", None),
        P("base"),
        P("base"),
    )
    out_specs = P("base", None, None)
    return jax.shard_map(
        per_device, mesh=mesh, in_specs=in_specs, out_specs=out_specs, check_vma=False
    )
```

time: 140 us -> 111 us (0.79)
  the two profiles are of different devices: /device:TPU:64 before, /device:TPU:32 now
where the time goes in v3:
time: 111 us; the launch traced here: 110 us
  starting transfers between devices  61.5 us (55%)
  waiting for transfers between devices  23.7 us (21%)
  Pallas kernels  19.4 us (17%)
  local copies, waits for them, and re-layouts  3.3 us (3%)
  other arithmetic  1.27 us (1%)
    ppermute x6, starting transfers between devices, across_chan(): return lax.ppermute(value, 'chan', [(i, i ^ bit) for i in range(count)])  32.5 us
    ppermute x4, starting transfers between devices, across_chips(): return lax.ppermute(value, ('chan', 'base'), perm)  25.2 us
    ppermute x6, waiting for transfers between devices, across_chan(): return lax.ppermute(value, 'chan', [(i, i ^ bit) for i in range(count)])  12.3 us
    ppermute x4, waiting for transfers between devices, across_chips(): return lax.ppermute(value, ('chan', 'base'), perm)  8.63 us
    pallas_call x2, Pallas kernels, hessian(): call(hessian_kernel, jax.ShapeDtypeStruct(delta_shape, jnp.bfloat16), [in...  7.12 us
    ppermute x2, starting transfers between devices, to_sibling(): return lax.ppermute(value, 'base', [(i, i ^ 1) for i in range(count)])  3.84 us
    pallas_call x2, Pallas kernels, turned_sky(): return call(kernel, quad_shape, [in_smem, in_vmem], [stage])(meta, value)  3.55 us
    pallas_call x2, Pallas kernels, turned_weights(): call(weights_kernel, quad_shape, [in_smem, in_vmem], [stage])(meta, value)  3.4 us
  transfers between devices with their start and end apart: 12, of which 9 were waited for; matrix products, arithmetic and copies ran while one was open for 1% of the time, Pallas kernels for 11%

profile of v3, /device:TPU:32, one launch (start us, length us, event | category | flops | bytes accessed | tf_op | source)
XLA Modules:
  0.0 110.1 jit_solution(2636724522419815499)
XLA Ops:
  0.0 0.0 copy-start
  0.0 0.0 copy-start.3
  0.0 1.0 copy-done.3
  1.0 0.0 copy-start.4
  1.0 0.9 copy-done.4
  2.0 0.2 shard_map.82.own
  2.2 16.5 %collective-permute-start = (bf16[4,2,2,32,128]{4,3,2,1,0:T(8,128)(2,1)S(1)}, bf16[4,2,2,32,128]{4,3,2,1,0:T(8,128)(2,1)S(1)}, u32[]{:S(2)}, u32[]{:S(2)}) collective-permute-start(bf16[4,2,2,32,128]{4,3,2,1,0:T(8,128)(2,1)S(1)} %shard_map.82.own), channel_id=1, source_target_pairs={{0,318},{1,319},{2,4},{3,5},{4,2},{5,3},{6,8},{7,9},{8,6},{9,7},{1... | collective-permute-start | bytes 393224 | tf_op jit(solution)/shard_map/ppermute | solution.py:56
  18.7 1.9 %collective-permute-start.1 = (bf16[4,2,2,32,128]{4,3,2,1,0:T(8,128)(2,1)S(1)}, bf16[4,2,2,32,128]{4,3,2,1,0:T(8,128)(2,1)S(1)}, u32[]{:S(2)}, u32[]{:S(2)}) collective-permute-start(bf16[4,2,2,32,128]{4,3,2,1,0:T(8,128)(2,1)S(1)} %shard_map.82.own), channel_id=1, source_target_pairs={{0,2},{1,3},{2,0},{3,1},{4,6},{5,7},{6,4},{7,5},{8,10},{9,11},{10,... | collective-permute-start | bytes 393224 | tf_op jit(solution)/shard_map/ppermute | solution.py:56
  20.6 0.0 copy-done
  20.6 1.0 pad_maximum_fusion
  21.6 2.9 %collective-permute-start.4 = (bf16[48,8,1024]{2,1,0:T(8,128)(2,1)S(1)}, bf16[48,8,1024]{2,1,0:T(8,128)(2,1)S(1)}, u32[]{:S(2)}, u32[]{:S(2)}) collective-permute-start(bf16[48,8,1024]{2,1,0:T(8,128)(2,1)S(1)} %pad_maximum_fusion), channel_id=1, source_target_pairs={{0,64},{64,0},{128,192},{192,128},{256,320},{320,256},{384,448},{4... | collective-permute-start | bytes 2359304 | tf_op jit(solution)/shard_map/ppermute | solution.py:35
  25.2 0.0 copy-start.6
  25.3 0.7 copy-done.6
  25.9 0.0 copy-start.5
  25.9 0.6 copy-done.5
  26.6 1.1 collective-permute-done.chip_a
  27.7 0.0 collective-permute-done.1.chip_b
  27.7 1.9 %collective-permute-start.2 = (bf16[2,4,2,2,32,128]{5,4,3,2,1,0:T(8,128)(2,1)S(1)}, bf16[2,4,2,2,32,128]{5,4,3,2,1,0:T(8,128)(2,1)S(1)}, u32[]{:S(2)}, u32[]{:S(2)}) collective-permute-start(bf16[2,4,2,2,32,128]{5,4,3,2,1,0:T(8,128)(2,1)S(1)} %pad_maximum_fusion.1), channel_id=1, source_target_pairs={{0,1},{1,0},{2,3},{3,2},{4,5},{5,4},{6,7},{7,6},{8,9},{9,8},{10,11... | collective-permute-start | bytes 786440 | tf_op jit(solution)/shard_map/ppermute | solution.py:40
  29.7 1.4 %collective-permute-done.2.sibling = bf16[2,4,2,2,32,128]{5,4,3,2,1,0:T(8,128)(2,1)S(1)} collective-permute-done((bf16[2,4,2,2,32,128]{5,4,3,2,1,0:T(8,128)(2,1)S(1)}, bf16[2,4,2,2,32,128]{5,4,3,2,1,0:T(8,128)(2,1)S(1)}, u32[]{:S(2)}, u32[]{:S(2)}) %collective-permute-start.2) | collective-permute-done | bytes 262176 | tf_op jit(solution)/shard_map/ppermute | solution.py:40
  31.1 2.0 %shard_map.83 = (bf16[8,2,2,16,128]{4,3,2,1,0:T(8,128)(2,1)S(1)}, f32[20,2,32,128]{3,2,1,0:T(8,128)S(1)}, f32[20,2,32,128]{3,2,1,0:T(8,128)S(1)}) custom-call(s32[8,32]{1,0:T(8,128)S(1)} %stack.41.meta.args_0_, bf16[4,2,2,32,128]{4,3,2,1,0:T(8,128)(2,1)S(1)} %shard_map.82.own, bf16[4,2,2,32,128]{4,3,2,1,0:T(8,128)(2,1)S(1)} %collective-permute-done.chip_a, ...), custom_call_target="tpu_custom_call" | custom-call | tf_op jit(solution)/shard_map/pallas_call | solution.py:460
  33.1 0.0 copy-start.2
  33.1 6.6 %collective-permute-start.3 = (bf16[8,2,2,16,128]{4,3,2,1,0:T(8,128)(2,1)S(1)}, bf16[8,2,2,16,128]{4,3,2,1,0:T(8,128)(2,1)S(1)}, u32[]{:S(2)}, u32[]{:S(2)}) collective-permute-start(bf16[8,2,2,16,128]{4,3,2,1,0:T(8,128)(2,1)S(1)} %get-tuple-element.14.delta), channel_id=1, source_target_pairs={{0,128},{64,192},{128,0},{192,64},{256,384},{320,448},{384,256},{4... | collective-permute-start | bytes 393224 | tf_op jit(solution)/shard_map/ppermute | solution.py:35
  39.8 1.7 %shard_map.84.weights_0 = bf16[8,8,32,128]{3,2,1,0:T(8,128)(2,1)S(1)} custom-call(s32[8,32]{1,0:T(8,128)S(1)} %stack.41.meta.args_0_, bf16[32,8,1024]{2,1,0:T(8,128)(2,1)S(1)} %copy-done), custom_call_target="tpu_custom_call" | custom-call | tf_op jit(solution)/shard_map/pallas_call | solution.py:479
  41.5 0.0 copy-done.2
  41.5 1.8 %shard_map.86.sky_0 = bf16[8,8,32,128]{3,2,1,0:T(8,128)(2,1)S(1)} custom-call(s32[8,32]{1,0:T(8,128)S(1)} %stack.41.meta.args_0_, bf16[16,8,1024]{2,1,0:T(8,128)(2,1)S(1)} %copy-done.2), custom_call_target="tpu_custom_call" | custom-call | tf_op jit(solution)/shard_map/pallas_call | solution.py:475
  43.3 3.5 %collective-permute-done.4.weights.sky = bf16[48,8,1024]{2,1,0:T(8,128)(2,1)S(1)} collective-permute-done((bf16[48,8,1024]{2,1,0:T(8,128)(2,1)S(1)}, bf16[48,8,1024]{2,1,0:T(8,128)(2,1)S(1)}, u32[]{:S(2)}, u32[]{:S(2)}) %collective-permute-start.4) | collective-permute-done | bytes 786464 | tf_op jit(solution)/shard_map/ppermute | solution.py:35
  46.8 1.7 %shard_map.85.weights_1 = bf16[8,8,32,128]{3,2,1,0:T(8,128)(2,1)S(1)} custom-call(s32[8,32]{1,0:T(8,128)S(1)} %stack.41.meta.args_0_, bf16[48,8,1024]{2,1,0:T(8,128)(2,1)S(1)} %collective-permute-done.4.weights.sky), custom_call_target="tpu_custom_call" | custom-call | tf_op jit(solution)/shard_map/pallas_call | solution.py:479
  48.5 0.0 copy-start.1
  48.5 1.8 %shard_map.87.sky_1 = bf16[8,8,32,128]{3,2,1,0:T(8,128)(2,1)S(1)} custom-call(s32[8,32]{1,0:T(8,128)S(1)} %stack.41.meta.args_0_, bf16[48,8,1024]{2,1,0:T(8,128)(2,1)S(1)} %collective-permute-done.4.weights.sky), custom_call_target="tpu_custom_call" | custom-call | tf_op jit(solution)/shard_map/pallas_call | solution.py:475
  50.3 0.0 collective-permute-done.3.delta
  50.3 0.0 copy-done.1
  50.3 3.6 %shard_map.88 = bf16[8,2,2,16,128]{4,3,2,1,0:T(8,128)(2,1)S(1)} custom-call(s32[8,32]{1,0:T(8,128)S(1)} %stack.41.meta.args_0_, bf16[8,2,2,16,128]{4,3,2,1,0:T(8,128)(2,1)S(1)} %collective-permute-done.3.delta, bf16[8,8,32,128]{3,2,1,0:T(8,128)(2,1)S(1)} %shard_map.84.weights_0, bf16[8,8,32,128]{3,2,1,0:T(8,128)(2,1)S(1)} %shard_map.85.weights_1, ...), custom_call_target="tpu_custom_call" | custom-call | tf_op jit(solution)/shard_map/pallas_call | solution.py:485
  53.8 3.4 %collective-permute-start.5 = (bf16[8,2,2,16,128]{4,3,2,1,0:T(8,128)(2,1)S(1)}, bf16[8,2,2,16,128]{4,3,2,1,0:T(8,128)(2,1)S(1)}, u32[]{:S(2)}, u32[]{:S(2)}) collective-permute-start(bf16[8,2,2,16,128]{4,3,2,1,0:T(8,128)(2,1)S(1)} %shard_map.88), channel_id=1, source_target_pairs={{0,128},{64,192},{128,0},{192,64},{256,384},{320,448},{384,256},{4... | collective-permute-start | bytes 393224 | tf_op jit(solution)/shard_map/ppermute | solution.py:35
  57.3 3.6 %shard_map.89.args_1_ = bf16[8,2,2,16,128]{4,3,2,1,0:T(8,128)(2,1)S(1)} custom-call(s32[8,32]{1,0:T(8,128)S(1)} %stack.41.meta.args_0_, bf16[8,2,2,16,128]{4,3,2,1,0:T(8,128)(2,1)S(1)} %get-tuple-element.14.delta, bf16[8,8,32,128]{3,2,1,0:T(8,128)(2,1)S(1)} %shard_map.84.weights_0, bf16[8,8,32,128]{3,2,1,0:T(8,128)(2,1)S(1)} %shard_map.85.weights_1, ...), custom_call_target="tpu_custom_call" | custom-call | tf_op jit(solution)/shard_map/pallas_call | solution.py:485
  60.8 0.8 collective-permute-done.5.args_2_
  61.6 2.2 %shard_map.90 = (f32[4,2,32,128]{3,2,1,0:T(8,128)S(1)}, f32[2,4,2,32,128]{4,3,2,1,0:T(8,128)S(1)}, bf16[2,4,2,32,128]{4,3,2,1,0:T(8,128)(2,1)S(1)}) custom-call(s32[8,32]{1,0:T(8,128)S(1)} %stack.41.meta.args_0_, bf16[8,2,2,16,128]{4,3,2,1,0:T(8,128)(2,1)S(1)} %shard_map.89.args_1_, bf16[8,2,2,16,128]{4,3,2,1,0:T(8,128)(2,1)S(1)} %collective-permute-done.5.args_2_, ...), custom_call_target="tpu_custom_call" | custom-call | tf_op jit(solution)/shard_map/pallas_call | solution.py:500
  63.8 1.9 %collective-permute-start.6 = (bf16[2,4,2,32,128]{4,3,2,1,0:T(8,128)(2,1)S(1)}, bf16[2,4,2,32,128]{4,3,2,1,0:T(8,128)(2,1)S(1)}, u32[]{:S(2)}, u32[]{:S(2)}) collective-permute-start(bf16[2,4,2,32,128]{4,3,2,1,0:T(8,128)(2,1)S(1)} %get-tuple-element.19), channel_id=1, source_target_pairs={{0,1},{1,0},{2,3},{3,2},{4,5},{5,4},{6,7},{7,6},{8,9},{9,8},{10,11... | collective-permute-start | bytes 393224 | tf_op jit(solution)/shard_map/ppermute | solution.py:40
  65.8 1.3 %collective-permute-done.6 = bf16[2,4,2,32,128]{4,3,2,1,0:T(8,128)(2,1)S(1)} collective-permute-done((bf16[2,4,2,32,128]{4,3,2,1,0:T(8,128)(2,1)S(1)}, bf16[2,4,2,32,128]{4,3,2,1,0:T(8,128)(2,1)S(1)}, u32[]{:S(2)}, u32[]{:S(2)}) %collective-permute-start.6) | collective-permute-done | bytes 131104 | tf_op jit(solution)/shard_map/ppermute | solution.py:40
  67.2 4.9 %collective-permute-start.7 = (bf16[4,2,32,128]{3,2,1,0:T(8,128)(2,1)S(1)}, bf16[4,2,32,128]{3,2,1,0:T(8,128)(2,1)S(1)}, u32[]{:S(2)}, u32[]{:S(2)}) collective-permute-start(bf16[4,2,32,128]{3,2,1,0:T(8,128)(2,1)S(1)} %get-tuple-element.23), channel_id=1, source_target_pairs={{0,318},{1,319},{2,4},{3,5},{4,2},{5,3},{6,8},{7,9},{8,6},{9,7},{1... | collective-permute-start | bytes 196616 | tf_op jit(solution)/shard_map/ppermute | solution.py:56
  72.1 1.9 %collective-permute-start.8 = (bf16[4,2,32,128]{3,2,1,0:T(8,128)(2,1)S(1)}, bf16[4,2,32,128]{3,2,1,0:T(8,128)(2,1)S(1)}, u32[]{:S(2)}, u32[]{:S(2)}) collective-permute-start(bf16[4,2,32,128]{3,2,1,0:T(8,128)(2,1)S(1)} %get-tuple-element.24), channel_id=1, source_target_pairs={{0,2},{1,3},{2,0},{3,1},{4,6},{5,7},{6,4},{7,5},{8,10},{9,11},{10,... | collective-permute-start | bytes 196616 | tf_op jit(solution)/shard_map/ppermute | solution.py:56
  74.0 7.6 %collective-permute-done.7 = bf16[4,2,32,128]{3,2,1,0:T(8,128)(2,1)S(1)} collective-permute-done((bf16[4,2,32,128]{3,2,1,0:T(8,128)(2,1)S(1)}, bf16[4,2,32,128]{3,2,1,0:T(8,128)(2,1)S(1)}, u32[]{:S(2)}, u32[]{:S(2)}) %collective-permute-start.7) | collective-permute-done | bytes 65568 | tf_op jit(solution)/shard_map/ppermute | solution.py:56
  81.5 0.0 collective-permute-done.8
  81.6 8.6 %collective-permute-start.9 = (bf16[4,2,32,128]{3,2,1,0:T(8,128)(2,1)S(1)}, bf16[4,2,32,128]{3,2,1,0:T(8,128)(2,1)S(1)}, u32[]{:S(2)}, u32[]{:S(2)}) collective-permute-start(bf16[4,2,32,128]{3,2,1,0:T(8,128)(2,1)S(1)} %fusion.3), channel_id=1, source_target_pairs={{0,256},{64,320},{128,384},{192,448},{256,0},{320,64},{384,128},{4... | collective-permute-start | bytes 196616 | tf_op jit(solution)/shard_map/ppermute | solution.py:35
  90.2 2.2 %collective-permute-done.9 = bf16[4,2,32,128]{3,2,1,0:T(8,128)(2,1)S(1)} collective-permute-done((bf16[4,2,32,128]{3,2,1,0:T(8,128)(2,1)S(1)}, bf16[4,2,32,128]{3,2,1,0:T(8,128)(2,1)S(1)}, u32[]{:S(2)}, u32[]{:S(2)}) %collective-permute-start.9) | collective-permute-done | bytes 65568 | tf_op jit(solution)/shard_map/ppermute | solution.py:35
  92.5 7.5 %collective-permute-start.10 = (bf16[4,2,32,128]{3,2,1,0:T(8,128)(2,1)S(1)}, bf16[4,2,32,128]{3,2,1,0:T(8,128)(2,1)S(1)}, u32[]{:S(2)}, u32[]{:S(2)}) collective-permute-start(bf16[4,2,32,128]{3,2,1,0:T(8,128)(2,1)S(1)} %add_convert_fusion.mine), channel_id=1, source_target_pairs={{0,128},{64,192},{128,0},{192,64},{256,384},{320,448},{384,256},{4... | collective-permute-start | bytes 196616 | tf_op jit(solution)/shard_map/ppermute | solution.py:35
  100.0 2.3 %collective-permute-done.10.over_two = bf16[4,2,32,128]{3,2,1,0:T(8,128)(2,1)S(1)} collective-permute-done((bf16[4,2,32,128]{3,2,1,0:T(8,128)(2,1)S(1)}, bf16[4,2,32,128]{3,2,1,0:T(8,128)(2,1)S(1)}, u32[]{:S(2)}, u32[]{:S(2)}) %collective-permute-start.10) | collective-permute-done | bytes 65568 | tf_op jit(solution)/shard_map/ppermute | solution.py:35
  102.3 3.4 %collective-permute-start.11 = (bf16[2,4,2,32,128]{4,3,2,1,0:T(8,128)(2,1)S(1)}, bf16[2,4,2,32,128]{4,3,2,1,0:T(8,128)(2,1)S(1)}, u32[]{:S(2)}, u32[]{:S(2)}) collective-permute-start(bf16[2,4,2,32,128]{4,3,2,1,0:T(8,128)(2,1)S(1)} %pad_maximum_fusion.2), channel_id=1, source_target_pairs={{0,64},{64,0},{128,192},{192,128},{256,320},{320,256},{384,448},{4... | collective-permute-start | bytes 393224 | tf_op jit(solution)/shard_map/ppermute | solution.py:35
  105.7 3.4 %collective-permute-done.11.over_one = bf16[2,4,2,32,128]{4,3,2,1,0:T(8,128)(2,1)S(1)} collective-permute-done((bf16[2,4,2,32,128]{4,3,2,1,0:T(8,128)(2,1)S(1)}, bf16[2,4,2,32,128]{4,3,2,1,0:T(8,128)(2,1)S(1)}, u32[]{:S(2)}, u32[]{:S(2)}) %collective-permute-start.11) | collective-permute-done | bytes 131104 | tf_op jit(solution)/shard_map/ppermute | solution.py:35
  109.2 1.0 shard_map.91
  (14 shorter events, 0.3 us)
Async XLA Ops:
  0.0 20.6 %copy-start = (bf16[32,8,1024]{2,1,0:T(8,128)(2,1)S(1)}, bf16[32,8,1024]{2,1,0:T(8,128)(2,1)}, u32[]{:S(2)}) copy-start(bf16[32,8,1024]{2,1,0:T(8,128)(2,1)} %weights.1) | copy-start | bytes 1572868
  0.0 1.0 copy-start.3
  1.0 0.9 copy-start.4
  2.2 25.5 %collective-permute-start = (bf16[4,2,2,32,128]{4,3,2,1,0:T(8,128)(2,1)S(1)}, bf16[4,2,2,32,128]{4,3,2,1,0:T(8,128)(2,1)S(1)}, u32[]{:S(2)}, u32[]{:S(2)}) collective-permute-start(bf16[4,2,2,32,128]{4,3,2,1,0:T(8,128)(2,1)S(1)} %shard_map.82.own), channel_id=1, source_target_pairs={{0,318},{1,319},{2,4},{3,5},{4,2},{5,3},{6,8},{7,9},{8,6},{9,7},{1... | collective-permute-start | bytes 393224 | tf_op jit(solution)/shard_map/ppermute | solution.py:56
  18.7 9.0 %collective-permute-start.1 = (bf16[4,2,2,32,128]{4,3,2,1,0:T(8,128)(2,1)S(1)}, bf16[4,2,2,32,128]{4,3,2,1,0:T(8,128)(2,1)S(1)}, u32[]{:S(2)}, u32[]{:S(2)}) collective-permute-start(bf16[4,2,2,32,128]{4,3,2,1,0:T(8,128)(2,1)S(1)} %shard_map.82.own), channel_id=1, source_target_pairs={{0,2},{1,3},{2,0},{3,1},{4,6},{5,7},{6,4},{7,5},{8,10},{9,11},{10,... | collective-permute-start | bytes 393224 | tf_op jit(solution)/shard_map/ppermute | solution.py:56
  21.6 25.1 %collective-permute-start.4 = (bf16[48,8,1024]{2,1,0:T(8,128)(2,1)S(1)}, bf16[48,8,1024]{2,1,0:T(8,128)(2,1)S(1)}, u32[]{:S(2)}, u32[]{:S(2)}) collective-permute-start(bf16[48,8,1024]{2,1,0:T(8,128)(2,1)S(1)} %pad_maximum_fusion), channel_id=1, source_target_pairs={{0,64},{64,0},{128,192},{192,128},{256,320},{320,256},{384,448},{4... | collective-permute-start | bytes 2359304 | tf_op jit(solution)/shard_map/ppermute | solution.py:35
  25.2 0.7 copy-start.6
  25.9 0.7 copy-start.5
  27.7 3.4 %collective-permute-start.2 = (bf16[2,4,2,2,32,128]{5,4,3,2,1,0:T(8,128)(2,1)S(1)}, bf16[2,4,2,2,32,128]{5,4,3,2,1,0:T(8,128)(2,1)S(1)}, u32[]{:S(2)}, u32[]{:S(2)}) collective-permute-start(bf16[2,4,2,2,32,128]{5,4,3,2,1,0:T(8,128)(2,1)S(1)} %pad_maximum_fusion.1), channel_id=1, source_target_pairs={{0,1},{1,0},{2,3},{3,2},{4,5},{5,4},{6,7},{7,6},{8,9},{9,8},{10,11... | collective-permute-start | bytes 786440 | tf_op jit(solution)/shard_map/ppermute | solution.py:40
  33.1 8.4 %copy-start.2 = (bf16[16,8,1024]{2,1,0:T(8,128)(2,1)S(1)}, bf16[16,8,1024]{2,1,0:T(8,128)(2,1)}, u32[]{:S(2)}) copy-start(bf16[16,8,1024]{2,1,0:T(8,128)(2,1)} %sky.1) | copy-start | bytes 786436
  33.1 17.1 %collective-permute-start.3 = (bf16[8,2,2,16,128]{4,3,2,1,0:T(8,128)(2,1)S(1)}, bf16[8,2,2,16,128]{4,3,2,1,0:T(8,128)(2,1)S(1)}, u32[]{:S(2)}, u32[]{:S(2)}) collective-permute-start(bf16[8,2,2,16,128]{4,3,2,1,0:T(8,128)(2,1)S(1)} %get-tuple-element.14.delta), channel_id=1, source_target_pairs={{0,128},{64,192},{128,0},{192,64},{256,384},{320,448},{384,256},{4... | collective-permute-start | bytes 393224 | tf_op jit(solution)/shard_map/ppermute | solution.py:35
  48.5 1.8 %copy-start.1 = (bf16[4,256,256]{2,1,0:T(8,128)(2,1)S(1)}, bf16[4,256,256]{2,1,0:T(8,128)(2,1)}, u32[]{:S(2)}) copy-start(bf16[4,256,256]{2,1,0:T(8,128)(2,1)} %constant.127.clone.tables) | copy-start | bytes 1572868
  53.8 7.8 %collective-permute-start.5 = (bf16[8,2,2,16,128]{4,3,2,1,0:T(8,128)(2,1)S(1)}, bf16[8,2,2,16,128]{4,3,2,1,0:T(8,128)(2,1)S(1)}, u32[]{:S(2)}, u32[]{:S(2)}) collective-permute-start(bf16[8,2,2,16,128]{4,3,2,1,0:T(8,128)(2,1)S(1)} %shard_map.88), channel_id=1, source_target_pairs={{0,128},{64,192},{128,0},{192,64},{256,384},{320,448},{384,256},{4... | collective-permute-start | bytes 393224 | tf_op jit(solution)/shard_map/ppermute | solution.py:35
  63.8 3.2 %collective-permute-start.6 = (bf16[2,4,2,32,128]{4,3,2,1,0:T(8,128)(2,1)S(1)}, bf16[2,4,2,32,128]{4,3,2,1,0:T(8,128)(2,1)S(1)}, u32[]{:S(2)}, u32[]{:S(2)}) collective-permute-start(bf16[2,4,2,32,128]{4,3,2,1,0:T(8,128)(2,1)S(1)} %get-tuple-element.19), channel_id=1, source_target_pairs={{0,1},{1,0},{2,3},{3,2},{4,5},{5,4},{6,7},{7,6},{8,9},{9,8},{10,11... | collective-permute-start | bytes 393224 | tf_op jit(solution)/shard_map/ppermute | solution.py:40
  67.2 14.4 %collective-permute-start.7 = (bf16[4,2,32,128]{3,2,1,0:T(8,128)(2,1)S(1)}, bf16[4,2,32,128]{3,2,1,0:T(8,128)(2,1)S(1)}, u32[]{:S(2)}, u32[]{:S(2)}) collective-permute-start(bf16[4,2,32,128]{3,2,1,0:T(8,128)(2,1)S(1)} %get-tuple-element.23), channel_id=1, source_target_pairs={{0,318},{1,319},{2,4},{3,5},{4,2},{5,3},{6,8},{7,9},{8,6},{9,7},{1... | collective-permute-start | bytes 196616 | tf_op jit(solution)/shard_map/ppermute | solution.py:56
  72.1 9.5 %collective-permute-start.8 = (bf16[4,2,32,128]{3,2,1,0:T(8,128)(2,1)S(1)}, bf16[4,2,32,128]{3,2,1,0:T(8,128)(2,1)S(1)}, u32[]{:S(2)}, u32[]{:S(2)}) collective-permute-start(bf16[4,2,32,128]{3,2,1,0:T(8,128)(2,1)S(1)} %get-tuple-element.24), channel_id=1, source_target_pairs={{0,2},{1,3},{2,0},{3,1},{4,6},{5,7},{6,4},{7,5},{8,10},{9,11},{10,... | collective-permute-start | bytes 196616 | tf_op jit(solution)/shard_map/ppermute | solution.py:56
  81.6 10.8 %collective-permute-start.9 = (bf16[4,2,32,128]{3,2,1,0:T(8,128)(2,1)S(1)}, bf16[4,2,32,128]{3,2,1,0:T(8,128)(2,1)S(1)}, u32[]{:S(2)}, u32[]{:S(2)}) collective-permute-start(bf16[4,2,32,128]{3,2,1,0:T(8,128)(2,1)S(1)} %fusion.3), channel_id=1, source_target_pairs={{0,256},{64,320},{128,384},{192,448},{256,0},{320,64},{384,128},{4... | collective-permute-start | bytes 196616 | tf_op jit(solution)/shard_map/ppermute | solution.py:35
  92.5 9.8 %collective-permute-start.10 = (bf16[4,2,32,128]{3,2,1,0:T(8,128)(2,1)S(1)}, bf16[4,2,32,128]{3,2,1,0:T(8,128)(2,1)S(1)}, u32[]{:S(2)}, u32[]{:S(2)}) collective-permute-start(bf16[4,2,32,128]{3,2,1,0:T(8,128)(2,1)S(1)} %add_convert_fusion.mine), channel_id=1, source_target_pairs={{0,128},{64,192},{128,0},{192,64},{256,384},{320,448},{384,256},{4... | collective-permute-start | bytes 196616 | tf_op jit(solution)/shard_map/ppermute | solution.py:35
  102.3 6.9 %collective-permute-start.11 = (bf16[2,4,2,32,128]{4,3,2,1,0:T(8,128)(2,1)S(1)}, bf16[2,4,2,32,128]{4,3,2,1,0:T(8,128)(2,1)S(1)}, u32[]{:S(2)}, u32[]{:S(2)}) collective-permute-start(bf16[2,4,2,32,128]{4,3,2,1,0:T(8,128)(2,1)S(1)} %pad_maximum_fusion.2), channel_id=1, source_target_pairs={{0,64},{64,0},{128,192},{192,128},{256,320},{320,256},{384,448},{4... | collective-permute-start | bytes 393224 | tf_op jit(solution)/shard_map/ppermute | solution.py:35

commit v4 on v3

--- a/solution.py
+++ b/solution.py
@@ -87,57 +87,94 @@
     return lax.broadcasted_iota(jnp.int32, (rows, 2 * G), 1)
 
 
-def to_row_order(value, dest):
-    for high in range(8):
-        dest[pl.ds(high, CH_DEV, stride=8), :] = value[:, high * LANES : (high + 1) * LANES]
-
-
-def exchange(first, second, keep, by):
-    return (
-        jnp.where(keep, first, pltpu.roll(second, by, 1)),
-        jnp.where(keep, pltpu.roll(first, LANES - by, 1), second),
+def slots_kernel(pairs, pointing, counts, out):
+    base_count = lax.axis_size("base")
+    myself = lax.axis_index("base")
+    core, chip_odd = lax.rem(myself, 2), lax.rem(myself // 2, 2)
+    live = counts[0]
+    slot = lax.broadcasted_iota(jnp.int32, (2, SUB_DEV), 1)
+    station = pairs[...]
+    offset = (station >> 2) - myself
+    offset = jnp.where(offset > base_count // 2, offset - base_count, offset)
+    offset = jnp.where(offset < -(base_count // 2), offset + base_count, offset)
+    two_away = jnp.where((offset > 0) == (chip_odd == 0), 1, 2)
+    one_away = jnp.where((offset > 0) == (core == 1), 4, 3)
+    far = jnp.abs(offset) == 2
+    block = jnp.where(offset == 0, 0, jnp.where(far, two_away, one_away))
+    place = jnp.where(slot < live, block * ST_DEV + (station & (ST_DEV - 1)), 0)
+    out[0:2, :] = place
+    point = pointing[...]
+
+    def start(index):
+        value = jnp.zeros_like(index)
+        for step in range(1, 4):
+            value = jnp.where(index == step, step * (G - W) // 3, value)
+        return value
+
+    row = start(point >> 2)
+    out[2:3, :] = (row + 1) >> 1
+    out[3:4, :] = start(point & 3)
+    out[4:5, :] = row >> 1
+    out[5:6, :] = jnp.full((1, SUB_DEV), live, jnp.int32)
+    out[6:7, :] = point
+    out[7:8, :] = row & 1
+
+
+def group_table():
+    place = np.arange(GROUP * LANES).reshape(GROUP, GROUP, W).transpose(1, 0, 2).reshape(-1)
+    return jnp.asarray(np.eye(GROUP * LANES)[:, place].astype(ml_dtypes.bfloat16))
+
+
+def prepare_kernel(first, meta, weights, sky, table, weight_out, sky_out, stage, sky_stage):
+    def store(value, dest):
+        for high in range(8):
+            dest[high * CH_DEV : (high + 1) * CH_DEV, :] = value[
+                :, high * LANES : (high + 1) * LANES
+            ]
+
+    def side_by_side(stages):
+        return jnp.concatenate(
+            [
+                jnp.concatenate(
+                    [
+                        stages(quad * GROUP + member)[pl.ds(channel, 8, stride=CH_DEV), :]
+                        for member in range(GROUP)
+                    ],
+                    axis=1,
+                )
+                for quad in range(QUADS)
+                for channel in range(CH_DEV)
+            ],
+            axis=0,
+        ).astype(jnp.bfloat16)
+
+    def write(moved, out):
+        for quad in range(QUADS):
+            for channel in range(CH_DEV):
+                rows = (quad * CH_DEV + channel) * 8
+                out[quad, channel] = jnp.concatenate(
+                    [
+                        moved[rows : rows + 8, low * LANES : (low + 1) * LANES]
+                        for low in (0, 2, 1, 3)
+                    ],
+                    axis=0,
+                ).astype(jnp.bfloat16)
+
+    for slot in range(SUB_DEV):
+        store(weights[slot].astype(jnp.float32), stage.at[slot])
+    for point in range(sky_stage.shape[0]):
+        store(sky[first + point].astype(jnp.float32), sky_stage.at[point])
+    mover = table[...]
+    moved = jnp.dot(
+        side_by_side(lambda slot: stage.at[slot]), mover, preferred_element_type=jnp.float32
     )
-
-
-def side_by_side(members):
-    lane = lane_index(8)
-    low_half = lane < 2 * W
-    even_group = lax.rem(lane, 2 * W) < W
-    a, c = exchange(members[0], members[2], low_half, 2 * W)
-    b, d = exchange(members[1], members[3], low_half, 2 * W)
-    a, b = exchange(a, b, even_group, W)
-    c, d = exchange(c, d, even_group, W)
-    return jnp.concatenate([a, c, b, d], axis=0).astype(jnp.bfloat16)
-
-
-def weights_kernel(meta, weights, out, stage):
-    def visit(quad, carry):
-        for member in range(GROUP):
-            value = weights[quad * GROUP + member].astype(jnp.float32)
-            to_row_order(value, stage.at[member])
-        for channel in range(CH_DEV):
-            rows = pl.ds(channel * 8, 8)
-            out[quad, channel] = side_by_side([stage[member, rows, :] for member in range(GROUP)])
-        return carry
-
-    lax.fori_loop(0, (meta[5, 0] + GROUP - 1) // GROUP, visit, 0)
-
-
-def sky_kernel(first, meta, sky, out, stage):
-    def turn(point, carry):
-        to_row_order(sky[first + point].astype(jnp.float32), stage.at[point])
-        return carry
-
-    lax.fori_loop(0, stage.shape[0], turn, 0)
-
-    def visit(quad, carry):
-        points = [meta[6, quad * GROUP + member] for member in range(GROUP)]
-        for channel in range(CH_DEV):
-            rows = pl.ds(channel * 8, 8)
-            out[quad, channel] = side_by_side([stage[point, rows, :] for point in points])
-        return carry
-
-    lax.fori_loop(0, (meta[5, 0] + GROUP - 1) // GROUP, visit, 0)
+    write(moved, weight_out)
+    moved = jnp.dot(
+        side_by_side(lambda slot: sky_stage.at[meta[6, slot]]),
+        mover,
+        preferred_element_type=jnp.float32,
+    )
+    write(moved, sky_out)
 
 
 def own_kernel(screens, direction, out, stage):
@@ -164,7 +201,9 @@
     return lane_index(rows) // W
 
 
-def delta_kernel(meta, own, chip_a, chip_b, sibling, out, beams, turned, probes, turn):
+def delta_kernel(
+    meta, own, chip_a, chip_b, sibling, out, beams, turned, probes, turn
+):
     quads = (meta[5, 0] + GROUP - 1) // GROUP
     for block, value in enumerate((own, chip_a, chip_b, sibling.at[0], sibling.at[1])):
         for member in range(ST_DEV):
@@ -176,8 +215,9 @@
                 turned[station, half] = swap_halves(beam)
     group = group_index(HALF_ROWS)
 
-    def visit(quad, carry):
-        for half in range(HALVES):
+    def visit(step, carry):
+        for half, later in [(half, later) for half in range(HALVES) for later in range(2)]:
+            quad = 2 * step + later
             same = [jnp.zeros((HALF_ROWS, LANES), jnp.float32)] * 2
             cross = [jnp.zeros((HALF_ROWS, LANES), jnp.float32)] * 2
             for member in range(GROUP):
@@ -203,13 +243,13 @@
             real = same[0] + swap_halves(same[1])
             imag = swap_halves(cross[1]) - cross[0]
             for part, value in enumerate((real, imag)):
-                turn[half, part] = value
+                turn[later, half, part] = value
                 out[quad, part, half] = jnp.concatenate(
-                    [turn[half, part, pl.ds(low, 8, stride=2), :] for low in range(2)], axis=0
+                    [turn[later, half, part, pl.ds(low, 8, stride=2), :] for low in range(2)], axis=0
                 ).astype(jnp.bfloat16)
         return carry
 
-    lax.fori_loop(0, quads, visit, 0)
+    lax.fori_loop(0, (quads + 1) // 2, visit, 0)
 
 
 def hessian_kernel(meta, delta, weights_0, weights_1, sky_0, sky_1, tables, out):
@@ -323,12 +363,17 @@
     out_own,
     out_chips,
     out_sibling,
-    totals,
+    totals_p0,
+    totals_p1,
+    totals_q0,
+    totals_q1,
     turn,
 ):
     live = meta[5, 0]
     quads = (live + GROUP - 1) // GROUP
-    totals[...] = jnp.zeros_like(totals)
+    totals_p, totals_q = (totals_p0, totals_p1), (totals_q0, totals_q1)
+    for totals in totals_p + totals_q:
+        totals[...] = jnp.zeros_like(totals)
     group = group_index(HALF_ROWS)
     scale = 1.0 / channels_total
 
@@ -355,21 +400,27 @@
                 grad_imag = jnp.where(low, -imag, jnp.where(high, imag_high, 0.0))
                 grad_real = pltpu.roll(grad_real, shift, 1)
                 grad_imag = pltpu.roll(grad_imag, shift, 1)
-                totals[station_p, half, rows, :] += (
+                totals_p[half][station_p, rows, :] += (
                     beams[station_q, half, rows, :] * grad_real
                     + turned[station_q, half, rows, :] * grad_imag
                 )
-                totals[station_q, half, rows, :] += (
+                totals_q[half][station_q, rows, :] += (
                     beams[station_p, half, rows, :] * grad_real
                     - turned[station_p, half, rows, :] * grad_imag
                 )
         return carry
 
     lax.fori_loop(0, quads, visit, 0)
-    out_own[...] = totals[:ST_DEV]
-    for block in range(2):
-        out_chips[block] = totals[pl.ds((1 + block) * ST_DEV, ST_DEV)]
-        out_sibling[block] = totals[pl.ds((3 + block) * ST_DEV, ST_DEV)].astype(jnp.bfloat16)
+
+    def total(block, half):
+        stations = pl.ds(block * ST_DEV, ST_DEV)
+        return totals_p[half][stations] + totals_q[half][stations]
+
+    for half in range(HALVES):
+        out_own[:, half] = total(0, half)
+        for block in range(2):
+            out_chips[block, :, half] = total(1 + block, half)
+            out_sibling[block, :, half] = total(3 + block, half).astype(jnp.bfloat16)
 
 
 def result_kernel(mine, over_two, over_one, out, stage):
@@ -392,14 +443,14 @@
             ]
 
 
-def call(kernel, out_shape, in_specs, scratch_shapes):
+def call(kernel, out_shape, in_specs, scratch_shapes, mebibytes=20):
     return pl.pallas_call(
         kernel,
         out_shape=out_shape,
         in_specs=in_specs,
         out_specs=jax.tree.map(lambda _: pl.BlockSpec(memory_space=VMEM), out_shape),
         scratch_shapes=scratch_shapes,
-        compiler_params=pltpu.CompilerParams(vmem_limit_bytes=48 * 1024 * 1024),
+        compiler_params=pltpu.CompilerParams(vmem_limit_bytes=mebibytes * 1024 * 1024),
     )
 
 
@@ -411,46 +462,24 @@
     in_smem = pl.BlockSpec(memory_space=SMEM)
     in_vmem = pl.BlockSpec(memory_space=VMEM)
 
-    alive = jnp.arange(SUB_DEV, dtype=jnp.int32) < counts[0]
-    offset = (pairs // ST_DEV - myself + REACH) % base_count - REACH
-    block = jnp.where(
-        offset == 0,
-        0,
-        jnp.where(
-            jnp.abs(offset) == 2,
-            1 + ((offset == 2) == (chip_odd == 0)),
-            3 + ((offset == 1) == (core == 1)),
-        ),
-    )
-    local = jnp.where(alive[:, None], block * ST_DEV + pairs % ST_DEV, 0)
-    row_start = pointing // 4 * (G - W) // 3
-
-    def spread(value):
-        return jnp.broadcast_to(value, (SUB_DEV,))
-
-    meta = jnp.stack(
-        [
-            local[:, 0],
-            local[:, 1],
-            (row_start + 1) // 2,
-            pointing % 4 * (G - W) // 3,
-            row_start // 2,
-            spread(counts[0]),
-            pointing,
-            row_start % 2,
-        ]
-    ).astype(jnp.int32)
-
     own = call(
         own_kernel,
         jax.ShapeDtypeStruct((ST_DEV, 2, HALVES, G // 2, 2 * G), jnp.bfloat16),
         [in_vmem] * 2,
         [pltpu.VMEM((2 * ST_DEV, G * POLS, 2 * G), jnp.float32)],
     )(screens, direction)
-    chip_a = across_chips(own, 1)
-    chip_b = across_chips(own, 0)
-    other = across_chan(jnp.concatenate([weights, sky]), 1)
-    shared_is_a = core != chip_odd
+    chip_a = across_chips(own, 0)
+    meta = call(
+        slots_kernel,
+        jax.ShapeDtypeStruct((8, SUB_DEV), jnp.int32),
+        [in_vmem] * 2 + [in_smem],
+        [],
+    )(pairs.T, pointing[None], counts)
+    chip_b = across_chips(own, 1)
+    weights_sent, sky_sent, meta = lax.optimization_barrier((weights, sky, meta))
+    other = across_chan(jnp.concatenate([weights_sent, sky_sent]), 1)
+    meta, chip_a, chip_b = lax.optimization_barrier((meta, chip_a, chip_b))
+    shared_is_a = core == chip_odd
     sibling = to_sibling(jnp.stack([own, jnp.where(shared_is_a, chip_a, chip_b)]))
 
     delta_shape = (QUADS, 2, HALVES, HALF_ROWS, LANES)
@@ -462,24 +491,30 @@
         [jax.ShapeDtypeStruct(delta_shape, jnp.bfloat16)]
         + [jax.ShapeDtypeStruct(field_shape, jnp.float32)] * 2,
         [in_smem] + [in_vmem] * 4,
-        [field, turn],
+        [field, pltpu.VMEM((2, HALVES, 2, HALF_ROWS, LANES), jnp.float32)],
     )(meta, own, chip_a, chip_b, sibling)
     over_two = across_chan(delta, 2)
     wide = jnp.float32
     tables = pass_tables()
     quad_shape = jax.ShapeDtypeStruct((QUADS, CH_DEV, W, LANES), jnp.bfloat16)
 
-    def turned_sky(value, first):
-        stage = pltpu.VMEM((sky.shape[0], CH_DEV * 8, LANES), wide)
-        kernel = functools.partial(sky_kernel, first)
-        return call(kernel, quad_shape, [in_smem, in_vmem], [stage])(meta, value)
-
-    def turned_weights(value):
-        stage = pltpu.VMEM((GROUP, CH_DEV * 8, LANES), wide)
-        return call(weights_kernel, quad_shape, [in_smem, in_vmem], [stage])(meta, value)
-
-    weighting = (turned_weights(weights), turned_weights(other))
-    brightness = (turned_sky(sky, 0), turned_sky(other, SUB_DEV))
+    mover = group_table()
+
+    def prepared(weights, sky, first):
+        return call(
+            functools.partial(prepare_kernel, first),
+            [quad_shape] * 2,
+            [in_smem] + [in_vmem] * 3,
+            [
+                pltpu.VMEM((SUB_DEV, 8 * CH_DEV, LANES), wide),
+                pltpu.VMEM((point_count, 8 * CH_DEV, LANES), wide),
+            ],
+        )(meta, weights, sky, mover)
+
+    point_count = sky.shape[0]
+    own_images = prepared(weights, sky, 0)
+    other_images = prepared(other, other, SUB_DEV)
+    weighting, brightness = zip(own_images, other_images)
 
     def hessian(delta):
         return call(
@@ -487,6 +522,7 @@
             jax.ShapeDtypeStruct(delta_shape, jnp.bfloat16),
             [in_smem] + [in_vmem] * 6,
             [],
+            40,
         )(meta, delta, *weighting, *brightness, tables)
 
     sent, delta = lax.optimization_barrier((hessian(over_two), delta))
@@ -505,14 +541,14 @@
             jax.ShapeDtypeStruct((2,) + block_shape, jnp.bfloat16),
         ],
         [in_smem] + [in_vmem] * 4,
-        [field, turn],
+        [pltpu.VMEM((NEAR * ST_DEV, G // 2, 2 * G), wide)] * 4 + [turn],
     )(meta, kept, back_two, beams, turned)
     from_sibling = to_sibling(sum_sibling).astype(wide)
     sum_a = sum_chips[0] + jnp.where(shared_is_a, from_sibling[1], 0.0)
     sum_b = sum_chips[1] + jnp.where(shared_is_a, 0.0, from_sibling[1])
-    from_a = across_chips(sum_a.astype(jnp.bfloat16), 1)
-    from_b = across_chips(sum_b.astype(jnp.bfloat16), 0)
-    mine = sum_own + from_sibling[0] + from_a.astype(wide) + from_b.astype(wide)
+    from_b = across_chips(sum_b.astype(jnp.bfloat16), 1)
+    from_a = across_chips(sum_a.astype(jnp.bfloat16), 0)
+    mine = sum_own + from_sibling[0] + from_b.astype(wide) + from_a.astype(wide)
     mine = mine.astype(jnp.bfloat16)
     other = across_chan(mine, 4)
     mine = (mine.astype(wide) + other.astype(wide)).astype(jnp.bfloat16)

time: 111 us -> 109 us (0.982)
  the two profiles are of different devices: /device:TPU:32 before, /device:TPU:8 now
where the time goes in v4:
time: 109 us
  starting transfers between devices  51.8 us (48%)
  waiting for transfers between devices  37.8 us (35%)
  Pallas kernels  14.3 us (13%)
  local copies, waits for them, and re-layouts  2.65 us (2%)
  other arithmetic  1.2 us (1%)
    ppermute x4, starting transfers between devices, across_chips(): return lax.ppermute(value, ('chan', 'base'), perm)  33.3 us
    ppermute x6, waiting for transfers between devices, across_chan(): return lax.ppermute(value, 'chan', [(i, i ^ bit) for i in range(count)])  32.6 us
    ppermute x6, starting transfers between devices, across_chan(): return lax.ppermute(value, 'chan', [(i, i ^ bit) for i in range(count)])  14.5 us
    pallas_call x2, Pallas kernels, hessian(): call(hessian_kernel, jax.ShapeDtypeStruct(delta_shape, jnp.bfloat16), [in...  7.12 us
    ppermute x2, starting transfers between devices, to_sibling(): return lax.ppermute(value, 'base', [(i, i ^ 1) for i in range(count)])  3.97 us
    ppermute x2, waiting for transfers between devices, to_sibling(): return lax.ppermute(value, 'base', [(i, i ^ 1) for i in range(count)])  2.81 us
    pallas_call x2, Pallas kernels, prepared(): call(functools.partial(prepare_kernel, first), [quad_shape] * 2, [in_smem...  2.68 us
    unnamed x16, local copies, waits for them, and re-layouts  2.65 us
  transfers between devices with their start and end apart: 12, of which 8 were waited for; matrix products, arithmetic and copies ran while one was open for 1% of the time, Pallas kernels for 7%

profile of v4, /device:TPU:8, one launch (start us, length us, event | category | flops | bytes accessed | tf_op | source)
XLA Modules:
  0.0 108.6 jit_solution(11919188767614041608)
XLA Ops:
  0.0 0.0 copy-start
  0.0 0.0 copy-start.4
  0.0 1.0 copy-done.4
  1.0 0.0 copy-start.5
  1.0 0.9 copy-done.5
  2.0 0.2 shard_map.92.own
  2.2 3.5 %collective-permute-start.1 = (bf16[4,2,2,32,128]{4,3,2,1,0:T(8,128)(2,1)S(1)}, bf16[4,2,2,32,128]{4,3,2,1,0:T(8,128)(2,1)S(1)}, u32[]{:S(2)}, u32[]{:S(2)}) collective-permute-start(bf16[4,2,2,32,128]{4,3,2,1,0:T(8,128)(2,1)S(1)} %shard_map.92.own), channel_id=1, source_target_pairs={{0,318},{1,319},{2,4},{3,5},{4,2},{5,3},{6,8},{7,9},{8,6},{9,7},{1... | collective-permute-start | bytes 393224 | tf_op jit(solution)/shard_map/ppermute | solution.py:56
  5.7 16.3 %collective-permute-start = (bf16[4,2,2,32,128]{4,3,2,1,0:T(8,128)(2,1)S(1)}, bf16[4,2,2,32,128]{4,3,2,1,0:T(8,128)(2,1)S(1)}, u32[]{:S(2)}, u32[]{:S(2)}) collective-permute-start(bf16[4,2,2,32,128]{4,3,2,1,0:T(8,128)(2,1)S(1)} %shard_map.92.own), channel_id=1, source_target_pairs={{0,2},{1,3},{2,0},{3,1},{4,6},{5,7},{6,4},{7,5},{8,10},{9,11},{10,... | collective-permute-start | bytes 393224 | tf_op jit(solution)/shard_map/ppermute | solution.py:56
  22.6 0.0 copy-start.6
  22.6 0.0 copy-start.7
  22.6 0.7 copy-done.6
  23.2 0.0 copy-done.7
  23.3 0.0 copy-done
  23.3 1.0 pad_maximum_fusion
  24.3 2.9 %collective-permute-start.4 = (bf16[48,8,1024]{2,1,0:T(8,128)(2,1)S(1)}, bf16[48,8,1024]{2,1,0:T(8,128)(2,1)S(1)}, u32[]{:S(2)}, u32[]{:S(2)}) collective-permute-start(bf16[48,8,1024]{2,1,0:T(8,128)(2,1)S(1)} %pad_maximum_fusion), channel_id=1, source_target_pairs={{0,64},{64,0},{128,192},{192,128},{256,320},{320,256},{384,448},{4... | collective-permute-start | bytes 2359304 | tf_op jit(solution)/shard_map/ppermute | solution.py:35
  27.3 0.0 collective-permute-done.1.chip_b
  27.3 0.0 collective-permute-done.chip_a
  27.3 0.0 copy-start.1
  27.4 0.0 copy-start.3
  27.4 2.1 %collective-permute-start.2 = (bf16[2,4,2,2,32,128]{5,4,3,2,1,0:T(8,128)(2,1)S(1)}, bf16[2,4,2,2,32,128]{5,4,3,2,1,0:T(8,128)(2,1)S(1)}, u32[]{:S(2)}, u32[]{:S(2)}) collective-permute-start(bf16[2,4,2,2,32,128]{5,4,3,2,1,0:T(8,128)(2,1)S(1)} %pad_maximum_fusion.1), channel_id=1, source_target_pairs={{0,1},{1,0},{2,3},{3,2},{4,5},{5,4},{6,7},{7,6},{8,9},{9,8},{10,11... | collective-permute-start | bytes 786440 | tf_op jit(solution)/shard_map/ppermute | solution.py:40
  29.4 1.5 %collective-permute-done.2.sibling = bf16[2,4,2,2,32,128]{5,4,3,2,1,0:T(8,128)(2,1)S(1)} collective-permute-done((bf16[2,4,2,2,32,128]{5,4,3,2,1,0:T(8,128)(2,1)S(1)}, bf16[2,4,2,2,32,128]{5,4,3,2,1,0:T(8,128)(2,1)S(1)}, u32[]{:S(2)}, u32[]{:S(2)}) %collective-permute-start.2) | collective-permute-done | bytes 262176 | tf_op jit(solution)/shard_map/ppermute | solution.py:40
  31.0 1.6 %shard_map.93 = (bf16[8,2,2,16,128]{4,3,2,1,0:T(8,128)(2,1)S(1)}, f32[20,2,32,128]{3,2,1,0:T(8,128)S(1)}, f32[20,2,32,128]{3,2,1,0:T(8,128)S(1)}) custom-call(s32[8,32]{1,0:T(8,128)S(1)} %shard_map.91.meta.args_0_, bf16[4,2,2,32,128]{4,3,2,1,0:T(8,128)(2,1)S(1)} %shard_map.92.own, bf16[4,2,2,32,128]{4,3,2,1,0:T(8,128)(2,1)S(1)} %collective-permute-done.chip_a, ...), custom_call_target="tpu_custom_call" | custom-call | tf_op jit(solution)/shard_map/pallas_call | solution.py:489
  32.5 3.4 %collective-permute-start.3 = (bf16[8,2,2,16,128]{4,3,2,1,0:T(8,128)(2,1)S(1)}, bf16[8,2,2,16,128]{4,3,2,1,0:T(8,128)(2,1)S(1)}, u32[]{:S(2)}, u32[]{:S(2)}) collective-permute-start(bf16[8,2,2,16,128]{4,3,2,1,0:T(8,128)(2,1)S(1)} %get-tuple-element.34.delta), channel_id=1, source_target_pairs={{0,128},{64,192},{128,0},{192,64},{256,384},{320,448},{384,256},{4... | collective-permute-start | bytes 393224 | tf_op jit(solution)/shard_map/ppermute | solution.py:35
  35.9 0.0 copy-done.1
  35.9 0.0 copy-done.3
  35.9 1.3 %shard_map.94 = (bf16[8,8,32,128]{3,2,1,0:T(8,128)(2,1)S(1)}, bf16[8,8,32,128]{3,2,1,0:T(8,128)(2,1)S(1)}) custom-call(s32[8,32]{1,0:T(8,128)S(1)} %shard_map.91.meta.args_0_, bf16[32,8,1024]{2,1,0:T(8,128)(2,1)S(1)} %copy-done, bf16[16,8,1024]{2,1,0:T(8,128)(2,1)S(1)} %copy-done.3, bf16[512,512]{1,0:T(8,128)(2,1)S(1)} %copy-done.1), custom_call_target="tpu_custom_call" | custom-call | tf_op jit(solution)/shard_map/pallas_call | solution.py:504
  37.3 0.0 copy-start.2
  37.3 10.4 %collective-permute-done.4.weights.sky = bf16[48,8,1024]{2,1,0:T(8,128)(2,1)S(1)} collective-permute-done((bf16[48,8,1024]{2,1,0:T(8,128)(2,1)S(1)}, bf16[48,8,1024]{2,1,0:T(8,128)(2,1)S(1)}, u32[]{:S(2)}, u32[]{:S(2)}) %collective-permute-start.4) | collective-permute-done | bytes 786464 | tf_op jit(solution)/shard_map/ppermute | solution.py:35
  47.7 1.3 %shard_map.95 = (bf16[8,8,32,128]{3,2,1,0:T(8,128)(2,1)S(1)}, bf16[8,8,32,128]{3,2,1,0:T(8,128)(2,1)S(1)}) custom-call(s32[8,32]{1,0:T(8,128)S(1)} %shard_map.91.meta.args_0_, bf16[48,8,1024]{2,1,0:T(8,128)(2,1)S(1)} %collective-permute-done.4.weights.sky, bf16[48,8,1024]{2,1,0:T(8,128)(2,1)S(1)} %collective-permute-done.4.weights.sky, ...), custom_call_target="tpu_custom_call" | custom-call | tf_op jit(solution)/shard_map/pallas_call | solution.py:504
  49.1 0.0 collective-permute-done.3.delta
  49.1 0.0 copy-done.2
  49.1 3.6 %shard_map.96 = bf16[8,2,2,16,128]{4,3,2,1,0:T(8,128)(2,1)S(1)} custom-call(s32[8,32]{1,0:T(8,128)S(1)} %shard_map.91.meta.args_0_, bf16[8,2,2,16,128]{4,3,2,1,0:T(8,128)(2,1)S(1)} %collective-permute-done.3.delta, bf16[8,8,32,128]{3,2,1,0:T(8,128)(2,1)S(1)} %get-tuple-element.28.weights_0, bf16[8,8,32,128]{3,2,1,0:T(8,128)(2,1)S(1)} %get-tuple-element.31.weights_1, ...), custom_call_target="tpu_custom_call" | custom-call | tf_op jit(solution)/shard_map/pallas_call | solution.py:520
  52.7 2.5 %collective-permute-start.5 = (bf16[8,2,2,16,128]{4,3,2,1,0:T(8,128)(2,1)S(1)}, bf16[8,2,2,16,128]{4,3,2,1,0:T(8,128)(2,1)S(1)}, u32[]{:S(2)}, u32[]{:S(2)}) collective-permute-start(bf16[8,2,2,16,128]{4,3,2,1,0:T(8,128)(2,1)S(1)} %shard_map.96), channel_id=1, source_target_pairs={{0,128},{64,192},{128,0},{192,64},{256,384},{320,448},{384,256},{4... | collective-permute-start | bytes 393224 | tf_op jit(solution)/shard_map/ppermute | solution.py:35
  55.1 3.6 %shard_map.97.args_1_ = bf16[8,2,2,16,128]{4,3,2,1,0:T(8,128)(2,1)S(1)} custom-call(s32[8,32]{1,0:T(8,128)S(1)} %shard_map.91.meta.args_0_, bf16[8,2,2,16,128]{4,3,2,1,0:T(8,128)(2,1)S(1)} %get-tuple-element.34.delta, bf16[8,8,32,128]{3,2,1,0:T(8,128)(2,1)S(1)} %get-tuple-element.28.weights_0, bf16[8,8,32,128]{3,2,1,0:T(8,128)(2,1)S(1)} %get-tuple-element.31.weights_1, ...), custom_call_target="tpu_custom_call" | custom-call | tf_op jit(solution)/shard_map/pallas_call | solution.py:520
  58.7 2.7 %collective-permute-done.5.args_2_ = bf16[8,2,2,16,128]{4,3,2,1,0:T(8,128)(2,1)S(1)} collective-permute-done((bf16[8,2,2,16,128]{4,3,2,1,0:T(8,128)(2,1)S(1)}, bf16[8,2,2,16,128]{4,3,2,1,0:T(8,128)(2,1)S(1)}, u32[]{:S(2)}, u32[]{:S(2)}) %collective-permute-start.5) | collective-permute-done | bytes 131104 | tf_op jit(solution)/shard_map/ppermute | solution.py:35
  61.4 1.7 %shard_map.98 = (f32[4,2,32,128]{3,2,1,0:T(8,128)S(1)}, f32[2,4,2,32,128]{4,3,2,1,0:T(8,128)S(1)}, bf16[2,4,2,32,128]{4,3,2,1,0:T(8,128)(2,1)S(1)}) custom-call(s32[8,32]{1,0:T(8,128)S(1)} %shard_map.91.meta.args_0_, bf16[8,2,2,16,128]{4,3,2,1,0:T(8,128)(2,1)S(1)} %shard_map.97.args_1_, bf16[8,2,2,16,128]{4,3,2,1,0:T(8,128)(2,1)S(1)} %collective-permute-done.5.args_2_, ...), custom_call_target="tpu_custom_call" | custom-call | tf_op jit(solution)/shard_map/pallas_call | solution.py:536
  63.1 1.9 %collective-permute-start.6 = (bf16[2,4,2,32,128]{4,3,2,1,0:T(8,128)(2,1)S(1)}, bf16[2,4,2,32,128]{4,3,2,1,0:T(8,128)(2,1)S(1)}, u32[]{:S(2)}, u32[]{:S(2)}) collective-permute-start(bf16[2,4,2,32,128]{4,3,2,1,0:T(8,128)(2,1)S(1)} %get-tuple-element.39), channel_id=1, source_target_pairs={{0,1},{1,0},{2,3},{3,2},{4,5},{5,4},{6,7},{7,6},{8,9},{9,8},{10,11... | collective-permute-start | bytes 393224 | tf_op jit(solution)/shard_map/ppermute | solution.py:40
  65.0 1.3 %collective-permute-done.6 = bf16[2,4,2,32,128]{4,3,2,1,0:T(8,128)(2,1)S(1)} collective-permute-done((bf16[2,4,2,32,128]{4,3,2,1,0:T(8,128)(2,1)S(1)}, bf16[2,4,2,32,128]{4,3,2,1,0:T(8,128)(2,1)S(1)}, u32[]{:S(2)}, u32[]{:S(2)}) %collective-permute-start.6) | collective-permute-done | bytes 131104 | tf_op jit(solution)/shard_map/ppermute | solution.py:40
  66.4 1.9 %collective-permute-start.7 = (bf16[4,2,32,128]{3,2,1,0:T(8,128)(2,1)S(1)}, bf16[4,2,32,128]{3,2,1,0:T(8,128)(2,1)S(1)}, u32[]{:S(2)}, u32[]{:S(2)}) collective-permute-start(bf16[4,2,32,128]{3,2,1,0:T(8,128)(2,1)S(1)} %get-tuple-element.41), channel_id=1, source_target_pairs={{0,318},{1,319},{2,4},{3,5},{4,2},{5,3},{6,8},{7,9},{8,6},{9,7},{1... | collective-permute-start | bytes 196616 | tf_op jit(solution)/shard_map/ppermute | solution.py:56
  68.3 11.6 %collective-permute-start.8 = (bf16[4,2,32,128]{3,2,1,0:T(8,128)(2,1)S(1)}, bf16[4,2,32,128]{3,2,1,0:T(8,128)(2,1)S(1)}, u32[]{:S(2)}, u32[]{:S(2)}) collective-permute-start(bf16[4,2,32,128]{3,2,1,0:T(8,128)(2,1)S(1)} %get-tuple-element.42), channel_id=1, source_target_pairs={{0,2},{1,3},{2,0},{3,1},{4,6},{5,7},{6,4},{7,5},{8,10},{9,11},{10,... | collective-permute-start | bytes 196616 | tf_op jit(solution)/shard_map/ppermute | solution.py:56
  79.9 0.0 collective-permute-done.7
  79.9 2.3 %collective-permute-done.8 = bf16[4,2,32,128]{3,2,1,0:T(8,128)(2,1)S(1)} collective-permute-done((bf16[4,2,32,128]{3,2,1,0:T(8,128)(2,1)S(1)}, bf16[4,2,32,128]{3,2,1,0:T(8,128)(2,1)S(1)}, u32[]{:S(2)}, u32[]{:S(2)}) %collective-permute-start.8) | collective-permute-done | bytes 65568 | tf_op jit(solution)/shard_map/ppermute | solution.py:56
  82.3 1.9 %collective-permute-start.9 = (bf16[4,2,32,128]{3,2,1,0:T(8,128)(2,1)S(1)}, bf16[4,2,32,128]{3,2,1,0:T(8,128)(2,1)S(1)}, u32[]{:S(2)}, u32[]{:S(2)}) collective-permute-start(bf16[4,2,32,128]{3,2,1,0:T(8,128)(2,1)S(1)} %fusion.3), channel_id=1, source_target_pairs={{0,256},{64,320},{128,384},{192,448},{256,0},{320,64},{384,128},{4... | collective-permute-start | bytes 196616 | tf_op jit(solution)/shard_map/ppermute | solution.py:35
  84.2 9.4 %collective-permute-done.9 = bf16[4,2,32,128]{3,2,1,0:T(8,128)(2,1)S(1)} collective-permute-done((bf16[4,2,32,128]{3,2,1,0:T(8,128)(2,1)S(1)}, bf16[4,2,32,128]{3,2,1,0:T(8,128)(2,1)S(1)}, u32[]{:S(2)}, u32[]{:S(2)}) %collective-permute-start.9) | collective-permute-done | bytes 65568 | tf_op jit(solution)/shard_map/ppermute | solution.py:35
  93.6 1.9 %collective-permute-start.10 = (bf16[4,2,32,128]{3,2,1,0:T(8,128)(2,1)S(1)}, bf16[4,2,32,128]{3,2,1,0:T(8,128)(2,1)S(1)}, u32[]{:S(2)}, u32[]{:S(2)}) collective-permute-start(bf16[4,2,32,128]{3,2,1,0:T(8,128)(2,1)S(1)} %add_convert_fusion.mine), channel_id=1, source_target_pairs={{0,128},{64,192},{128,0},{192,64},{256,384},{320,448},{384,256},{4... | collective-permute-start | bytes 196616 | tf_op jit(solution)/shard_map/ppermute | solution.py:35
  95.5 5.2 %collective-permute-done.10.over_two = bf16[4,2,32,128]{3,2,1,0:T(8,128)(2,1)S(1)} collective-permute-done((bf16[4,2,32,128]{3,2,1,0:T(8,128)(2,1)S(1)}, bf16[4,2,32,128]{3,2,1,0:T(8,128)(2,1)S(1)}, u32[]{:S(2)}, u32[]{:S(2)}) %collective-permute-start.10) | collective-permute-done | bytes 65568 | tf_op jit(solution)/shard_map/ppermute | solution.py:35
  100.8 1.9 %collective-permute-start.11 = (bf16[2,4,2,32,128]{4,3,2,1,0:T(8,128)(2,1)S(1)}, bf16[2,4,2,32,128]{4,3,2,1,0:T(8,128)(2,1)S(1)}, u32[]{:S(2)}, u32[]{:S(2)}) collective-permute-start(bf16[2,4,2,32,128]{4,3,2,1,0:T(8,128)(2,1)S(1)} %pad_maximum_fusion.2), channel_id=1, source_target_pairs={{0,64},{64,0},{128,192},{192,128},{256,320},{320,256},{384,448},{4... | collective-permute-start | bytes 393224 | tf_op jit(solution)/shard_map/ppermute | solution.py:35
  102.7 4.9 %collective-permute-done.11.over_one = bf16[2,4,2,32,128]{4,3,2,1,0:T(8,128)(2,1)S(1)} collective-permute-done((bf16[2,4,2,32,128]{4,3,2,1,0:T(8,128)(2,1)S(1)}, bf16[2,4,2,32,128]{4,3,2,1,0:T(8,128)(2,1)S(1)}, u32[]{:S(2)}, u32[]{:S(2)}) %collective-permute-start.11) | collective-permute-done | bytes 131104 | tf_op jit(solution)/shard_map/ppermute | solution.py:35
  107.6 1.0 shard_map.99
  (8 shorter events, 0.2 us)
Async XLA Ops:
  0.0 23.3 %copy-start = (bf16[32,8,1024]{2,1,0:T(8,128)(2,1)S(1)}, bf16[32,8,1024]{2,1,0:T(8,128)(2,1)}, u32[]{:S(2)}) copy-start(bf16[32,8,1024]{2,1,0:T(8,128)(2,1)} %weights.1) | copy-start | bytes 1572868
  0.0 1.0 copy-start.4
  1.0 0.9 copy-start.5
  2.2 25.1 %collective-permute-start.1 = (bf16[4,2,2,32,128]{4,3,2,1,0:T(8,128)(2,1)S(1)}, bf16[4,2,2,32,128]{4,3,2,1,0:T(8,128)(2,1)S(1)}, u32[]{:S(2)}, u32[]{:S(2)}) collective-permute-start(bf16[4,2,2,32,128]{4,3,2,1,0:T(8,128)(2,1)S(1)} %shard_map.92.own), channel_id=1, source_target_pairs={{0,318},{1,319},{2,4},{3,5},{4,2},{5,3},{6,8},{7,9},{8,6},{9,7},{1... | collective-permute-start | bytes 393224 | tf_op jit(solution)/shard_map/ppermute | solution.py:56
  5.7 21.6 %collective-permute-start = (bf16[4,2,2,32,128]{4,3,2,1,0:T(8,128)(2,1)S(1)}, bf16[4,2,2,32,128]{4,3,2,1,0:T(8,128)(2,1)S(1)}, u32[]{:S(2)}, u32[]{:S(2)}) collective-permute-start(bf16[4,2,2,32,128]{4,3,2,1,0:T(8,128)(2,1)S(1)} %shard_map.92.own), channel_id=1, source_target_pairs={{0,2},{1,3},{2,0},{3,1},{4,6},{5,7},{6,4},{7,5},{8,10},{9,11},{10,... | collective-permute-start | bytes 393224 | tf_op jit(solution)/shard_map/ppermute | solution.py:56
  22.6 0.7 copy-start.6
  22.6 0.7 copy-start.7
  24.3 23.4 %collective-permute-start.4 = (bf16[48,8,1024]{2,1,0:T(8,128)(2,1)S(1)}, bf16[48,8,1024]{2,1,0:T(8,128)(2,1)S(1)}, u32[]{:S(2)}, u32[]{:S(2)}) collective-permute-start(bf16[48,8,1024]{2,1,0:T(8,128)(2,1)S(1)} %pad_maximum_fusion), channel_id=1, source_target_pairs={{0,64},{64,0},{128,192},{192,128},{256,320},{320,256},{384,448},{4... | collective-permute-start | bytes 2359304 | tf_op jit(solution)/shard_map/ppermute | solution.py:35
  27.3 8.6 %copy-start.1 = (bf16[512,512]{1,0:T(8,128)(2,1)S(1)}, bf16[512,512]{1,0:T(8,128)(2,1)}, u32[]{:S(2)}) copy-start(bf16[512,512]{1,0:T(8,128)(2,1)} %constant.39.clone.table) | copy-start | bytes 1572868
  27.4 8.6 %copy-start.3 = (bf16[16,8,1024]{2,1,0:T(8,128)(2,1)S(1)}, bf16[16,8,1024]{2,1,0:T(8,128)(2,1)}, u32[]{:S(2)}) copy-start(bf16[16,8,1024]{2,1,0:T(8,128)(2,1)} %sky.1) | copy-start | bytes 786436
  27.4 3.6 %collective-permute-start.2 = (bf16[2,4,2,2,32,128]{5,4,3,2,1,0:T(8,128)(2,1)S(1)}, bf16[2,4,2,2,32,128]{5,4,3,2,1,0:T(8,128)(2,1)S(1)}, u32[]{:S(2)}, u32[]{:S(2)}) collective-permute-start(bf16[2,4,2,2,32,128]{5,4,3,2,1,0:T(8,128)(2,1)S(1)} %pad_maximum_fusion.1), channel_id=1, source_target_pairs={{0,1},{1,0},{2,3},{3,2},{4,5},{5,4},{6,7},{7,6},{8,9},{9,8},{10,11... | collective-permute-start | bytes 786440 | tf_op jit(solution)/shard_map/ppermute | solution.py:40
  32.5 16.5 %collective-permute-start.3 = (bf16[8,2,2,16,128]{4,3,2,1,0:T(8,128)(2,1)S(1)}, bf16[8,2,2,16,128]{4,3,2,1,0:T(8,128)(2,1)S(1)}, u32[]{:S(2)}, u32[]{:S(2)}) collective-permute-start(bf16[8,2,2,16,128]{4,3,2,1,0:T(8,128)(2,1)S(1)} %get-tuple-element.34.delta), channel_id=1, source_target_pairs={{0,128},{64,192},{128,0},{192,64},{256,384},{320,448},{384,256},{4... | collective-permute-start | bytes 393224 | tf_op jit(solution)/shard_map/ppermute | solution.py:35
  37.3 11.8 %copy-start.2 = (bf16[4,256,256]{2,1,0:T(8,128)(2,1)S(1)}, bf16[4,256,256]{2,1,0:T(8,128)(2,1)}, u32[]{:S(2)}) copy-start(bf16[4,256,256]{2,1,0:T(8,128)(2,1)} %constant.38.clone.tables) | copy-start | bytes 1572868
  52.7 8.7 %collective-permute-start.5 = (bf16[8,2,2,16,128]{4,3,2,1,0:T(8,128)(2,1)S(1)}, bf16[8,2,2,16,128]{4,3,2,1,0:T(8,128)(2,1)S(1)}, u32[]{:S(2)}, u32[]{:S(2)}) collective-permute-start(bf16[8,2,2,16,128]{4,3,2,1,0:T(8,128)(2,1)S(1)} %shard_map.96), channel_id=1, source_target_pairs={{0,128},{64,192},{128,0},{192,64},{256,384},{320,448},{384,256},{4... | collective-permute-start | bytes 393224 | tf_op jit(solution)/shard_map/ppermute | solution.py:35
  63.1 3.2 %collective-permute-start.6 = (bf16[2,4,2,32,128]{4,3,2,1,0:T(8,128)(2,1)S(1)}, bf16[2,4,2,32,128]{4,3,2,1,0:T(8,128)(2,1)S(1)}, u32[]{:S(2)}, u32[]{:S(2)}) collective-permute-start(bf16[2,4,2,32,128]{4,3,2,1,0:T(8,128)(2,1)S(1)} %get-tuple-element.39), channel_id=1, source_target_pairs={{0,1},{1,0},{2,3},{3,2},{4,5},{5,4},{6,7},{7,6},{8,9},{9,8},{10,11... | collective-permute-start | bytes 393224 | tf_op jit(solution)/shard_map/ppermute | solution.py:40
  66.4 13.5 %collective-permute-start.7 = (bf16[4,2,32,128]{3,2,1,0:T(8,128)(2,1)S(1)}, bf16[4,2,32,128]{3,2,1,0:T(8,128)(2,1)S(1)}, u32[]{:S(2)}, u32[]{:S(2)}) collective-permute-start(bf16[4,2,32,128]{3,2,1,0:T(8,128)(2,1)S(1)} %get-tuple-element.41), channel_id=1, source_target_pairs={{0,318},{1,319},{2,4},{3,5},{4,2},{5,3},{6,8},{7,9},{8,6},{9,7},{1... | collective-permute-start | bytes 196616 | tf_op jit(solution)/shard_map/ppermute | solution.py:56
  68.3 13.9 %collective-permute-start.8 = (bf16[4,2,32,128]{3,2,1,0:T(8,128)(2,1)S(1)}, bf16[4,2,32,128]{3,2,1,0:T(8,128)(2,1)S(1)}, u32[]{:S(2)}, u32[]{:S(2)}) collective-permute-start(bf16[4,2,32,128]{3,2,1,0:T(8,128)(2,1)S(1)} %get-tuple-element.42), channel_id=1, source_target_pairs={{0,2},{1,3},{2,0},{3,1},{4,6},{5,7},{6,4},{7,5},{8,10},{9,11},{10,... | collective-permute-start | bytes 196616 | tf_op jit(solution)/shard_map/ppermute | solution.py:56
  82.3 11.3 %collective-permute-start.9 = (bf16[4,2,32,128]{3,2,1,0:T(8,128)(2,1)S(1)}, bf16[4,2,32,128]{3,2,1,0:T(8,128)(2,1)S(1)}, u32[]{:S(2)}, u32[]{:S(2)}) collective-permute-start(bf16[4,2,32,128]{3,2,1,0:T(8,128)(2,1)S(1)} %fusion.3), channel_id=1, source_target_pairs={{0,256},{64,320},{128,384},{192,448},{256,0},{320,64},{384,128},{4... | collective-permute-start | bytes 196616 | tf_op jit(solution)/shard_map/ppermute | solution.py:35
  93.6 7.2 %collective-permute-start.10 = (bf16[4,2,32,128]{3,2,1,0:T(8,128)(2,1)S(1)}, bf16[4,2,32,128]{3,2,1,0:T(8,128)(2,1)S(1)}, u32[]{:S(2)}, u32[]{:S(2)}) collective-permute-start(bf16[4,2,32,128]{3,2,1,0:T(8,128)(2,1)S(1)} %add_convert_fusion.mine), channel_id=1, source_target_pairs={{0,128},{64,192},{128,0},{192,64},{256,384},{320,448},{384,256},{4... | collective-permute-start | bytes 196616 | tf_op jit(solution)/shard_map/ppermute | solution.py:35
  100.8 6.9 %collective-permute-start.11 = (bf16[2,4,2,32,128]{4,3,2,1,0:T(8,128)(2,1)S(1)}, bf16[2,4,2,32,128]{4,3,2,1,0:T(8,128)(2,1)S(1)}, u32[]{:S(2)}, u32[]{:S(2)}) collective-permute-start(bf16[2,4,2,32,128]{4,3,2,1,0:T(8,128)(2,1)S(1)} %pad_maximum_fusion.2), channel_id=1, source_target_pairs={{0,64},{64,0},{128,192},{192,128},{256,320},{320,256},{384,448},{4... | collective-permute-start | bytes 393224 | tf_op jit(solution)/shard_map/ppermute | solution.py:35

commit v5 on v4

--- a/solution.py
+++ b/solution.py
@@ -24,7 +24,7 @@
 PARTS = POLS * HALVES
 LANES = GROUP * W
 NEAR = 2 * REACH + 1
-QUADS_STEP = 4
+QUADS_STEP = 8
 SETS = 2
 SMEM = pltpu.SMEM
 VMEM = pltpu.VMEM
@@ -462,6 +462,8 @@
     in_smem = pl.BlockSpec(memory_space=SMEM)
     in_vmem = pl.BlockSpec(memory_space=VMEM)
 
+    both = jnp.concatenate([weights, sky])
+    both, screens, direction = lax.optimization_barrier((both, screens, direction))
     own = call(
         own_kernel,
         jax.ShapeDtypeStruct((ST_DEV, 2, HALVES, G // 2, 2 * G), jnp.bfloat16),
@@ -476,8 +478,8 @@
         [],
     )(pairs.T, pointing[None], counts)
     chip_b = across_chips(own, 1)
-    weights_sent, sky_sent, meta = lax.optimization_barrier((weights, sky, meta))
-    other = across_chan(jnp.concatenate([weights_sent, sky_sent]), 1)
+    both, meta = lax.optimization_barrier((both, meta))
+    other = across_chan(both, 1)
     meta, chip_a, chip_b = lax.optimization_barrier((meta, chip_a, chip_b))
     shared_is_a = core == chip_odd
     sibling = to_sibling(jnp.stack([own, jnp.where(shared_is_a, chip_a, chip_b)]))

time: 109 us -> 108 us (level)
  the two profiles are of different devices: /device:TPU:8 before, /device:TPU:32 now
where the time goes in v5:
time: 108 us; the launch traced here: 107 us
  starting transfers between devices  62.8 us (58%)
  waiting for transfers between devices  27.7 us (26%)
  Pallas kernels  13.6 us (13%)
  other arithmetic  1.42 us (1%)
    ppermute x6, starting transfers between devices, across_chan(): return lax.ppermute(value, 'chan', [(i, i ^ bit) for i in range(count)])  31.5 us
    ppermute x4, starting transfers between devices, across_chips(): return lax.ppermute(value, ('chan', 'base'), perm)  27.3 us
    ppermute x6, waiting for transfers between devices, across_chan(): return lax.ppermute(value, 'chan', [(i, i ^ bit) for i in range(count)])  16.7 us
    ppermute x4, waiting for transfers between devices, across_chips(): return lax.ppermute(value, ('chan', 'base'), perm)  8.19 us
    pallas_call x2, Pallas kernels, hessian(): call(hessian_kernel, jax.ShapeDtypeStruct(delta_shape, jnp.bfloat16), [in...  6.47 us
    ppermute x2, starting transfers between devices, to_sibling(): return lax.ppermute(value, 'base', [(i, i ^ 1) for i in range(count)])  3.97 us
    ppermute x2, waiting for transfers between devices, to_sibling(): return lax.ppermute(value, 'base', [(i, i ^ 1) for i in range(count)])  2.81 us
    pallas_call x2, Pallas kernels, prepared(): call(functools.partial(prepare_kernel, first), [quad_shape] * 2, [in_smem...  2.66 us
  transfers between devices with their start and end apart: 12, of which 9 were waited for; matrix products, arithmetic and copies ran while one was open for 0% of the time, Pallas kernels for 7%

profile of v5, /device:TPU:32, one launch (start us, length us, event | category | flops | bytes accessed | tf_op | source)
XLA Modules:
  0.0 107.2 jit_solution(16149438663397889911)
XLA Ops:
  0.0 0.0 copy-start.5
  0.0 0.0 copy-start.4
  0.0 1.2 %pad_maximum_fusion = bf16[48,8,1024]{2,1,0:T(8,128)(2,1)S(1)} fusion(bf16[16,8,1024]{2,1,0:T(8,128)(2,1)} %sky.1, bf16[32,8,1024]{2,1,0:T(8,128)(2,1)} %weights.1), kind=kLoop, calls=%fused_computation | loop fusion | flops 393216 | bytes 1572864 | tf_op jit(solution)/shard_map/concatenate | solution.py:465
  1.3 0.0 copy-done.5
  1.3 0.0 copy-done.4
  1.3 0.2 shard_map.92.own
  1.5 16.5 %collective-permute-start.1 = (bf16[4,2,2,32,128]{4,3,2,1,0:T(8,128)(2,1)S(1)}, bf16[4,2,2,32,128]{4,3,2,1,0:T(8,128)(2,1)S(1)}, u32[]{:S(2)}, u32[]{:S(2)}) collective-permute-start(bf16[4,2,2,32,128]{4,3,2,1,0:T(8,128)(2,1)S(1)} %shard_map.92.own), channel_id=1, source_target_pairs={{0,318},{1,319},{2,4},{3,5},{4,2},{5,3},{6,8},{7,9},{8,6},{9,7},{1... | collective-permute-start | bytes 393224 | tf_op jit(solution)/shard_map/ppermute | solution.py:56
  18.0 1.9 %collective-permute-start = (bf16[4,2,2,32,128]{4,3,2,1,0:T(8,128)(2,1)S(1)}, bf16[4,2,2,32,128]{4,3,2,1,0:T(8,128)(2,1)S(1)}, u32[]{:S(2)}, u32[]{:S(2)}) collective-permute-start(bf16[4,2,2,32,128]{4,3,2,1,0:T(8,128)(2,1)S(1)} %shard_map.92.own), channel_id=1, source_target_pairs={{0,2},{1,3},{2,0},{3,1},{4,6},{5,7},{6,4},{7,5},{8,10},{9,11},{10,... | collective-permute-start | bytes 393224 | tf_op jit(solution)/shard_map/ppermute | solution.py:56
  20.5 0.0 copy-start.6
  20.6 0.0 copy-start.7
  20.6 0.7 copy-done.6
  21.2 0.0 copy-done.7
  21.3 2.9 %collective-permute-start.4 = (bf16[48,8,1024]{2,1,0:T(8,128)(2,1)S(1)}, bf16[48,8,1024]{2,1,0:T(8,128)(2,1)S(1)}, u32[]{:S(2)}, u32[]{:S(2)}) collective-permute-start(bf16[48,8,1024]{2,1,0:T(8,128)(2,1)S(1)} %pad_maximum_fusion), channel_id=1, source_target_pairs={{0,64},{64,0},{128,192},{192,128},{256,320},{320,256},{384,448},{4... | collective-permute-start | bytes 2359304 | tf_op jit(solution)/shard_map/ppermute | solution.py:35
  24.2 2.8 %collective-permute-done.1.chip_b = bf16[4,2,2,32,128]{4,3,2,1,0:T(8,128)(2,1)S(1)} collective-permute-done((bf16[4,2,2,32,128]{4,3,2,1,0:T(8,128)(2,1)S(1)}, bf16[4,2,2,32,128]{4,3,2,1,0:T(8,128)(2,1)S(1)}, u32[]{:S(2)}, u32[]{:S(2)}) %collective-permute-start.1) | collective-permute-done | bytes 131104 | tf_op jit(solution)/shard_map/ppermute | solution.py:56
  27.0 0.0 collective-permute-done.chip_a
  27.0 0.0 copy-start.3
  27.0 0.0 copy-start
  27.0 0.0 copy-start.1
  27.1 2.1 %collective-permute-start.2 = (bf16[2,4,2,2,32,128]{5,4,3,2,1,0:T(8,128)(2,1)S(1)}, bf16[2,4,2,2,32,128]{5,4,3,2,1,0:T(8,128)(2,1)S(1)}, u32[]{:S(2)}, u32[]{:S(2)}) collective-permute-start(bf16[2,4,2,2,32,128]{5,4,3,2,1,0:T(8,128)(2,1)S(1)} %pad_maximum_fusion.1), channel_id=1, source_target_pairs={{0,1},{1,0},{2,3},{3,2},{4,5},{5,4},{6,7},{7,6},{8,9},{9,8},{10,11... | collective-permute-start | bytes 786440 | tf_op jit(solution)/shard_map/ppermute | solution.py:40
  29.1 1.5 %collective-permute-done.2.sibling = bf16[2,4,2,2,32,128]{5,4,3,2,1,0:T(8,128)(2,1)S(1)} collective-permute-done((bf16[2,4,2,2,32,128]{5,4,3,2,1,0:T(8,128)(2,1)S(1)}, bf16[2,4,2,2,32,128]{5,4,3,2,1,0:T(8,128)(2,1)S(1)}, u32[]{:S(2)}, u32[]{:S(2)}) %collective-permute-start.2) | collective-permute-done | bytes 262176 | tf_op jit(solution)/shard_map/ppermute | solution.py:40
  30.6 1.6 %shard_map.93 = (bf16[8,2,2,16,128]{4,3,2,1,0:T(8,128)(2,1)S(1)}, f32[20,2,32,128]{3,2,1,0:T(8,128)S(1)}, f32[20,2,32,128]{3,2,1,0:T(8,128)S(1)}) custom-call(s32[8,32]{1,0:T(8,128)S(1)} %shard_map.91.meta.args_0_, bf16[4,2,2,32,128]{4,3,2,1,0:T(8,128)(2,1)S(1)} %shard_map.92.own, bf16[4,2,2,32,128]{4,3,2,1,0:T(8,128)(2,1)S(1)} %collective-permute-done.chip_a, ...), custom_call_target="tpu_custom_call" | custom-call | tf_op jit(solution)/shard_map/pallas_call | solution.py:491
  32.2 6.5 %collective-permute-start.3 = (bf16[8,2,2,16,128]{4,3,2,1,0:T(8,128)(2,1)S(1)}, bf16[8,2,2,16,128]{4,3,2,1,0:T(8,128)(2,1)S(1)}, u32[]{:S(2)}, u32[]{:S(2)}) collective-permute-start(bf16[8,2,2,16,128]{4,3,2,1,0:T(8,128)(2,1)S(1)} %get-tuple-element.38.delta), channel_id=1, source_target_pairs={{0,128},{64,192},{128,0},{192,64},{256,384},{320,448},{384,256},{4... | collective-permute-start | bytes 393224 | tf_op jit(solution)/shard_map/ppermute | solution.py:35
  38.7 0.0 copy-done.3
  38.7 0.0 copy-done
  38.7 0.0 copy-done.1
  38.7 1.3 %shard_map.94 = (bf16[8,8,32,128]{3,2,1,0:T(8,128)(2,1)S(1)}, bf16[8,8,32,128]{3,2,1,0:T(8,128)(2,1)S(1)}) custom-call(s32[8,32]{1,0:T(8,128)S(1)} %shard_map.91.meta.args_0_, bf16[32,8,1024]{2,1,0:T(8,128)(2,1)S(1)} %copy-done, bf16[16,8,1024]{2,1,0:T(8,128)(2,1)S(1)} %copy-done.3, bf16[512,512]{1,0:T(8,128)(2,1)S(1)} %copy-done.1), custom_call_target="tpu_custom_call" | custom-call | tf_op jit(solution)/shard_map/pallas_call | solution.py:506
  40.1 0.0 copy-start.2
  40.1 6.0 %collective-permute-done.4.weights.sky = bf16[48,8,1024]{2,1,0:T(8,128)(2,1)S(1)} collective-permute-done((bf16[48,8,1024]{2,1,0:T(8,128)(2,1)S(1)}, bf16[48,8,1024]{2,1,0:T(8,128)(2,1)S(1)}, u32[]{:S(2)}, u32[]{:S(2)}) %collective-permute-start.4) | collective-permute-done | bytes 786464 | tf_op jit(solution)/shard_map/ppermute | solution.py:35
  46.1 1.3 %shard_map.95 = (bf16[8,8,32,128]{3,2,1,0:T(8,128)(2,1)S(1)}, bf16[8,8,32,128]{3,2,1,0:T(8,128)(2,1)S(1)}) custom-call(s32[8,32]{1,0:T(8,128)S(1)} %shard_map.91.meta.args_0_, bf16[48,8,1024]{2,1,0:T(8,128)(2,1)S(1)} %collective-permute-done.4.weights.sky, bf16[48,8,1024]{2,1,0:T(8,128)(2,1)S(1)} %collective-permute-done.4.weights.sky, ...), custom_call_target="tpu_custom_call" | custom-call | tf_op jit(solution)/shard_map/pallas_call | solution.py:506
  47.4 0.0 collective-permute-done.3.delta
  47.4 0.0 copy-done.2
  47.4 3.2 %shard_map.96 = bf16[8,2,2,16,128]{4,3,2,1,0:T(8,128)(2,1)S(1)} custom-call(s32[8,32]{1,0:T(8,128)S(1)} %shard_map.91.meta.args_0_, bf16[8,2,2,16,128]{4,3,2,1,0:T(8,128)(2,1)S(1)} %collective-permute-done.3.delta, bf16[8,8,32,128]{3,2,1,0:T(8,128)(2,1)S(1)} %get-tuple-element.33.weights_0, bf16[8,8,32,128]{3,2,1,0:T(8,128)(2,1)S(1)} %get-tuple-element.35.weights_1, ...), custom_call_target="tpu_custom_call" | custom-call | tf_op jit(solution)/shard_map/pallas_call | solution.py:522
  50.7 2.9 %collective-permute-start.5 = (bf16[8,2,2,16,128]{4,3,2,1,0:T(8,128)(2,1)S(1)}, bf16[8,2,2,16,128]{4,3,2,1,0:T(8,128)(2,1)S(1)}, u32[]{:S(2)}, u32[]{:S(2)}) collective-permute-start(bf16[8,2,2,16,128]{4,3,2,1,0:T(8,128)(2,1)S(1)} %shard_map.96), channel_id=1, source_target_pairs={{0,128},{64,192},{128,0},{192,64},{256,384},{320,448},{384,256},{4... | collective-permute-start | bytes 393224 | tf_op jit(solution)/shard_map/ppermute | solution.py:35
  53.6 3.2 %shard_map.97.args_1_ = bf16[8,2,2,16,128]{4,3,2,1,0:T(8,128)(2,1)S(1)} custom-call(s32[8,32]{1,0:T(8,128)S(1)} %shard_map.91.meta.args_0_, bf16[8,2,2,16,128]{4,3,2,1,0:T(8,128)(2,1)S(1)} %get-tuple-element.38.delta, bf16[8,8,32,128]{3,2,1,0:T(8,128)(2,1)S(1)} %get-tuple-element.33.weights_0, bf16[8,8,32,128]{3,2,1,0:T(8,128)(2,1)S(1)} %get-tuple-element.35.weights_1, ...), custom_call_target="tpu_custom_call" | custom-call | tf_op jit(solution)/shard_map/pallas_call | solution.py:522
  56.8 2.3 %collective-permute-done.5.args_2_ = bf16[8,2,2,16,128]{4,3,2,1,0:T(8,128)(2,1)S(1)} collective-permute-done((bf16[8,2,2,16,128]{4,3,2,1,0:T(8,128)(2,1)S(1)}, bf16[8,2,2,16,128]{4,3,2,1,0:T(8,128)(2,1)S(1)}, u32[]{:S(2)}, u32[]{:S(2)}) %collective-permute-start.5) | collective-permute-done | bytes 131104 | tf_op jit(solution)/shard_map/ppermute | solution.py:35
  59.2 1.7 %shard_map.98 = (f32[4,2,32,128]{3,2,1,0:T(8,128)S(1)}, f32[2,4,2,32,128]{4,3,2,1,0:T(8,128)S(1)}, bf16[2,4,2,32,128]{4,3,2,1,0:T(8,128)(2,1)S(1)}) custom-call(s32[8,32]{1,0:T(8,128)S(1)} %shard_map.91.meta.args_0_, bf16[8,2,2,16,128]{4,3,2,1,0:T(8,128)(2,1)S(1)} %shard_map.97.args_1_, bf16[8,2,2,16,128]{4,3,2,1,0:T(8,128)(2,1)S(1)} %collective-permute-done.5.args_2_, ...), custom_call_target="tpu_custom_call" | custom-call | tf_op jit(solution)/shard_map/pallas_call | solution.py:538
  60.8 1.9 %collective-permute-start.6 = (bf16[2,4,2,32,128]{4,3,2,1,0:T(8,128)(2,1)S(1)}, bf16[2,4,2,32,128]{4,3,2,1,0:T(8,128)(2,1)S(1)}, u32[]{:S(2)}, u32[]{:S(2)}) collective-permute-start(bf16[2,4,2,32,128]{4,3,2,1,0:T(8,128)(2,1)S(1)} %get-tuple-element.43), channel_id=1, source_target_pairs={{0,1},{1,0},{2,3},{3,2},{4,5},{5,4},{6,7},{7,6},{8,9},{9,8},{10,11... | collective-permute-start | bytes 393224 | tf_op jit(solution)/shard_map/ppermute | solution.py:40
  62.8 1.3 %collective-permute-done.6 = bf16[2,4,2,32,128]{4,3,2,1,0:T(8,128)(2,1)S(1)} collective-permute-done((bf16[2,4,2,32,128]{4,3,2,1,0:T(8,128)(2,1)S(1)}, bf16[2,4,2,32,128]{4,3,2,1,0:T(8,128)(2,1)S(1)}, u32[]{:S(2)}, u32[]{:S(2)}) %collective-permute-start.6) | collective-permute-done | bytes 131104 | tf_op jit(solution)/shard_map/ppermute | solution.py:40
  64.2 7.0 %collective-permute-start.7 = (bf16[4,2,32,128]{3,2,1,0:T(8,128)(2,1)S(1)}, bf16[4,2,32,128]{3,2,1,0:T(8,128)(2,1)S(1)}, u32[]{:S(2)}, u32[]{:S(2)}) collective-permute-start(bf16[4,2,32,128]{3,2,1,0:T(8,128)(2,1)S(1)} %get-tuple-element.45), channel_id=1, source_target_pairs={{0,318},{1,319},{2,4},{3,5},{4,2},{5,3},{6,8},{7,9},{8,6},{9,7},{1... | collective-permute-start | bytes 196616 | tf_op jit(solution)/shard_map/ppermute | solution.py:56
  71.1 1.9 %collective-permute-start.8 = (bf16[4,2,32,128]{3,2,1,0:T(8,128)(2,1)S(1)}, bf16[4,2,32,128]{3,2,1,0:T(8,128)(2,1)S(1)}, u32[]{:S(2)}, u32[]{:S(2)}) collective-permute-start(bf16[4,2,32,128]{3,2,1,0:T(8,128)(2,1)S(1)} %get-tuple-element.46), channel_id=1, source_target_pairs={{0,2},{1,3},{2,0},{3,1},{4,6},{5,7},{6,4},{7,5},{8,10},{9,11},{10,... | collective-permute-start | bytes 196616 | tf_op jit(solution)/shard_map/ppermute | solution.py:56
  73.1 5.4 %collective-permute-done.7 = bf16[4,2,32,128]{3,2,1,0:T(8,128)(2,1)S(1)} collective-permute-done((bf16[4,2,32,128]{3,2,1,0:T(8,128)(2,1)S(1)}, bf16[4,2,32,128]{3,2,1,0:T(8,128)(2,1)S(1)}, u32[]{:S(2)}, u32[]{:S(2)}) %collective-permute-start.7) | collective-permute-done | bytes 65568 | tf_op jit(solution)/shard_map/ppermute | solution.py:56
  78.5 0.0 collective-permute-done.8
  78.5 7.1 %collective-permute-start.9 = (bf16[4,2,32,128]{3,2,1,0:T(8,128)(2,1)S(1)}, bf16[4,2,32,128]{3,2,1,0:T(8,128)(2,1)S(1)}, u32[]{:S(2)}, u32[]{:S(2)}) collective-permute-start(bf16[4,2,32,128]{3,2,1,0:T(8,128)(2,1)S(1)} %fusion.3), channel_id=1, source_target_pairs={{0,256},{64,320},{128,384},{192,448},{256,0},{320,64},{384,128},{4... | collective-permute-start | bytes 196616 | tf_op jit(solution)/shard_map/ppermute | solution.py:35
  85.7 2.9 %collective-permute-done.9 = bf16[4,2,32,128]{3,2,1,0:T(8,128)(2,1)S(1)} collective-permute-done((bf16[4,2,32,128]{3,2,1,0:T(8,128)(2,1)S(1)}, bf16[4,2,32,128]{3,2,1,0:T(8,128)(2,1)S(1)}, u32[]{:S(2)}, u32[]{:S(2)}) %collective-permute-start.9) | collective-permute-done | bytes 65568 | tf_op jit(solution)/shard_map/ppermute | solution.py:35
  88.6 8.3 %collective-permute-start.10 = (bf16[4,2,32,128]{3,2,1,0:T(8,128)(2,1)S(1)}, bf16[4,2,32,128]{3,2,1,0:T(8,128)(2,1)S(1)}, u32[]{:S(2)}, u32[]{:S(2)}) collective-permute-start(bf16[4,2,32,128]{3,2,1,0:T(8,128)(2,1)S(1)} %add_convert_fusion.mine), channel_id=1, source_target_pairs={{0,128},{64,192},{128,0},{192,64},{256,384},{320,448},{384,256},{4... | collective-permute-start | bytes 196616 | tf_op jit(solution)/shard_map/ppermute | solution.py:35
  97.0 2.3 %collective-permute-done.10.over_two = bf16[4,2,32,128]{3,2,1,0:T(8,128)(2,1)S(1)} collective-permute-done((bf16[4,2,32,128]{3,2,1,0:T(8,128)(2,1)S(1)}, bf16[4,2,32,128]{3,2,1,0:T(8,128)(2,1)S(1)}, u32[]{:S(2)}, u32[]{:S(2)}) %collective-permute-start.10) | collective-permute-done | bytes 65568 | tf_op jit(solution)/shard_map/ppermute | solution.py:35
  99.3 3.8 %collective-permute-start.11 = (bf16[2,4,2,32,128]{4,3,2,1,0:T(8,128)(2,1)S(1)}, bf16[2,4,2,32,128]{4,3,2,1,0:T(8,128)(2,1)S(1)}, u32[]{:S(2)}, u32[]{:S(2)}) collective-permute-start(bf16[2,4,2,32,128]{4,3,2,1,0:T(8,128)(2,1)S(1)} %pad_maximum_fusion.2), channel_id=1, source_target_pairs={{0,64},{64,0},{128,192},{192,128},{256,320},{320,256},{384,448},{4... | collective-permute-start | bytes 393224 | tf_op jit(solution)/shard_map/ppermute | solution.py:35
  103.1 3.1 %collective-permute-done.11.over_one = bf16[2,4,2,32,128]{4,3,2,1,0:T(8,128)(2,1)S(1)} collective-permute-done((bf16[2,4,2,32,128]{4,3,2,1,0:T(8,128)(2,1)S(1)}, bf16[2,4,2,32,128]{4,3,2,1,0:T(8,128)(2,1)S(1)}, u32[]{:S(2)}, u32[]{:S(2)}) %collective-permute-start.11) | collective-permute-done | bytes 131104 | tf_op jit(solution)/shard_map/ppermute | solution.py:35
  106.2 1.0 shard_map.99
  (8 shorter events, 0.2 us)
Async XLA Ops:
  0.0 1.3 %copy-start.5 = (bf16[4,8,4096]{2,1,0:T(8,128)(2,1)S(1)}, bf16[4,8,4096]{2,1,0:T(8,128)(2,1)}, u32[]{:S(2)}) copy-start(bf16[4,8,4096]{2,1,0:T(8,128)(2,1)} %direction) | copy-start | bytes 786436
  0.0 1.3 %copy-start.4 = (bf16[4,8,4096]{2,1,0:T(8,128)(2,1)S(1)}, bf16[4,8,4096]{2,1,0:T(8,128)(2,1)}, u32[]{:S(2)}) copy-start(bf16[4,8,4096]{2,1,0:T(8,128)(2,1)} %screens) | copy-start | bytes 786436
  1.5 25.5 %collective-permute-start.1 = (bf16[4,2,2,32,128]{4,3,2,1,0:T(8,128)(2,1)S(1)}, bf16[4,2,2,32,128]{4,3,2,1,0:T(8,128)(2,1)S(1)}, u32[]{:S(2)}, u32[]{:S(2)}) collective-permute-start(bf16[4,2,2,32,128]{4,3,2,1,0:T(8,128)(2,1)S(1)} %shard_map.92.own), channel_id=1, source_target_pairs={{0,318},{1,319},{2,4},{3,5},{4,2},{5,3},{6,8},{7,9},{8,6},{9,7},{1... | collective-permute-start | bytes 393224 | tf_op jit(solution)/shard_map/ppermute | solution.py:56
  18.0 9.0 %collective-permute-start = (bf16[4,2,2,32,128]{4,3,2,1,0:T(8,128)(2,1)S(1)}, bf16[4,2,2,32,128]{4,3,2,1,0:T(8,128)(2,1)S(1)}, u32[]{:S(2)}, u32[]{:S(2)}) collective-permute-start(bf16[4,2,2,32,128]{4,3,2,1,0:T(8,128)(2,1)S(1)} %shard_map.92.own), channel_id=1, source_target_pairs={{0,2},{1,3},{2,0},{3,1},{4,6},{5,7},{6,4},{7,5},{8,10},{9,11},{10,... | collective-permute-start | bytes 393224 | tf_op jit(solution)/shard_map/ppermute | solution.py:56
  20.5 0.7 copy-start.6
  20.6 0.7 copy-start.7
  21.3 24.8 %collective-permute-start.4 = (bf16[48,8,1024]{2,1,0:T(8,128)(2,1)S(1)}, bf16[48,8,1024]{2,1,0:T(8,128)(2,1)S(1)}, u32[]{:S(2)}, u32[]{:S(2)}) collective-permute-start(bf16[48,8,1024]{2,1,0:T(8,128)(2,1)S(1)} %pad_maximum_fusion), channel_id=1, source_target_pairs={{0,64},{64,0},{128,192},{192,128},{256,320},{320,256},{384,448},{4... | collective-permute-start | bytes 2359304 | tf_op jit(solution)/shard_map/ppermute | solution.py:35
  27.0 11.7 %copy-start.3 = (bf16[16,8,1024]{2,1,0:T(8,128)(2,1)S(1)}, bf16[16,8,1024]{2,1,0:T(8,128)(2,1)}, u32[]{:S(2)}) copy-start(bf16[16,8,1024]{2,1,0:T(8,128)(2,1)} %sky.1) | copy-start | bytes 786436
  27.0 11.7 %copy-start = (bf16[32,8,1024]{2,1,0:T(8,128)(2,1)S(1)}, bf16[32,8,1024]{2,1,0:T(8,128)(2,1)}, u32[]{:S(2)}) copy-start(bf16[32,8,1024]{2,1,0:T(8,128)(2,1)} %weights.1) | copy-start | bytes 1572868
  27.0 11.7 %copy-start.1 = (bf16[512,512]{1,0:T(8,128)(2,1)S(1)}, bf16[512,512]{1,0:T(8,128)(2,1)}, u32[]{:S(2)}) copy-start(bf16[512,512]{1,0:T(8,128)(2,1)} %constant.39.clone.table) | copy-start | bytes 1572868
  27.1 3.6 %collective-permute-start.2 = (bf16[2,4,2,2,32,128]{5,4,3,2,1,0:T(8,128)(2,1)S(1)}, bf16[2,4,2,2,32,128]{5,4,3,2,1,0:T(8,128)(2,1)S(1)}, u32[]{:S(2)}, u32[]{:S(2)}) collective-permute-start(bf16[2,4,2,2,32,128]{5,4,3,2,1,0:T(8,128)(2,1)S(1)} %pad_maximum_fusion.1), channel_id=1, source_target_pairs={{0,1},{1,0},{2,3},{3,2},{4,5},{5,4},{6,7},{7,6},{8,9},{9,8},{10,11... | collective-permute-start | bytes 786440 | tf_op jit(solution)/shard_map/ppermute | solution.py:40
  32.2 15.2 %collective-permute-start.3 = (bf16[8,2,2,16,128]{4,3,2,1,0:T(8,128)(2,1)S(1)}, bf16[8,2,2,16,128]{4,3,2,1,0:T(8,128)(2,1)S(1)}, u32[]{:S(2)}, u32[]{:S(2)}) collective-permute-start(bf16[8,2,2,16,128]{4,3,2,1,0:T(8,128)(2,1)S(1)} %get-tuple-element.38.delta), channel_id=1, source_target_pairs={{0,128},{64,192},{128,0},{192,64},{256,384},{320,448},{384,256},{4... | collective-permute-start | bytes 393224 | tf_op jit(solution)/shard_map/ppermute | solution.py:35
  40.1 7.3 %copy-start.2 = (bf16[4,256,256]{2,1,0:T(8,128)(2,1)S(1)}, bf16[4,256,256]{2,1,0:T(8,128)(2,1)}, u32[]{:S(2)}) copy-start(bf16[4,256,256]{2,1,0:T(8,128)(2,1)} %constant.38.clone.tables) | copy-start | bytes 1572868
  50.7 8.5 %collective-permute-start.5 = (bf16[8,2,2,16,128]{4,3,2,1,0:T(8,128)(2,1)S(1)}, bf16[8,2,2,16,128]{4,3,2,1,0:T(8,128)(2,1)S(1)}, u32[]{:S(2)}, u32[]{:S(2)}) collective-permute-start(bf16[8,2,2,16,128]{4,3,2,1,0:T(8,128)(2,1)S(1)} %shard_map.96), channel_id=1, source_target_pairs={{0,128},{64,192},{128,0},{192,64},{256,384},{320,448},{384,256},{4... | collective-permute-start | bytes 393224 | tf_op jit(solution)/shard_map/ppermute | solution.py:35
  60.8 3.2 %collective-permute-start.6 = (bf16[2,4,2,32,128]{4,3,2,1,0:T(8,128)(2,1)S(1)}, bf16[2,4,2,32,128]{4,3,2,1,0:T(8,128)(2,1)S(1)}, u32[]{:S(2)}, u32[]{:S(2)}) collective-permute-start(bf16[2,4,2,32,128]{4,3,2,1,0:T(8,128)(2,1)S(1)} %get-tuple-element.43), channel_id=1, source_target_pairs={{0,1},{1,0},{2,3},{3,2},{4,5},{5,4},{6,7},{7,6},{8,9},{9,8},{10,11... | collective-permute-start | bytes 393224 | tf_op jit(solution)/shard_map/ppermute | solution.py:40
  64.2 14.3 %collective-permute-start.7 = (bf16[4,2,32,128]{3,2,1,0:T(8,128)(2,1)S(1)}, bf16[4,2,32,128]{3,2,1,0:T(8,128)(2,1)S(1)}, u32[]{:S(2)}, u32[]{:S(2)}) collective-permute-start(bf16[4,2,32,128]{3,2,1,0:T(8,128)(2,1)S(1)} %get-tuple-element.45), channel_id=1, source_target_pairs={{0,318},{1,319},{2,4},{3,5},{4,2},{5,3},{6,8},{7,9},{8,6},{9,7},{1... | collective-permute-start | bytes 196616 | tf_op jit(solution)/shard_map/ppermute | solution.py:56
  71.1 7.4 %collective-permute-start.8 = (bf16[4,2,32,128]{3,2,1,0:T(8,128)(2,1)S(1)}, bf16[4,2,32,128]{3,2,1,0:T(8,128)(2,1)S(1)}, u32[]{:S(2)}, u32[]{:S(2)}) collective-permute-start(bf16[4,2,32,128]{3,2,1,0:T(8,128)(2,1)S(1)} %get-tuple-element.46), channel_id=1, source_target_pairs={{0,2},{1,3},{2,0},{3,1},{4,6},{5,7},{6,4},{7,5},{8,10},{9,11},{10,... | collective-permute-start | bytes 196616 | tf_op jit(solution)/shard_map/ppermute | solution.py:56
  78.5 10.1 %collective-permute-start.9 = (bf16[4,2,32,128]{3,2,1,0:T(8,128)(2,1)S(1)}, bf16[4,2,32,128]{3,2,1,0:T(8,128)(2,1)S(1)}, u32[]{:S(2)}, u32[]{:S(2)}) collective-permute-start(bf16[4,2,32,128]{3,2,1,0:T(8,128)(2,1)S(1)} %fusion.3), channel_id=1, source_target_pairs={{0,256},{64,320},{128,384},{192,448},{256,0},{320,64},{384,128},{4... | collective-permute-start | bytes 196616 | tf_op jit(solution)/shard_map/ppermute | solution.py:35
  88.6 10.6 %collective-permute-start.10 = (bf16[4,2,32,128]{3,2,1,0:T(8,128)(2,1)S(1)}, bf16[4,2,32,128]{3,2,1,0:T(8,128)(2,1)S(1)}, u32[]{:S(2)}, u32[]{:S(2)}) collective-permute-start(bf16[4,2,32,128]{3,2,1,0:T(8,128)(2,1)S(1)} %add_convert_fusion.mine), channel_id=1, source_target_pairs={{0,128},{64,192},{128,0},{192,64},{256,384},{320,448},{384,256},{4... | collective-permute-start | bytes 196616 | tf_op jit(solution)/shard_map/ppermute | solution.py:35
  99.3 6.9 %collective-permute-start.11 = (bf16[2,4,2,32,128]{4,3,2,1,0:T(8,128)(2,1)S(1)}, bf16[2,4,2,32,128]{4,3,2,1,0:T(8,128)(2,1)S(1)}, u32[]{:S(2)}, u32[]{:S(2)}) collective-permute-start(bf16[2,4,2,32,128]{4,3,2,1,0:T(8,128)(2,1)S(1)} %pad_maximum_fusion.2), channel_id=1, source_target_pairs={{0,64},{64,0},{128,192},{192,128},{256,320},{320,256},{384,448},{4... | collective-permute-start | bytes 393224 | tf_op jit(solution)/shard_map/ppermute | solution.py:35

commit v6 on v5

--- a/solution.py
+++ b/solution.py
@@ -377,7 +377,7 @@
     group = group_index(HALF_ROWS)
     scale = 1.0 / channels_total
 
-    def visit(quad, carry):
+    def add(quad, turn):
         for half in range(HALVES):
             for part in range(2):
                 total = kept[quad, part, half].astype(jnp.float32)
@@ -408,9 +408,13 @@
                     beams[station_p, half, rows, :] * grad_real
                     - turned[station_p, half, rows, :] * grad_imag
                 )
+
+    def visit(step, carry):
+        for later in range(2):
+            add(2 * step + later, turn.at[later])
         return carry
 
-    lax.fori_loop(0, quads, visit, 0)
+    lax.fori_loop(0, (quads + 1) // 2, visit, 0)
 
     def total(block, half):
         stations = pl.ds(block * ST_DEV, ST_DEV)
@@ -543,7 +547,8 @@
             jax.ShapeDtypeStruct((2,) + block_shape, jnp.bfloat16),
         ],
         [in_smem] + [in_vmem] * 4,
-        [pltpu.VMEM((NEAR * ST_DEV, G // 2, 2 * G), wide)] * 4 + [turn],
+        [pltpu.VMEM((NEAR * ST_DEV, G // 2, 2 * G), wide)] * 4
+        + [pltpu.VMEM((2, HALVES, 2, HALF_ROWS, LANES), wide)],
     )(meta, kept, back_two, beams, turned)
     from_sibling = to_sibling(sum_sibling).astype(wide)
     sum_a = sum_chips[0] + jnp.where(shared_is_a, from_sibling[1], 0.0)

time: 108 us -> 107 us (level)
  no operation moved by 1% of the time
where the time goes in v6:
time: 107 us
  starting transfers between devices  63.2 us (59%)
  waiting for transfers between devices  27.5 us (26%)
  Pallas kernels  12.9 us (12%)
  other arithmetic  1.42 us (1%)
    ppermute x6, starting transfers between devices, across_chan(): return lax.ppermute(value, 'chan', [(i, i ^ bit) for i in range(count)])  31.5 us
    ppermute x4, starting transfers between devices, across_chips(): return lax.ppermute(value, ('chan', 'base'), perm)  27.8 us
    ppermute x6, waiting for transfers between devices, across_chan(): return lax.ppermute(value, 'chan', [(i, i ^ bit) for i in range(count)])  17 us
    ppermute x4, waiting for transfers between devices, across_chips(): return lax.ppermute(value, ('chan', 'base'), perm)  7.71 us
    pallas_call x2, Pallas kernels, hessian(): call(hessian_kernel, jax.ShapeDtypeStruct(delta_shape, jnp.bfloat16), [in...  6.47 us
    ppermute x2, starting transfers between devices, to_sibling(): return lax.ppermute(value, 'base', [(i, i ^ 1) for i in range(count)])  3.97 us
    ppermute x2, waiting for transfers between devices, to_sibling(): return lax.ppermute(value, 'base', [(i, i ^ 1) for i in range(count)])  2.81 us
    pallas_call x2, Pallas kernels, prepared(): call(functools.partial(prepare_kernel, first), [quad_shape] * 2, [in_smem...  2.66 us
  transfers between devices with their start and end apart: 12, of which 9 were waited for; matrix products, arithmetic and copies ran while one was open for 0% of the time, Pallas kernels for 7%

profile of v6, /device:TPU:32, one launch (start us, length us, event | category | flops | bytes accessed | tf_op | source)
XLA Modules:
  0.0 106.7 jit_solution(11332468765733672358)
XLA Ops:
  0.0 0.0 copy-start.5
  0.0 0.0 copy-start.4
  0.0 1.2 %pad_maximum_fusion = bf16[48,8,1024]{2,1,0:T(8,128)(2,1)S(1)} fusion(bf16[16,8,1024]{2,1,0:T(8,128)(2,1)} %sky.1, bf16[32,8,1024]{2,1,0:T(8,128)(2,1)} %weights.1), kind=kLoop, calls=%fused_computation | loop fusion | flops 393216 | bytes 1572864 | tf_op jit(solution)/shard_map/concatenate | solution.py:469
  1.3 0.0 copy-done.5
  1.3 0.0 copy-done.4
  1.3 0.2 shard_map.92.own
  1.5 16.5 %collective-permute-start.1 = (bf16[4,2,2,32,128]{4,3,2,1,0:T(8,128)(2,1)S(1)}, bf16[4,2,2,32,128]{4,3,2,1,0:T(8,128)(2,1)S(1)}, u32[]{:S(2)}, u32[]{:S(2)}) collective-permute-start(bf16[4,2,2,32,128]{4,3,2,1,0:T(8,128)(2,1)S(1)} %shard_map.92.own), channel_id=1, source_target_pairs={{0,318},{1,319},{2,4},{3,5},{4,2},{5,3},{6,8},{7,9},{8,6},{9,7},{1... | collective-permute-start | bytes 393224 | tf_op jit(solution)/shard_map/ppermute | solution.py:56
  18.0 1.9 %collective-permute-start = (bf16[4,2,2,32,128]{4,3,2,1,0:T(8,128)(2,1)S(1)}, bf16[4,2,2,32,128]{4,3,2,1,0:T(8,128)(2,1)S(1)}, u32[]{:S(2)}, u32[]{:S(2)}) collective-permute-start(bf16[4,2,2,32,128]{4,3,2,1,0:T(8,128)(2,1)S(1)} %shard_map.92.own), channel_id=1, source_target_pairs={{0,2},{1,3},{2,0},{3,1},{4,6},{5,7},{6,4},{7,5},{8,10},{9,11},{10,... | collective-permute-start | bytes 393224 | tf_op jit(solution)/shard_map/ppermute | solution.py:56
  20.5 0.0 copy-start.6
  20.6 0.0 copy-start.7
  20.6 0.7 copy-done.6
  21.2 0.0 copy-done.7
  21.3 2.9 %collective-permute-start.4 = (bf16[48,8,1024]{2,1,0:T(8,128)(2,1)S(1)}, bf16[48,8,1024]{2,1,0:T(8,128)(2,1)S(1)}, u32[]{:S(2)}, u32[]{:S(2)}) collective-permute-start(bf16[48,8,1024]{2,1,0:T(8,128)(2,1)S(1)} %pad_maximum_fusion), channel_id=1, source_target_pairs={{0,64},{64,0},{128,192},{192,128},{256,320},{320,256},{384,448},{4... | collective-permute-start | bytes 2359304 | tf_op jit(solution)/shard_map/ppermute | solution.py:35
  24.2 2.8 %collective-permute-done.1.chip_b = bf16[4,2,2,32,128]{4,3,2,1,0:T(8,128)(2,1)S(1)} collective-permute-done((bf16[4,2,2,32,128]{4,3,2,1,0:T(8,128)(2,1)S(1)}, bf16[4,2,2,32,128]{4,3,2,1,0:T(8,128)(2,1)S(1)}, u32[]{:S(2)}, u32[]{:S(2)}) %collective-permute-start.1) | collective-permute-done | bytes 131104 | tf_op jit(solution)/shard_map/ppermute | solution.py:56
  27.0 0.0 collective-permute-done.chip_a
  27.0 0.0 copy-start.3
  27.0 0.0 copy-start
  27.0 0.0 copy-start.1
  27.1 2.1 %collective-permute-start.2 = (bf16[2,4,2,2,32,128]{5,4,3,2,1,0:T(8,128)(2,1)S(1)}, bf16[2,4,2,2,32,128]{5,4,3,2,1,0:T(8,128)(2,1)S(1)}, u32[]{:S(2)}, u32[]{:S(2)}) collective-permute-start(bf16[2,4,2,2,32,128]{5,4,3,2,1,0:T(8,128)(2,1)S(1)} %pad_maximum_fusion.1), channel_id=1, source_target_pairs={{0,1},{1,0},{2,3},{3,2},{4,5},{5,4},{6,7},{7,6},{8,9},{9,8},{10,11... | collective-permute-start | bytes 786440 | tf_op jit(solution)/shard_map/ppermute | solution.py:40
  29.1 1.5 %collective-permute-done.2.sibling = bf16[2,4,2,2,32,128]{5,4,3,2,1,0:T(8,128)(2,1)S(1)} collective-permute-done((bf16[2,4,2,2,32,128]{5,4,3,2,1,0:T(8,128)(2,1)S(1)}, bf16[2,4,2,2,32,128]{5,4,3,2,1,0:T(8,128)(2,1)S(1)}, u32[]{:S(2)}, u32[]{:S(2)}) %collective-permute-start.2) | collective-permute-done | bytes 262176 | tf_op jit(solution)/shard_map/ppermute | solution.py:40
  30.6 1.3 %shard_map.93 = (bf16[8,2,2,16,128]{4,3,2,1,0:T(8,128)(2,1)S(1)}, f32[20,2,32,128]{3,2,1,0:T(8,128)S(1)}, f32[20,2,32,128]{3,2,1,0:T(8,128)S(1)}) custom-call(s32[8,32]{1,0:T(8,128)S(1)} %shard_map.91.meta.args_0_, bf16[4,2,2,32,128]{4,3,2,1,0:T(8,128)(2,1)S(1)} %shard_map.92.own, bf16[4,2,2,32,128]{4,3,2,1,0:T(8,128)(2,1)S(1)} %collective-permute-done.chip_a, ...), custom_call_target="tpu_custom_call" | custom-call | tf_op jit(solution)/shard_map/pallas_call | solution.py:495
  31.9 6.5 %collective-permute-start.3 = (bf16[8,2,2,16,128]{4,3,2,1,0:T(8,128)(2,1)S(1)}, bf16[8,2,2,16,128]{4,3,2,1,0:T(8,128)(2,1)S(1)}, u32[]{:S(2)}, u32[]{:S(2)}) collective-permute-start(bf16[8,2,2,16,128]{4,3,2,1,0:T(8,128)(2,1)S(1)} %get-tuple-element.38.delta), channel_id=1, source_target_pairs={{0,128},{64,192},{128,0},{192,64},{256,384},{320,448},{384,256},{4... | collective-permute-start | bytes 393224 | tf_op jit(solution)/shard_map/ppermute | solution.py:35
  38.4 0.0 copy-done.3
  38.5 0.0 copy-done
  38.5 0.0 copy-done.1
  38.5 1.3 %shard_map.94 = (bf16[8,8,32,128]{3,2,1,0:T(8,128)(2,1)S(1)}, bf16[8,8,32,128]{3,2,1,0:T(8,128)(2,1)S(1)}) custom-call(s32[8,32]{1,0:T(8,128)S(1)} %shard_map.91.meta.args_0_, bf16[32,8,1024]{2,1,0:T(8,128)(2,1)S(1)} %copy-done, bf16[16,8,1024]{2,1,0:T(8,128)(2,1)S(1)} %copy-done.3, bf16[512,512]{1,0:T(8,128)(2,1)S(1)} %copy-done.1), custom_call_target="tpu_custom_call" | custom-call | tf_op jit(solution)/shard_map/pallas_call | solution.py:510
  39.8 0.0 copy-start.2
  39.8 6.3 %collective-permute-done.4.weights.sky = bf16[48,8,1024]{2,1,0:T(8,128)(2,1)S(1)} collective-permute-done((bf16[48,8,1024]{2,1,0:T(8,128)(2,1)S(1)}, bf16[48,8,1024]{2,1,0:T(8,128)(2,1)S(1)}, u32[]{:S(2)}, u32[]{:S(2)}) %collective-permute-start.4) | collective-permute-done | bytes 786464 | tf_op jit(solution)/shard_map/ppermute | solution.py:35
  46.1 1.3 %shard_map.95 = (bf16[8,8,32,128]{3,2,1,0:T(8,128)(2,1)S(1)}, bf16[8,8,32,128]{3,2,1,0:T(8,128)(2,1)S(1)}) custom-call(s32[8,32]{1,0:T(8,128)S(1)} %shard_map.91.meta.args_0_, bf16[48,8,1024]{2,1,0:T(8,128)(2,1)S(1)} %collective-permute-done.4.weights.sky, bf16[48,8,1024]{2,1,0:T(8,128)(2,1)S(1)} %collective-permute-done.4.weights.sky, ...), custom_call_target="tpu_custom_call" | custom-call | tf_op jit(solution)/shard_map/pallas_call | solution.py:510
  47.4 0.0 collective-permute-done.3.delta
  47.4 0.0 copy-done.2
  47.4 3.2 %shard_map.96 = bf16[8,2,2,16,128]{4,3,2,1,0:T(8,128)(2,1)S(1)} custom-call(s32[8,32]{1,0:T(8,128)S(1)} %shard_map.91.meta.args_0_, bf16[8,2,2,16,128]{4,3,2,1,0:T(8,128)(2,1)S(1)} %collective-permute-done.3.delta, bf16[8,8,32,128]{3,2,1,0:T(8,128)(2,1)S(1)} %get-tuple-element.33.weights_0, bf16[8,8,32,128]{3,2,1,0:T(8,128)(2,1)S(1)} %get-tuple-element.35.weights_1, ...), custom_call_target="tpu_custom_call" | custom-call | tf_op jit(solution)/shard_map/pallas_call | solution.py:526
  50.7 2.9 %collective-permute-start.5 = (bf16[8,2,2,16,128]{4,3,2,1,0:T(8,128)(2,1)S(1)}, bf16[8,2,2,16,128]{4,3,2,1,0:T(8,128)(2,1)S(1)}, u32[]{:S(2)}, u32[]{:S(2)}) collective-permute-start(bf16[8,2,2,16,128]{4,3,2,1,0:T(8,128)(2,1)S(1)} %shard_map.96), channel_id=1, source_target_pairs={{0,128},{64,192},{128,0},{192,64},{256,384},{320,448},{384,256},{4... | collective-permute-start | bytes 393224 | tf_op jit(solution)/shard_map/ppermute | solution.py:35
  53.6 3.2 %shard_map.97.args_1_ = bf16[8,2,2,16,128]{4,3,2,1,0:T(8,128)(2,1)S(1)} custom-call(s32[8,32]{1,0:T(8,128)S(1)} %shard_map.91.meta.args_0_, bf16[8,2,2,16,128]{4,3,2,1,0:T(8,128)(2,1)S(1)} %get-tuple-element.38.delta, bf16[8,8,32,128]{3,2,1,0:T(8,128)(2,1)S(1)} %get-tuple-element.33.weights_0, bf16[8,8,32,128]{3,2,1,0:T(8,128)(2,1)S(1)} %get-tuple-element.35.weights_1, ...), custom_call_target="tpu_custom_call" | custom-call | tf_op jit(solution)/shard_map/pallas_call | solution.py:526
  56.8 2.3 %collective-permute-done.5.args_2_ = bf16[8,2,2,16,128]{4,3,2,1,0:T(8,128)(2,1)S(1)} collective-permute-done((bf16[8,2,2,16,128]{4,3,2,1,0:T(8,128)(2,1)S(1)}, bf16[8,2,2,16,128]{4,3,2,1,0:T(8,128)(2,1)S(1)}, u32[]{:S(2)}, u32[]{:S(2)}) %collective-permute-start.5) | collective-permute-done | bytes 131104 | tf_op jit(solution)/shard_map/ppermute | solution.py:35
  59.2 1.2 %shard_map.98 = (f32[4,2,32,128]{3,2,1,0:T(8,128)S(1)}, f32[2,4,2,32,128]{4,3,2,1,0:T(8,128)S(1)}, bf16[2,4,2,32,128]{4,3,2,1,0:T(8,128)(2,1)S(1)}) custom-call(s32[8,32]{1,0:T(8,128)S(1)} %shard_map.91.meta.args_0_, bf16[8,2,2,16,128]{4,3,2,1,0:T(8,128)(2,1)S(1)} %shard_map.97.args_1_, bf16[8,2,2,16,128]{4,3,2,1,0:T(8,128)(2,1)S(1)} %collective-permute-done.5.args_2_, ...), custom_call_target="tpu_custom_call" | custom-call | tf_op jit(solution)/shard_map/pallas_call | solution.py:542
  60.4 1.9 %collective-permute-start.6 = (bf16[2,4,2,32,128]{4,3,2,1,0:T(8,128)(2,1)S(1)}, bf16[2,4,2,32,128]{4,3,2,1,0:T(8,128)(2,1)S(1)}, u32[]{:S(2)}, u32[]{:S(2)}) collective-permute-start(bf16[2,4,2,32,128]{4,3,2,1,0:T(8,128)(2,1)S(1)} %get-tuple-element.43), channel_id=1, source_target_pairs={{0,1},{1,0},{2,3},{3,2},{4,5},{5,4},{6,7},{7,6},{8,9},{9,8},{10,11... | collective-permute-start | bytes 393224 | tf_op jit(solution)/shard_map/ppermute | solution.py:40
  62.3 1.3 %collective-permute-done.6 = bf16[2,4,2,32,128]{4,3,2,1,0:T(8,128)(2,1)S(1)} collective-permute-done((bf16[2,4,2,32,128]{4,3,2,1,0:T(8,128)(2,1)S(1)}, bf16[2,4,2,32,128]{4,3,2,1,0:T(8,128)(2,1)S(1)}, u32[]{:S(2)}, u32[]{:S(2)}) %collective-permute-start.6) | collective-permute-done | bytes 131104 | tf_op jit(solution)/shard_map/ppermute | solution.py:40
  63.7 7.5 %collective-permute-start.7 = (bf16[4,2,32,128]{3,2,1,0:T(8,128)(2,1)S(1)}, bf16[4,2,32,128]{3,2,1,0:T(8,128)(2,1)S(1)}, u32[]{:S(2)}, u32[]{:S(2)}) collective-permute-start(bf16[4,2,32,128]{3,2,1,0:T(8,128)(2,1)S(1)} %get-tuple-element.45), channel_id=1, source_target_pairs={{0,318},{1,319},{2,4},{3,5},{4,2},{5,3},{6,8},{7,9},{8,6},{9,7},{1... | collective-permute-start | bytes 196616 | tf_op jit(solution)/shard_map/ppermute | solution.py:56
  71.2 1.9 %collective-permute-start.8 = (bf16[4,2,32,128]{3,2,1,0:T(8,128)(2,1)S(1)}, bf16[4,2,32,128]{3,2,1,0:T(8,128)(2,1)S(1)}, u32[]{:S(2)}, u32[]{:S(2)}) collective-permute-start(bf16[4,2,32,128]{3,2,1,0:T(8,128)(2,1)S(1)} %get-tuple-element.46), channel_id=1, source_target_pairs={{0,2},{1,3},{2,0},{3,1},{4,6},{5,7},{6,4},{7,5},{8,10},{9,11},{10,... | collective-permute-start | bytes 196616 | tf_op jit(solution)/shard_map/ppermute | solution.py:56
  73.1 4.9 %collective-permute-done.7 = bf16[4,2,32,128]{3,2,1,0:T(8,128)(2,1)S(1)} collective-permute-done((bf16[4,2,32,128]{3,2,1,0:T(8,128)(2,1)S(1)}, bf16[4,2,32,128]{3,2,1,0:T(8,128)(2,1)S(1)}, u32[]{:S(2)}, u32[]{:S(2)}) %collective-permute-start.7) | collective-permute-done | bytes 65568 | tf_op jit(solution)/shard_map/ppermute | solution.py:56
  78.1 0.0 collective-permute-done.8
  78.1 7.1 %collective-permute-start.9 = (bf16[4,2,32,128]{3,2,1,0:T(8,128)(2,1)S(1)}, bf16[4,2,32,128]{3,2,1,0:T(8,128)(2,1)S(1)}, u32[]{:S(2)}, u32[]{:S(2)}) collective-permute-start(bf16[4,2,32,128]{3,2,1,0:T(8,128)(2,1)S(1)} %fusion.3), channel_id=1, source_target_pairs={{0,256},{64,320},{128,384},{192,448},{256,0},{320,64},{384,128},{4... | collective-permute-start | bytes 196616 | tf_op jit(solution)/shard_map/ppermute | solution.py:35
  85.2 3.0 %collective-permute-done.9 = bf16[4,2,32,128]{3,2,1,0:T(8,128)(2,1)S(1)} collective-permute-done((bf16[4,2,32,128]{3,2,1,0:T(8,128)(2,1)S(1)}, bf16[4,2,32,128]{3,2,1,0:T(8,128)(2,1)S(1)}, u32[]{:S(2)}, u32[]{:S(2)}) %collective-permute-start.9) | collective-permute-done | bytes 65568 | tf_op jit(solution)/shard_map/ppermute | solution.py:35
  88.2 8.3 %collective-permute-start.10 = (bf16[4,2,32,128]{3,2,1,0:T(8,128)(2,1)S(1)}, bf16[4,2,32,128]{3,2,1,0:T(8,128)(2,1)S(1)}, u32[]{:S(2)}, u32[]{:S(2)}) collective-permute-start(bf16[4,2,32,128]{3,2,1,0:T(8,128)(2,1)S(1)} %add_convert_fusion.mine), channel_id=1, source_target_pairs={{0,128},{64,192},{128,0},{192,64},{256,384},{320,448},{384,256},{4... | collective-permute-start | bytes 196616 | tf_op jit(solution)/shard_map/ppermute | solution.py:35
  96.5 2.3 %collective-permute-done.10.over_two = bf16[4,2,32,128]{3,2,1,0:T(8,128)(2,1)S(1)} collective-permute-done((bf16[4,2,32,128]{3,2,1,0:T(8,128)(2,1)S(1)}, bf16[4,2,32,128]{3,2,1,0:T(8,128)(2,1)S(1)}, u32[]{:S(2)}, u32[]{:S(2)}) %collective-permute-start.10) | collective-permute-done | bytes 65568 | tf_op jit(solution)/shard_map/ppermute | solution.py:35
  98.9 3.8 %collective-permute-start.11 = (bf16[2,4,2,32,128]{4,3,2,1,0:T(8,128)(2,1)S(1)}, bf16[2,4,2,32,128]{4,3,2,1,0:T(8,128)(2,1)S(1)}, u32[]{:S(2)}, u32[]{:S(2)}) collective-permute-start(bf16[2,4,2,32,128]{4,3,2,1,0:T(8,128)(2,1)S(1)} %pad_maximum_fusion.2), channel_id=1, source_target_pairs={{0,64},{64,0},{128,192},{192,128},{256,320},{320,256},{384,448},{4... | collective-permute-start | bytes 393224 | tf_op jit(solution)/shard_map/ppermute | solution.py:35
  102.6 3.1 %collective-permute-done.11.over_one = bf16[2,4,2,32,128]{4,3,2,1,0:T(8,128)(2,1)S(1)} collective-permute-done((bf16[2,4,2,32,128]{4,3,2,1,0:T(8,128)(2,1)S(1)}, bf16[2,4,2,32,128]{4,3,2,1,0:T(8,128)(2,1)S(1)}, u32[]{:S(2)}, u32[]{:S(2)}) %collective-permute-start.11) | collective-permute-done | bytes 131104 | tf_op jit(solution)/shard_map/ppermute | solution.py:35
  105.7 1.0 shard_map.99
  (8 shorter events, 0.2 us)
Async XLA Ops:
  0.0 1.3 %copy-start.5 = (bf16[4,8,4096]{2,1,0:T(8,128)(2,1)S(1)}, bf16[4,8,4096]{2,1,0:T(8,128)(2,1)}, u32[]{:S(2)}) copy-start(bf16[4,8,4096]{2,1,0:T(8,128)(2,1)} %direction) | copy-start | bytes 786436
  0.0 1.3 %copy-start.4 = (bf16[4,8,4096]{2,1,0:T(8,128)(2,1)S(1)}, bf16[4,8,4096]{2,1,0:T(8,128)(2,1)}, u32[]{:S(2)}) copy-start(bf16[4,8,4096]{2,1,0:T(8,128)(2,1)} %screens) | copy-start | bytes 786436
  1.5 25.5 %collective-permute-start.1 = (bf16[4,2,2,32,128]{4,3,2,1,0:T(8,128)(2,1)S(1)}, bf16[4,2,2,32,128]{4,3,2,1,0:T(8,128)(2,1)S(1)}, u32[]{:S(2)}, u32[]{:S(2)}) collective-permute-start(bf16[4,2,2,32,128]{4,3,2,1,0:T(8,128)(2,1)S(1)} %shard_map.92.own), channel_id=1, source_target_pairs={{0,318},{1,319},{2,4},{3,5},{4,2},{5,3},{6,8},{7,9},{8,6},{9,7},{1... | collective-permute-start | bytes 393224 | tf_op jit(solution)/shard_map/ppermute | solution.py:56
  18.0 9.0 %collective-permute-start = (bf16[4,2,2,32,128]{4,3,2,1,0:T(8,128)(2,1)S(1)}, bf16[4,2,2,32,128]{4,3,2,1,0:T(8,128)(2,1)S(1)}, u32[]{:S(2)}, u32[]{:S(2)}) collective-permute-start(bf16[4,2,2,32,128]{4,3,2,1,0:T(8,128)(2,1)S(1)} %shard_map.92.own), channel_id=1, source_target_pairs={{0,2},{1,3},{2,0},{3,1},{4,6},{5,7},{6,4},{7,5},{8,10},{9,11},{10,... | collective-permute-start | bytes 393224 | tf_op jit(solution)/shard_map/ppermute | solution.py:56
  20.5 0.7 copy-start.6
  20.6 0.7 copy-start.7
  21.3 24.8 %collective-permute-start.4 = (bf16[48,8,1024]{2,1,0:T(8,128)(2,1)S(1)}, bf16[48,8,1024]{2,1,0:T(8,128)(2,1)S(1)}, u32[]{:S(2)}, u32[]{:S(2)}) collective-permute-start(bf16[48,8,1024]{2,1,0:T(8,128)(2,1)S(1)} %pad_maximum_fusion), channel_id=1, source_target_pairs={{0,64},{64,0},{128,192},{192,128},{256,320},{320,256},{384,448},{4... | collective-permute-start | bytes 2359304 | tf_op jit(solution)/shard_map/ppermute | solution.py:35
  27.0 11.5 %copy-start.3 = (bf16[16,8,1024]{2,1,0:T(8,128)(2,1)S(1)}, bf16[16,8,1024]{2,1,0:T(8,128)(2,1)}, u32[]{:S(2)}) copy-start(bf16[16,8,1024]{2,1,0:T(8,128)(2,1)} %sky.1) | copy-start | bytes 786436
  27.0 11.5 %copy-start = (bf16[32,8,1024]{2,1,0:T(8,128)(2,1)S(1)}, bf16[32,8,1024]{2,1,0:T(8,128)(2,1)}, u32[]{:S(2)}) copy-start(bf16[32,8,1024]{2,1,0:T(8,128)(2,1)} %weights.1) | copy-start | bytes 1572868
  27.0 11.5 %copy-start.1 = (bf16[512,512]{1,0:T(8,128)(2,1)S(1)}, bf16[512,512]{1,0:T(8,128)(2,1)}, u32[]{:S(2)}) copy-start(bf16[512,512]{1,0:T(8,128)(2,1)} %constant.39.clone.table) | copy-start | bytes 1572868
  27.1 3.6 %collective-permute-start.2 = (bf16[2,4,2,2,32,128]{5,4,3,2,1,0:T(8,128)(2,1)S(1)}, bf16[2,4,2,2,32,128]{5,4,3,2,1,0:T(8,128)(2,1)S(1)}, u32[]{:S(2)}, u32[]{:S(2)}) collective-permute-start(bf16[2,4,2,2,32,128]{5,4,3,2,1,0:T(8,128)(2,1)S(1)} %pad_maximum_fusion.1), channel_id=1, source_target_pairs={{0,1},{1,0},{2,3},{3,2},{4,5},{5,4},{6,7},{7,6},{8,9},{9,8},{10,11... | collective-permute-start | bytes 786440 | tf_op jit(solution)/shard_map/ppermute | solution.py:40
  31.9 15.5 %collective-permute-start.3 = (bf16[8,2,2,16,128]{4,3,2,1,0:T(8,128)(2,1)S(1)}, bf16[8,2,2,16,128]{4,3,2,1,0:T(8,128)(2,1)S(1)}, u32[]{:S(2)}, u32[]{:S(2)}) collective-permute-start(bf16[8,2,2,16,128]{4,3,2,1,0:T(8,128)(2,1)S(1)} %get-tuple-element.38.delta), channel_id=1, source_target_pairs={{0,128},{64,192},{128,0},{192,64},{256,384},{320,448},{384,256},{4... | collective-permute-start | bytes 393224 | tf_op jit(solution)/shard_map/ppermute | solution.py:35
  39.8 7.6 %copy-start.2 = (bf16[4,256,256]{2,1,0:T(8,128)(2,1)S(1)}, bf16[4,256,256]{2,1,0:T(8,128)(2,1)}, u32[]{:S(2)}) copy-start(bf16[4,256,256]{2,1,0:T(8,128)(2,1)} %constant.38.clone.tables) | copy-start | bytes 1572868
  50.7 8.5 %collective-permute-start.5 = (bf16[8,2,2,16,128]{4,3,2,1,0:T(8,128)(2,1)S(1)}, bf16[8,2,2,16,128]{4,3,2,1,0:T(8,128)(2,1)S(1)}, u32[]{:S(2)}, u32[]{:S(2)}) collective-permute-start(bf16[8,2,2,16,128]{4,3,2,1,0:T(8,128)(2,1)S(1)} %shard_map.96), channel_id=1, source_target_pairs={{0,128},{64,192},{128,0},{192,64},{256,384},{320,448},{384,256},{4... | collective-permute-start | bytes 393224 | tf_op jit(solution)/shard_map/ppermute | solution.py:35
  60.4 3.2 %collective-permute-start.6 = (bf16[2,4,2,32,128]{4,3,2,1,0:T(8,128)(2,1)S(1)}, bf16[2,4,2,32,128]{4,3,2,1,0:T(8,128)(2,1)S(1)}, u32[]{:S(2)}, u32[]{:S(2)}) collective-permute-start(bf16[2,4,2,32,128]{4,3,2,1,0:T(8,128)(2,1)S(1)} %get-tuple-element.43), channel_id=1, source_target_pairs={{0,1},{1,0},{2,3},{3,2},{4,5},{5,4},{6,7},{7,6},{8,9},{9,8},{10,11... | collective-permute-start | bytes 393224 | tf_op jit(solution)/shard_map/ppermute | solution.py:40
  63.7 14.3 %collective-permute-start.7 = (bf16[4,2,32,128]{3,2,1,0:T(8,128)(2,1)S(1)}, bf16[4,2,32,128]{3,2,1,0:T(8,128)(2,1)S(1)}, u32[]{:S(2)}, u32[]{:S(2)}) collective-permute-start(bf16[4,2,32,128]{3,2,1,0:T(8,128)(2,1)S(1)} %get-tuple-element.45), channel_id=1, source_target_pairs={{0,318},{1,319},{2,4},{3,5},{4,2},{5,3},{6,8},{7,9},{8,6},{9,7},{1... | collective-permute-start | bytes 196616 | tf_op jit(solution)/shard_map/ppermute | solution.py:56
  71.2 6.9 %collective-permute-start.8 = (bf16[4,2,32,128]{3,2,1,0:T(8,128)(2,1)S(1)}, bf16[4,2,32,128]{3,2,1,0:T(8,128)(2,1)S(1)}, u32[]{:S(2)}, u32[]{:S(2)}) collective-permute-start(bf16[4,2,32,128]{3,2,1,0:T(8,128)(2,1)S(1)} %get-tuple-element.46), channel_id=1, source_target_pairs={{0,2},{1,3},{2,0},{3,1},{4,6},{5,7},{6,4},{7,5},{8,10},{9,11},{10,... | collective-permute-start | bytes 196616 | tf_op jit(solution)/shard_map/ppermute | solution.py:56
  78.1 10.1 %collective-permute-start.9 = (bf16[4,2,32,128]{3,2,1,0:T(8,128)(2,1)S(1)}, bf16[4,2,32,128]{3,2,1,0:T(8,128)(2,1)S(1)}, u32[]{:S(2)}, u32[]{:S(2)}) collective-permute-start(bf16[4,2,32,128]{3,2,1,0:T(8,128)(2,1)S(1)} %fusion.3), channel_id=1, source_target_pairs={{0,256},{64,320},{128,384},{192,448},{256,0},{320,64},{384,128},{4... | collective-permute-start | bytes 196616 | tf_op jit(solution)/shard_map/ppermute | solution.py:35
  88.2 10.6 %collective-permute-start.10 = (bf16[4,2,32,128]{3,2,1,0:T(8,128)(2,1)S(1)}, bf16[4,2,32,128]{3,2,1,0:T(8,128)(2,1)S(1)}, u32[]{:S(2)}, u32[]{:S(2)}) collective-permute-start(bf16[4,2,32,128]{3,2,1,0:T(8,128)(2,1)S(1)} %add_convert_fusion.mine), channel_id=1, source_target_pairs={{0,128},{64,192},{128,0},{192,64},{256,384},{320,448},{384,256},{4... | collective-permute-start | bytes 196616 | tf_op jit(solution)/shard_map/ppermute | solution.py:35
  98.9 6.9 %collective-permute-start.11 = (bf16[2,4,2,32,128]{4,3,2,1,0:T(8,128)(2,1)S(1)}, bf16[2,4,2,32,128]{4,3,2,1,0:T(8,128)(2,1)S(1)}, u32[]{:S(2)}, u32[]{:S(2)}) collective-permute-start(bf16[2,4,2,32,128]{4,3,2,1,0:T(8,128)(2,1)S(1)} %pad_maximum_fusion.2), channel_id=1, source_target_pairs={{0,64},{64,0},{128,192},{192,128},{256,320},{320,256},{384,448},{4... | collective-permute-start | bytes 393224 | tf_op jit(solution)/shard_map/ppermute | solution.py:35
